TPU v7x, 32 devices: a whole 2x2x4 slice. The times are simulated.
32 devices in a mesh: row: 4 (over y, x), col: 8 (over z, core).
Axes of the slice: x: 2, y: 2, z: 4, core: 2. Of those that a mesh axis runs over, the one named last changes fastest.
Arguments:
- tiles: bfloat16 [3072, 128, 128], P(('row', 'col')), may hold values from -0.5 to 0.5
- tile_rows: int32 [3072], P(('row', 'col')), may hold values from 0 to 15
- tile_cols: int32 [3072], P(('row', 'col')), may hold values from 0 to 7
- counts: int32 [32], P(('row', 'col')), may hold values from 32 to 96, as said below
- omega: bfloat16 [8192, 256], P('col'), may hold values from -6 to 6
Outputs:
- basis: bfloat16 [8192, 256], P(('row', 'col'))
- projected: bfloat16 [8192, 256], P('col')
Inputs may be any that keep to these rules, and one draw needn't show every extreme that they name: `counts`: within one device the live and dead slots name distinct blocks; some device has all 96 slots live and some has 32.
All inputs are finite; a program needn't handle non-finite values.
Results may differ from a plain program's by a relative error of at most 0.0095.
Values may be sent and summed in bfloat16 or wider, within the bound.
No kernel may reach another device: no remote copies, remote signals or barrier semaphores. Data moves between devices by JAX's collectives and lax.ppermute only.
A program may use at most 128 MiB of HBM per device.

v0:
```python
import jax
import jax.numpy as jnp
from jax import lax
from jax.sharding import PartitionSpec as P

RB_DEV = 16


def block_sum(selector, terms):
    high_part = terms.astype(jnp.bfloat16)
    low_part = (terms - high_part.astype(jnp.float32)).astype(jnp.bfloat16)
    select_bf = selector.astype(jnp.bfloat16)
    upper_sum = jnp.einsum("rs,sik->rik", select_bf, high_part, preferred_element_type=jnp.float32)
    lower_sum = jnp.einsum("rs,sik->rik", select_bf, low_part, preferred_element_type=jnp.float32)
    return upper_sum + lower_sum


def factor_rows(sketch_rows, gram, total_rows):
    lower = jnp.linalg.cholesky(gram)
    solved = jax.scipy.linalg.solve_triangular(lower, sketch_rows.T, lower=True).T
    return (solved * jnp.sqrt(jnp.float32(total_rows))).astype(jnp.bfloat16)


def shards(tiles, tile_rows, tile_cols, counts, omega):
    slots = tiles.shape[0]
    size_b = tiles.shape[1]
    rank = omega.shape[1]
    col_blocks = omega.shape[0] // size_b
    row_groups = lax.axis_size("row")
    col_groups = lax.axis_size("col")
    live = (jnp.arange(slots, dtype=jnp.int32) < counts[0]).astype(jnp.float32)
    row_select = (jnp.arange(RB_DEV, dtype=jnp.int32)[:, None] == tile_rows[None, :]).astype(
        jnp.float32
    ) * live[None, :]
    col_select = (jnp.arange(col_blocks, dtype=jnp.int32)[:, None] == tile_cols[None, :]).astype(
        jnp.float32
    ) * live[None, :]
    picked = omega.reshape(col_blocks, size_b, rank)[tile_cols]
    terms = jnp.einsum("sij,sjk->sik", tiles, picked, preferred_element_type=jnp.float32)
    partial_rows = block_sum(row_select, terms).reshape(RB_DEV * size_b, rank)
    total_rows = RB_DEV * size_b * row_groups
    share = RB_DEV * size_b // col_groups
    sketch_rows = lax.psum(partial_rows, "col")
    own_rows = lax.dynamic_slice_in_dim(sketch_rows, lax.axis_index("col") * share, share, 0)
    local_gram = jnp.dot(own_rows.T, own_rows, precision=lax.Precision.HIGHEST)
    gram = lax.psum(local_gram, ("row", "col"))
    group_basis = factor_rows(sketch_rows, gram, total_rows)
    basis = lax.dynamic_slice_in_dim(group_basis, lax.axis_index("col") * share, share, 0)
    basis_picked = group_basis.reshape(RB_DEV, size_b, rank)[tile_rows]
    back_terms = jnp.einsum("sji,sjk->sik", tiles, basis_picked, preferred_element_type=jnp.float32)
    partial_cols = block_sum(col_select, back_terms).reshape(col_blocks * size_b, rank)
    projected = lax.psum(partial_cols, "row")
    projected = projected / jnp.sqrt(jnp.float32(RB_DEV * row_groups))
    return (basis, projected.astype(jnp.bfloat16))


def solution(mesh):
    return jax.shard_map(
        shards,
        mesh=mesh,
        in_specs=(
            P(("row", "col"), None, None),
            P(("row", "col")),
            P(("row", "col")),
            P(("row", "col")),
            P("col", None),
        ),
        out_specs=(P(("row", "col"), None), P("col", None)),
        check_vma=False,
    )
```

profile of v0, /device:TPU:0, one launch (start us, length us, event | category | flops | bytes accessed | tf_op | source)
XLA Modules:
  0.0 434.5 jit_solution(16608744967227862481)
XLA Ops:
  8.0 7.0 %gather_fusion = bf16[96,128,256]{2,1,0:T(8,128)(2,1)} fusion(bf16[8,128,256]{2,1,0:T(8,128)(2,1)} %bitcast.70, s32[1024]{0:T(1024)S(1)} %pad_clamp_fusion.1), kind=kCustom, calls=%fused_computation | custom fusion | bytes 12583296 | tf_op jit(solution)/shard_map/gather | solution.py:38
  15.1 10.1 %fusion.1 = (bf16[96,128,256]{1,2,0:T(8,128)(2,1)}, bf16[96,128,256]{1,2,0:T(8,128)(2,1)}) fusion(bf16[96,128,256]{2,1,0:T(8,128)(2,1)} %gather_fusion, bf16[96,128,128]{2,1,0:T(8,128)(2,1)S(1)} %copy-done), kind=kOutput, calls=%fused_computation.9 | convolution fusion | flops 817889280 | bytes 22020096 | tf_op jit(solution)/shard_map/sij,sjk->sik/dot_general | solution.py:39
  25.1 9.1 %copy.15 = bf16[96,128,256]{2,0,1:T(8,128)(2,1)} copy(bf16[96,128,256]{1,2,0:T(8,128)(2,1)} %get-tuple-element.25) | data formatting | bytes 12582912 | tf_op jit(solution)/shard_map/convert_element_type | solution.py:10
  34.9 9.0 %copy.16 = bf16[96,128,256]{2,0,1:T(8,128)(2,1)} copy(bf16[96,128,256]{1,2,0:T(8,128)(2,1)} %get-tuple-element.24) | data formatting | bytes 12582912 | tf_op jit(solution)/shard_map/convert_element_type | solution.py:11
  44.0 3.9 fusion.15
  49.5 2.5 copy.17
  52.1 67.7 %all-reduce.5.cloned.1.call-done = f32[2048,256]{1,0:T(8,128)} async-done(((f32[2048,256]{1,0:T(8,128)}), f32[2048,256]{1,0:T(8,128)}) %all-reduce.5.cloned.1.call-update) | async-done | bytes 2097168 | tf_op jit(solution)/shard_map/psum | solution.py:43
  119.8 2.3 fusion.6
  122.4 128.1 %all-reduce.7.cloned.1.call-done = f32[256,256]{0,1:T(8,128)} async-done(((f32[256,256]{0,1:T(8,128)}), f32[256,256]{0,1:T(8,128)}) %all-reduce.7.cloned.1.call-update) | async-done | bytes 262160 | tf_op jit(solution)/shard_map/psum | solution.py:46
  250.5 1.1 copy.19
  253.3 11.7 %cholesky.50 = f32[128,128]{1,0:T(8,128)S(1)} custom-call(f32[128,128]{1,0:T(8,128)S(1)} %cholesky.118), custom_call_target="Cholesky" | custom-call | tf_op jit(solution)/shard_map/jit(cholesky)/cholesky | solution.py:19
  265.1 9.8 %custom-call.15 = f32[1,128,128]{1,2,0:T(8,128)S(1)} custom-call(f32[1,128,128]{2,1,0:T(8,128)S(1)} %get-tuple-element.31), custom_call_target="InvertDiagBlocksLowerTriangular" | custom-call | tf_op jit(solution)/shard_map/jit(cholesky)/cholesky | solution.py:19
  275.9 1.1 convolution_subtract_fusion.1
  277.0 11.7 %cholesky.105 = f32[128,128]{1,0:T(8,128)S(1)} custom-call(f32[128,128]{1,0:T(8,128)S(1)} %convolution_subtract_fusion.1), custom_call_target="Cholesky" | custom-call | tf_op jit(solution)/shard_map/jit(cholesky)/cholesky | solution.py:19
  291.7 5.4 %while.1 = (s32[]{:T(128)}, f32[256,256]{1,0:T(8,128)S(1)}, s32[2,2]{1,0:T(2,128)S(1)}, f32[2,128,128]{2,1,0:T(8,128)}, s32[]{:T(128)}) while((s32[]{:T(128)}, f32[256,256]{1,0:T(8,128)S(1)}, s32[2,2]{1,0:T(2,128)S(1)}, f32[2,128,128]{2,1,0:T(8,128)}, s32[]{:T(128)}) %tuple.31), condition=%wide.while_cond, body=%wide.while_body.sunk | while | flops 2 | bytes 132205 | solution.py:20
  292.5 2.0 bitcast_dynamic-update-slice_fusion.2
  295.1 2.0 bitcast_dynamic-update-slice_fusion.2
  297.1 20.5 %custom-call.16 = f32[2,128,128]{1,2,0:T(8,128)S(1)} custom-call(f32[2,128,128]{2,1,0:T(8,128)} %get-tuple-element.9), custom_call_target="InvertDiagBlocksLowerTriangular" | custom-call | tf_op jit(solution)/shard_map/jit(_solve_triangular)/triangular_solve | solution.py:20
  317.5 2.3 fusion.3
  319.8 3.4 convolution_subtract_fusion
  325.3 1.2 fusion.51
  326.5 2.3 copy.29
  328.8 7.2 %gather_fusion.1 = bf16[96,128,256]{2,1,0:T(8,128)(2,1)} fusion(bf16[16,128,256]{2,1,0:T(8,128)(2,1)} %bitcast.71, s32[1024]{0:T(1024)S(1)} %pad_clamp_fusion), kind=kCustom, calls=%fused_computation.1 | custom fusion | bytes 12583296 | tf_op jit(solution)/shard_map/gather | solution.py:49
  336.0 10.0 %fusion = (bf16[96,128,256]{1,2,0:T(8,128)(2,1)}, bf16[96,128,256]{1,2,0:T(8,128)(2,1)}) fusion(bf16[96,128,256]{2,1,0:T(8,128)(2,1)} %gather_fusion.1, bf16[96,128,128]{2,1,0:T(8,128)(2,1)S(1)} %copy-done), kind=kOutput, calls=%fused_computation.6 | convolution fusion | flops 817889280 | bytes 22020096 | tf_op jit(solution)/shard_map/sji,sjk->sik/dot_general | solution.py:50
  346.0 9.0 %copy.22 = bf16[96,128,256]{2,0,1:T(8,128)(2,1)} copy(bf16[96,128,256]{1,2,0:T(8,128)(2,1)} %get-tuple-element.23) | data formatting | bytes 12582912 | tf_op jit(solution)/shard_map/convert_element_type | solution.py:10
  355.1 4.7 %fusion.25 = f32[8,128,256]{2,0,1:T(8,128)} fusion(bf16[96,128,256]{2,0,1:T(8,128)(2,1)} %copy.22, bf16[96]{0:T(256)(128)(2,1)S(1)} %compare_convert_fusion, s32[96]{0:T(128)S(1)} %copy-done.7), kind=kOutput, calls=%fused_computation.55 | convolution fusion | flops 50333184 | bytes 7340608 | tf_op jit(solution)/shard_map/rs,sik->rik/dot_general | solution.py:13
  359.8 9.0 %copy.23 = bf16[96,128,256]{2,0,1:T(8,128)(2,1)} copy(bf16[96,128,256]{1,2,0:T(8,128)(2,1)} %get-tuple-element.22) | data formatting | bytes 12582912 | tf_op jit(solution)/shard_map/convert_element_type | solution.py:11
  368.8 4.0 convolution_add_fusion.1
  372.8 1.3 copy.24
  374.1 1.7 fusion.2
  376.7 49.2 %all-reduce.9.cloned.1.call-done = f32[1024,256]{1,0:T(8,128)} async-done(((f32[1024,256]{1,0:T(8,128)}), f32[1024,256]{1,0:T(8,128)}) %all-reduce.9.cloned.1.call-update) | async-done | bytes 1048592 | tf_op jit(solution)/shard_map/psum | solution.py:52
  425.9 2.1 multiply_convert_fusion
  (46 shorter events, 11.4 us)
Async XLA Ops:
  7.2 7.9 %copy-start = (bf16[96,128,128]{2,1,0:T(8,128)(2,1)S(1)}, bf16[96,128,128]{2,1,0:T(8,128)(2,1)}, u32[]{:S(2)}) copy-start(bf16[96,128,128]{2,1,0:T(8,128)(2,1)} %param.5) | copy-start | bytes 9437188
  7.2 112.6 %all-reduce.5.cloned.1.call-start = ((), (), s32[]{:S(2)}) async-start(), calls=%async_computation | async-start | bytes 4194304 | tf_op jit(solution)/shard_map/psum | solution.py:43
  34.9 9.0 %copy-start.6 = (s32[96]{0:T(128)S(1)}, s32[96]{0:T(128)}, u32[]{:S(2)}) copy-start(s32[96]{0:T(128)} %param.6) | copy-start | bytes 1156
  44.0 4.6 %copy-start.1 = (bf16[96,128,256]{2,0,1:T(8,128)(2,1)S(1)}, bf16[96,128,256]{2,0,1:T(8,128)(2,1)}, u32[]{:S(2)}) copy-start(bf16[96,128,256]{2,0,1:T(8,128)(2,1)} %copy.16) | copy-start | bytes 18874372
  52.0 198.5 %all-reduce.7.cloned.1.call-start = ((), (), s32[]{:S(2)}) async-start(), calls=%async_computation.1 | async-start | bytes 524288 | tf_op jit(solution)/shard_map/psum | solution.py:46
  122.1 303.7 %all-reduce.9.cloned.1.call-start = ((), (), s32[]{:S(2)}) async-start(), calls=%async_computation.2 | async-start | bytes 2097152 | tf_op jit(solution)/shard_map/psum | solution.py:52
  252.6 0.7 copy-start.5
  288.8 1.8 copy-start.4
  319.8 4.5 %copy-start.2 = (f32[128,2048]{1,0:T(8,128)}, f32[128,2048]{1,0:T(8,128)S(1)}, u32[]{:S(2)}) copy-start(f32[128,2048]{1,0:T(8,128)S(1)} %fusion.3) | copy-start | bytes 3145732
  324.4 1.0 copy-start.3
  346.0 9.0 %copy-start.7 = (s32[96]{0:T(128)S(1)}, s32[96]{0:T(128)}, u32[]{:S(2)}) copy-start(s32[96]{0:T(128)} %param.7) | copy-start | bytes 1156
Sparse Core Ops, SparseCore 0:
  52.2 67.5 all-reduce.4
  125.9 124.5 all-reduce.6
  374.3 51.5 all-reduce.8
where the time goes:
time: 436 us; the launch traced here: 435 us
  waiting for transfers between devices  245 us (56%)
  local copies, waits for them, and re-layouts  66.1 us (15%)
  other arithmetic  62.3 us (14%)
  matrix products  44.8 us (10%)
  between operations  15.8 us (4%)
    psum x1, waiting for transfers between devices, shards(): gram = lax.psum(local_gram, ('row', 'col'))  128 us
    psum x1, waiting for transfers between devices, shards(): sketch_rows = lax.psum(partial_rows, 'col')  67.7 us
    psum x1, waiting for transfers between devices, shards(): projected = lax.psum(partial_cols, 'row')  49.2 us
    another operation x6, other arithmetic, factor_rows(): lower = jnp.linalg.cholesky(gram)  33.9 us
    another operation x3, other arithmetic, factor_rows(): jax.scipy.linalg.solve_triangular(lower, sketch_rows.T, lower=True)  21.5 us
    convert_element_type x2, local copies, waits for them, and re-layouts, block_sum(): high_part = terms.astype(jnp.bfloat16)  18.1 us
    convert_element_type x2, local copies, waits for them, and re-layouts, block_sum(): low_part = (terms - high_part.astype(jnp.float32)).astype(jnp.bfloat16)  18 us
    dot_general x1, matrix products, shards(): jnp.einsum('sij,sjk->sik', tiles, picked, preferred_element_type=jnp.floa...  10.1 us
  transfers between devices with their start and end apart: 3, of which 3 were waited for; matrix products, arithmetic and copies ran while one was open for 1% of the time, Pallas kernels for 0%

commit v1 on v0

v1 whole, which is shorter than its diff:
```python
import functools

import jax
import jax.numpy as jnp
from jax import lax
from jax.experimental import pallas as pl
from jax.experimental.pallas import tpu as pltpu
from jax.sharding import PartitionSpec as P

RB_DEV = 16
CORES = 2
MIB = 1024 * 1024
BF = jnp.bfloat16
F32 = jnp.float32

NT = (((1,), (1,)), ((), ()))
TN = (((0,), (0,)), ((), ()))


def vmem():
    return pl.BlockSpec(memory_space=pltpu.VMEM)


def smem():
    return pl.BlockSpec(memory_space=pltpu.SMEM)


def call(body, ins, outs, scratch=(), limit=24, flops=0, nbytes=0, name=None):
    return pl.pallas_call(
        body,
        out_shape=outs,
        in_specs=[smem() if scalar else vmem() for _, scalar in ins],
        out_specs=[vmem() for _ in outs],
        scratch_shapes=list(scratch),
        compiler_params=pltpu.CompilerParams(vmem_limit_bytes=limit * MIB),
        cost_estimate=pl.CostEstimate(flops=flops, bytes_accessed=nbytes, transcendentals=0),
        name=name,
    )(*[array for array, _ in ins])


def dot(a, b, dims=None):
    if dims is None:
        dims = (((1,), (0,)), ((), ()))
    return lax.dot_general(a, b, dims, preferred_element_type=F32)


def split(x):
    high = x.astype(BF)
    return high, (x - high.astype(F32)).astype(BF)


def dot3(a, b, dims=None):
    a_high, a_low = split(a)
    b_high, b_low = split(b)
    return dot(a_high, b_high, dims) + (dot(a_high, b_low, dims) + dot(a_low, b_high, dims))


def sketch_kernel(share, pos, counts, rows, cols, tiles, omega, sent, kept, dense):
    size_b = tiles.shape[1]
    dense[...] = jnp.zeros_like(dense)

    def place(slot, carry):
        start = pl.multiple_of(rows[slot] * size_b, size_b)
        dense[cols[slot], pl.ds(start, size_b), :] = tiles[slot]
        return carry

    lax.fori_loop(0, counts[0], place, 0)
    core = pos[1]
    for out, owner in ((sent, 1 - core), (kept, core)):
        for step in range(out.shape[0] // share):
            start = pl.multiple_of((step * CORES + owner) * share, share)
            left = jnp.concatenate([dense[c, pl.ds(start, share), :] for c in range(dense.shape[0])], axis=1)
            out[step * share : (step + 1) * share, :] = dot(left, omega[...]).astype(out.dtype)


def transpose_kernel(counts, rows, cols, tiles, turned):
    size_b = tiles.shape[1]
    turned[...] = jnp.zeros_like(turned)

    def place(slot, carry):
        start = pl.multiple_of(cols[slot] * size_b, size_b)
        turned[rows[slot], pl.ds(start, size_b), :] = tiles[slot].T
        return carry

    lax.fori_loop(0, counts[0], place, 0)


def pair_kernel(share, pos, kept, came, own, *sends):
    z = pos[0]
    for step in range(len(sends) + 1):
        start = pl.multiple_of((z ^ step) * share, share)
        rows = pl.ds(start, share)
        total = kept[rows, :] + came[rows, :].astype(F32)
        if step == 0:
            own[...] = total
        else:
            sends[step - 1][...] = total.astype(BF)


def sum_kernel(count, own, *refs):
    total = own[...]
    for ref in refs[:count]:
        total = total + ref[...].astype(F32)
    for out in refs[count:]:
        out[...] = total.astype(out.dtype)


def gram_kernel(share, zs, pos, *refs):
    chunks, (full, gram) = refs[: 2 * zs], refs[2 * zs :]
    z, core = pos[0], pos[1]
    for step in range(zs):
        for side in range(CORES):
            place = (z ^ step) * CORES + (core ^ side)
            full[pl.ds(pl.multiple_of(place * share, share), share), :] = chunks[step * CORES + side][...]
    half = gram.shape[0]

    for side in range(CORES):

        @pl.when(core == side)
        def _():
            gram[...] = dot(full[:, side * half : (side + 1) * half], full[...], TN)


def back_kernel(pos, turned, full, own, *sends):
    me = pos[2]
    share = own.shape[0]
    for step in range(len(sends) + 1):
        start = pl.multiple_of((me ^ step) * share, share)
        left = jnp.concatenate([turned[r, pl.ds(start, share), :] for r in range(turned.shape[0])], axis=1)
        product = dot(left, full[...])
        if step == 0:
            own[...] = product
        else:
            sends[step - 1][...] = product.astype(BF)


def factor_kernel(scale, pos, mine, other, rows, high, low, basis, work, norm_ref, inverse, trail):
    core = pos[1]
    half, size = mine.shape
    work[pl.ds(pl.multiple_of(core * half, half), half), :] = mine[...]
    work[pl.ds(pl.multiple_of((1 - core) * half, half), half), :] = other[...]
    gram = work[...]
    row_id = lax.broadcasted_iota(jnp.int32, (size, size), 0)
    col_id = lax.broadcasted_iota(jnp.int32, (size, size), 1)
    eye = (row_id == col_id).astype(F32)
    diagonal = gram * eye
    scale_col = lax.rsqrt(jnp.sum(diagonal, axis=1, keepdims=True))
    scale_row = lax.rsqrt(jnp.sum(diagonal, axis=0, keepdims=True))
    excess = gram * scale_col * scale_row - eye
    below = (row_id > col_id).astype(F32)
    phi_mask = below + 0.5 * eye
    keep_mask = below + 2.0 * eye
    phi = excess * phi_mask
    near = -phi
    for step in range(3):
        mul = dot3 if step == 2 else (lambda a, b, dims=None: dot(a.astype(BF), b.astype(BF), dims))
        turn = excess + mul(near, excess)
        rest = near * keep_mask + turn + mul(near + turn, near, NT)
        phi = rest * phi_mask
        near = near - phi - mul(phi, near)
    worst = jnp.max(jnp.abs(phi))
    inverse[...] = (near + eye) * scale_row
    converged = worst < 1e-2

    @pl.when(jnp.logical_not(converged))
    def _():
        trail[...] = gram * scale_col * scale_row
        inverse[...] = eye

        def eliminate(k, carry):
            row = trail[pl.ds(k, 1), :]
            pivot = jnp.sum(jnp.where(col_id[:1] == k, row, 0.0), axis=1, keepdims=True)
            column = jnp.sum(jnp.where(col_id == k, trail[...], 0.0), axis=1, keepdims=True)
            factor = jnp.where(row_id[:, :1] > k, column / pivot, 0.0)
            source = inverse[pl.ds(k, 1), :]
            inverse[...] = inverse[...] - factor * source
            inverse[pl.ds(k, 1), :] = source * lax.rsqrt(pivot)
            trail[...] = trail[...] - factor * row
            return carry

        lax.fori_loop(0, size, eliminate, 0)
        inverse[...] = inverse[...] * scale_row

    scaled = inverse[...] * scale
    high_part, low_part = split(scaled)
    high[...] = high_part
    low[...] = low_part
    row_high, row_low = split(rows[...])
    basis[...] = (
        dot(row_high, high_part, NT) + (dot(row_high, low_part, NT) + dot(row_low, high_part, NT))
    ).astype(BF)


def project_kernel(scale, pos, high, low, *refs):
    chunks, out = refs[:-1], refs[-1]
    me = pos[2]
    share = chunks[0].shape[0]
    for step, chunk in enumerate(chunks):
        start = pl.multiple_of((me ^ step) * share, share)
        product = dot(chunk[...], high[...], NT) + dot(chunk[...], low[...], NT)
        out[pl.ds(start, share), :] = (product * scale).astype(BF)


def tree_sum(terms):
    while len(terms) > 1:
        terms = [terms[i] + terms[i + 1] for i in range(0, len(terms), 2)]
    return terms[0]


def shards(tiles, tile_rows, tile_cols, counts, omega):
    size_b = tiles.shape[1]
    rank = omega.shape[1]
    cols_here = omega.shape[0]
    col_blocks = cols_here // size_b
    row_groups = lax.axis_size("row")
    col_groups = lax.axis_size("col")
    zs = col_groups // CORES
    rows_here = RB_DEV * size_b
    share = rows_here // col_groups
    back_share = cols_here // row_groups
    total_rows = rows_here * row_groups
    half = rank // CORES
    index_col = lax.axis_index("col")
    pos = jnp.stack([index_col // CORES, index_col % CORES, lax.axis_index("row")]).astype(jnp.int32)

    def swap_core(x):
        return lax.ppermute(x, "col", [(i, i ^ 1) for i in range(col_groups)])

    def swap_z(x, step):
        return lax.ppermute(x, "col", [(i, i ^ (CORES * step)) for i in range(col_groups)])

    def swap_row(x, step):
        return lax.ppermute(x, "row", [(i, i ^ step) for i in range(row_groups)])

    def array(shape, kind):
        return jax.ShapeDtypeStruct(shape, kind)

    part = (share, rank)
    sent, kept = call(
        functools.partial(sketch_kernel, share),
        [(pos, 1), (counts, 1), (tile_rows, 1), (tile_cols, 1), (tiles, 0), (omega, 0)],
        [array((zs * share, rank), BF), array((zs * share, rank), F32)],
        [pltpu.VMEM((col_blocks, rows_here, size_b), BF)],
        flops=2 * rows_here * cols_here * rank,
        nbytes=6 * MIB,
        name="sketch",
    )
    came = swap_core(sent)
    (turned,) = call(
        transpose_kernel,
        [(counts, 1), (tile_rows, 1), (tile_cols, 1), (tiles, 0)],
        [array((RB_DEV, cols_here, size_b), BF)],
        nbytes=8 * MIB,
        name="turn",
    )
    own, *sends = call(
        functools.partial(pair_kernel, share),
        [(pos, 1), (kept, 0), (came, 0)],
        [array(part, F32)] + [array(part, BF)] * (zs - 1),
        nbytes=2 * MIB,
        name="pair",
    )
    gets = [swap_z(x, k + 1) for k, x in enumerate(sends)]
    own_rows, own_short = call(
        functools.partial(sum_kernel, len(gets)),
        [(own, 0)] + [(x, 0) for x in gets],
        [array(part, F32), array(part, BF)],
        nbytes=MIB,
        name="rows",
    )
    chunks = []
    for k in range(zs):
        chunk = swap_z(own_short, k) if k else own_short
        chunks += [chunk, swap_core(chunk)]
    full, gram = call(
        functools.partial(gram_kernel, share, zs),
        [(pos, 1)] + [(x, 0) for x in chunks],
        [array((rows_here, rank), BF), array((half, rank), F32)],
        flops=2 * rows_here * rank * half,
        nbytes=2 * MIB,
        name="gram",
    )
    gram_half = tree_sum([gram] + [swap_row(gram, k) for k in range(1, row_groups)])
    gram_other = swap_core(gram_half)
    back_own, *back_sends = call(
        back_kernel,
        [(pos, 1), (turned, 0), (full, 0)],
        [array((back_share, rank), F32)] + [array((back_share, rank), BF)] * (row_groups - 1),
        flops=2 * rows_here * cols_here * rank,
        nbytes=6 * MIB,
        name="back",
    )
    back_gets = [swap_row(x, k + 1) for k, x in enumerate(back_sends)]
    (back_sum,) = call(
        functools.partial(sum_kernel, len(back_gets)),
        [(back_own, 0)] + [(x, 0) for x in back_gets],
        [array((back_share, rank), BF)],
        nbytes=MIB,
        name="columns",
    )
    back_all = [back_sum] + [swap_row(back_sum, k) for k in range(1, row_groups)]
    high, low, basis = call(
        functools.partial(factor_kernel, float(total_rows) ** 0.5),
        [(pos, 1), (gram_half, 0), (gram_other, 0), (own_rows, 0)],
        [array((rank, rank), BF), array((rank, rank), BF), array(part, BF)],
        [pltpu.VMEM((rank, rank), F32), pltpu.SMEM((1,), F32), pltpu.VMEM((rank, rank), F32), pltpu.VMEM((rank, rank), F32)],
        flops=2 * 20 * rank**3,
        nbytes=MIB,
        name="factor",
    )
    (projected,) = call(
        functools.partial(project_kernel, float(RB_DEV * row_groups) ** -0.5),
        [(pos, 1), (high, 0), (low, 0)] + [(x, 0) for x in back_all],
        [array((cols_here, rank), BF)],
        flops=4 * cols_here * rank * rank,
        nbytes=2 * MIB,
        name="project",
    )
    return basis, projected


def solution(mesh):
    return jax.shard_map(
        shards,
        mesh=mesh,
        in_specs=(
            P(("row", "col"), None, None),
            P(("row", "col")),
            P(("row", "col")),
            P(("row", "col")),
            P("col", None),
        ),
        out_specs=(P(("row", "col"), None), P("col", None)),
        check_vma=False,
    )
```

time: 436 us -> 111 us (0.25)
  waiting for transfers between devices: 245 us -> 27.9 us
  other arithmetic: 62.3 us -> 0.11 us
  local copies, waits for them, and re-layouts: 66.1 us -> 4.26 us
  Pallas kernels: 0 us -> 54.8 us
  matrix products: 44.8 us -> 0 us
  starting transfers between devices: 0.3 us -> 22.2 us
  between operations: 15.8 us -> 1.4 us
    psum x3 -> x0, waiting for transfers between devices: 245 us -> none  [the longest x1 128 us: shards(): gram = lax.psum(local_gram, ('row', 'col'))]
    another operation x9 -> x1, other arithmetic: 55.4 us -> 0.08 us  [shards(): jnp.stack([index_col // CORES, index_col % CORES, lax.axis_index('row')])]
    pallas_call x0 -> x9, Pallas kernels: none -> 54.8 us  [call(): pl.pallas_call(body, out_shape=outs, in_specs=[smem() if scalar else vmem...]
    convert_element_type x4 -> x0, local copies, waits for them, and re-layouts: 36.2 us -> none  [the longest x2 18.1 us: block_sum(): high_part = terms.astype(jnp.bfloat16)]
    dot_general x7 -> x0, matrix products: 35.9 us -> none  [the longest x1 10.1 us: shards(): jnp.einsum('sij,sjk->sik', tiles, picked, preferred_element_type=jnp.floa...]
    ppermute x0 -> x21, waiting for transfers between devices: none -> 27.9 us  [the longest x6 19.5 us: swap_z(): lax.ppermute(x, 'col', [(i, i ^ CORES * step) for i in range(col_groups)])]
    ppermute x0 -> x21, starting transfers between devices: none -> 22.2 us  [the longest x9 11.2 us: swap_row(): return lax.ppermute(x, 'row', [(i, i ^ step) for i in range(row_groups)])]
    gather x2 -> x0, local copies, waits for them, and re-layouts: 14.2 us -> none  [the longest x1 7.2 us: shards(): basis_picked = group_basis.reshape(RB_DEV, size_b, rank)[tile_rows]]
  transfers between devices with their start and end apart: 3 -> 21, of which waited for: 3 -> 9; matrix products, arithmetic and copies ran while one was open for 1% -> 0% of each run, Pallas kernels for 0% -> 44%
where the time goes in v1:
time: 111 us
  Pallas kernels  54.8 us (49%)
  waiting for transfers between devices  27.9 us (25%)
  starting transfers between devices  22.2 us (20%)
  local copies, waits for them, and re-layouts  4.26 us (4%)
  between operations  1.4 us (1%)
    pallas_call x9, Pallas kernels, call(): pl.pallas_call(body, out_shape=outs, in_specs=[smem() if scalar else vmem...  54.8 us
    ppermute x6, waiting for transfers between devices, swap_z(): lax.ppermute(x, 'col', [(i, i ^ CORES * step) for i in range(col_groups)])  19.5 us
    ppermute x9, starting transfers between devices, swap_row(): return lax.ppermute(x, 'row', [(i, i ^ step) for i in range(row_groups)])  11.2 us
    ppermute x6, starting transfers between devices, swap_z(): lax.ppermute(x, 'col', [(i, i ^ CORES * step) for i in range(col_groups)])  10.2 us
    ppermute x9, waiting for transfers between devices, swap_row(): return lax.ppermute(x, 'row', [(i, i ^ step) for i in range(row_groups)])  5.61 us
    unnamed x14, local copies, waits for them, and re-layouts  4.26 us
    ppermute x6, waiting for transfers between devices, swap_core(): return lax.ppermute(x, 'col', [(i, i ^ 1) for i in range(col_groups)])  2.78 us
  transfers between devices with their start and end apart: 21, of which 9 were waited for; matrix products, arithmetic and copies ran while one was open for 0% of the time, Pallas kernels for 44%

profile of v1, /device:TPU:0, one launch (start us, length us, event | category | flops | bytes accessed | tf_op | source)
XLA Modules:
  0.0 110.6 jit_solution(9567748070386918847)
XLA Ops:
  1.4 1.9 %copy-done = bf16[96,128,128]{2,1,0:T(8,128)(2,1)S(1)} copy-done((bf16[96,128,128]{2,1,0:T(8,128)(2,1)S(1)}, bf16[96,128,128]{2,1,0:T(8,128)(2,1)}, u32[]{:S(2)}) %copy-start) | copy-done | bytes 3145752
  3.3 0.7 copy-done.2
  3.9 0.7 copy-done.4
  4.6 1.0 copy-done.6
  5.6 2.9 %sketch.1 = (bf16[1024,256]{1,0:T(8,128)(2,1)S(1)}, f32[1024,256]{1,0:T(8,128)S(1)}) custom-call(s32[3]{0:T(128)S(1)} %pad_add_fusion.pos, s32[1]{0:T(128)S(6)} %copy.7.counts, s32[96]{0:T(128)S(1)} %copy-done.2, s32[96]{0:T(128)S(1)} %copy-done.4, bf16[96,128,128]{2,1,0:T(8,128)(2,1)S(1)} %copy-done, bf16[1024,256]{1,0:T(8,128)(2,1)S(1)} %copy-done.6), custom_call_target="tpu_custom_call" | custom-call | flops 1073741824 | bytes 6291456 | tf_op jit(solution)/shard_map/sketch/pallas_call | solution.py:29
  8.8 1.8 %collective-permute-done.came = bf16[1024,256]{1,0:T(8,128)(2,1)S(1)} collective-permute-done((bf16[1024,256]{1,0:T(8,128)(2,1)S(1)}, bf16[1024,256]{1,0:T(8,128)(2,1)S(1)}, u32[]{:S(2)}, u32[]{:S(2)}) %collective-permute-start) | collective-permute-done | bytes 524320 | tf_op jit(solution)/shard_map/ppermute | solution.py:227
  10.5 0.7 pair.1
  11.2 2.9 %collective-permute-start.1 = (bf16[256,256]{1,0:T(8,128)(2,1)S(1)}, bf16[256,256]{1,0:T(8,128)(2,1)S(1)}, u32[]{:S(2)}, u32[]{:S(2)}) collective-permute-start(bf16[256,256]{1,0:T(8,128)(2,1)S(1)} %get-tuple-element.22), channel_id=1, source_target_pairs={{0,2},{1,3},{2,0},{3,1},{4,6},{5,7},{6,4},{7,5},{8,10},{9,11},{10,... | collective-permute-start | bytes 393224 | tf_op jit(solution)/shard_map/ppermute | solution.py:230
  14.1 2.8 %collective-permute-start.2 = (bf16[256,256]{1,0:T(8,128)(2,1)S(1)}, bf16[256,256]{1,0:T(8,128)(2,1)S(1)}, u32[]{:S(2)}, u32[]{:S(2)}) collective-permute-start(bf16[256,256]{1,0:T(8,128)(2,1)S(1)} %get-tuple-element.23), channel_id=1, source_target_pairs={{0,4},{1,5},{2,6},{3,7},{4,0},{5,1},{6,2},{7,3},{8,12},{9,13},{10,... | collective-permute-start | bytes 393224 | tf_op jit(solution)/shard_map/ppermute | solution.py:230
  17.0 2.9 %collective-permute-done.1.refs_0_ = bf16[256,256]{1,0:T(8,128)(2,1)S(1)} collective-permute-done((bf16[256,256]{1,0:T(8,128)(2,1)S(1)}, bf16[256,256]{1,0:T(8,128)(2,1)S(1)}, u32[]{:S(2)}, u32[]{:S(2)}) %collective-permute-start.1) | collective-permute-done | bytes 131104 | tf_op jit(solution)/shard_map/ppermute | solution.py:230
  19.9 7.2 %collective-permute-done.2.refs_1_ = bf16[256,256]{1,0:T(8,128)(2,1)S(1)} collective-permute-done((bf16[256,256]{1,0:T(8,128)(2,1)S(1)}, bf16[256,256]{1,0:T(8,128)(2,1)S(1)}, u32[]{:S(2)}, u32[]{:S(2)}) %collective-permute-start.2) | collective-permute-done | bytes 131104 | tf_op jit(solution)/shard_map/ppermute | solution.py:230
  27.1 2.6 %collective-permute-start.9 = (bf16[256,256]{1,0:T(8,128)(2,1)S(1)}, bf16[256,256]{1,0:T(8,128)(2,1)S(1)}, u32[]{:S(2)}, u32[]{:S(2)}) collective-permute-start(bf16[256,256]{1,0:T(8,128)(2,1)S(1)} %get-tuple-element.25.refs_0_), channel_id=1, source_target_pairs={{0,6},{1,7},{2,4},{3,5},{4,2},{5,3},{6,0},{7,1},{8,14},{9,15},{10,... | collective-permute-start | bytes 393224 | tf_op jit(solution)/shard_map/ppermute | solution.py:230
  29.7 1.4 %collective-permute-start.7 = (bf16[256,256]{1,0:T(8,128)(2,1)S(1)}, bf16[256,256]{1,0:T(8,128)(2,1)S(1)}, u32[]{:S(2)}, u32[]{:S(2)}) collective-permute-start(bf16[256,256]{1,0:T(8,128)(2,1)S(1)} %get-tuple-element.25.refs_0_), channel_id=1, source_target_pairs={{0,4},{1,5},{2,6},{3,7},{4,0},{5,1},{6,2},{7,3},{8,12},{9,13},{10,... | collective-permute-start | bytes 393224 | tf_op jit(solution)/shard_map/ppermute | solution.py:230
  31.1 0.5 collective-permute-start.5
  31.6 3.5 %collective-permute-done.9.refs_6_ = bf16[256,256]{1,0:T(8,128)(2,1)S(1)} collective-permute-done((bf16[256,256]{1,0:T(8,128)(2,1)S(1)}, bf16[256,256]{1,0:T(8,128)(2,1)S(1)}, u32[]{:S(2)}, u32[]{:S(2)}) %collective-permute-start.9) | collective-permute-done | bytes 131104 | tf_op jit(solution)/shard_map/ppermute | solution.py:230
  35.1 5.9 %collective-permute-done.7.refs_4_ = bf16[256,256]{1,0:T(8,128)(2,1)S(1)} collective-permute-done((bf16[256,256]{1,0:T(8,128)(2,1)S(1)}, bf16[256,256]{1,0:T(8,128)(2,1)S(1)}, u32[]{:S(2)}, u32[]{:S(2)}) %collective-permute-start.7) | collective-permute-done | bytes 131104 | tf_op jit(solution)/shard_map/ppermute | solution.py:230
  41.0 0.5 collective-permute-start.6
  41.5 0.8 collective-permute-done.8.refs_5_
  42.6 1.0 gram.1
  43.5 2.3 %collective-permute-start.13 = (f32[128,256]{1,0:T(8,128)S(1)}, f32[128,256]{1,0:T(8,128)S(1)}, u32[]{:S(2)}, u32[]{:S(2)}) collective-permute-start(f32[128,256]{1,0:T(8,128)S(1)} %get-tuple-element.26), channel_id=1, source_target_pairs={{0,24},{8,16},{16,8},{24,0},{1,25},{9,17},{17,9},{25,1},{2,26},{10... | collective-permute-start | bytes 393224 | tf_op jit(solution)/shard_map/ppermute | solution.py:233
  45.9 0.8 collective-permute-start.12
  47.1 6.2 %turn.1.turned = bf16[16,1024,128]{2,1,0:T(8,128)(2,1)S(1)} custom-call(s32[1]{0:T(128)S(6)} %copy.7.counts, s32[96]{0:T(128)S(1)} %copy-done.3, s32[96]{0:T(128)S(1)} %copy-done.5, bf16[96,128,128]{2,1,0:T(8,128)(2,1)S(1)} %copy-done.1), custom_call_target="tpu_custom_call" | custom-call | bytes 8388608 | tf_op jit(solution)/shard_map/turn/pallas_call | solution.py:29
  53.3 1.8 %back.1 = (f32[256,256]{1,0:T(8,128)S(1)}, bf16[256,256]{1,0:T(8,128)(2,1)S(1)}, bf16[256,256]{1,0:T(8,128)(2,1)S(1)}, bf16[256,256]{1,0:T(8,128)(2,1)S(1)}) custom-call(s32[3]{0:T(128)S(1)} %pad_add_fusion.pos, bf16[16,1024,128]{2,1,0:T(8,128)(2,1)S(1)} %turn.1.turned, bf16[2048,256]{1,0:T(8,128)(2,1)S(1)} %get-tuple-element.31.full), custom_call_target="tpu_custom_call" | custom-call | flops 1073741824 | bytes 6291456 | tf_op jit(solution)/shard_map/back/pallas_call | solution.py:29
  55.0 2.5 %collective-permute-start.15 = (bf16[256,256]{1,0:T(8,128)(2,1)S(1)}, bf16[256,256]{1,0:T(8,128)(2,1)S(1)}, u32[]{:S(2)}, u32[]{:S(2)}) collective-permute-start(bf16[256,256]{1,0:T(8,128)(2,1)S(1)} %get-tuple-element.33), channel_id=1, source_target_pairs={{0,8},{8,0},{16,24},{24,16},{1,9},{9,1},{17,25},{25,17},{2,10},{10... | collective-permute-start | bytes 393224 | tf_op jit(solution)/shard_map/ppermute | solution.py:233
  57.6 1.5 %collective-permute-start.17 = (bf16[256,256]{1,0:T(8,128)(2,1)S(1)}, bf16[256,256]{1,0:T(8,128)(2,1)S(1)}, u32[]{:S(2)}, u32[]{:S(2)}) collective-permute-start(bf16[256,256]{1,0:T(8,128)(2,1)S(1)} %get-tuple-element.35), channel_id=1, source_target_pairs={{0,24},{8,16},{16,8},{24,0},{1,25},{9,17},{17,9},{25,1},{2,26},{10... | collective-permute-start | bytes 393224 | tf_op jit(solution)/shard_map/ppermute | solution.py:233
  59.2 2.4 %collective-permute-done.15.refs_0_ = bf16[256,256]{1,0:T(8,128)(2,1)S(1)} collective-permute-done((bf16[256,256]{1,0:T(8,128)(2,1)S(1)}, bf16[256,256]{1,0:T(8,128)(2,1)S(1)}, u32[]{:S(2)}, u32[]{:S(2)}) %collective-permute-start.15) | collective-permute-done | bytes 131104 | tf_op jit(solution)/shard_map/ppermute | solution.py:233
  61.6 3.2 %collective-permute-done.16.refs_1_ = bf16[256,256]{1,0:T(8,128)(2,1)S(1)} collective-permute-done((bf16[256,256]{1,0:T(8,128)(2,1)S(1)}, bf16[256,256]{1,0:T(8,128)(2,1)S(1)}, u32[]{:S(2)}, u32[]{:S(2)}) %collective-permute-start.16) | collective-permute-done | bytes 131104 | tf_op jit(solution)/shard_map/ppermute | solution.py:233
  64.9 1.4 %collective-permute-start.20 = (bf16[256,256]{1,0:T(8,128)(2,1)S(1)}, bf16[256,256]{1,0:T(8,128)(2,1)S(1)}, u32[]{:S(2)}, u32[]{:S(2)}) collective-permute-start(bf16[256,256]{1,0:T(8,128)(2,1)S(1)} %columns.1.refs_0_), channel_id=1, source_target_pairs={{0,24},{8,16},{16,8},{24,0},{1,25},{9,17},{17,9},{25,1},{2,26},{10... | collective-permute-start | bytes 393224 | tf_op jit(solution)/shard_map/ppermute | solution.py:233
  66.3 0.8 collective-permute-start.19
  67.0 1.4 %collective-permute-start.18 = (bf16[256,256]{1,0:T(8,128)(2,1)S(1)}, bf16[256,256]{1,0:T(8,128)(2,1)S(1)}, u32[]{:S(2)}, u32[]{:S(2)}) collective-permute-start(bf16[256,256]{1,0:T(8,128)(2,1)S(1)} %columns.1.refs_0_), channel_id=1, source_target_pairs={{0,8},{8,0},{16,24},{24,16},{1,9},{9,1},{17,25},{25,17},{2,10},{10... | collective-permute-start | bytes 393224 | tf_op jit(solution)/shard_map/ppermute | solution.py:233
  68.4 40.4 %factor.1 = (bf16[256,256]{1,0:T(8,128)(2,1)S(1)}, bf16[256,256]{1,0:T(8,128)(2,1)S(1)}, bf16[256,256]{1,0:T(8,128)(2,1)}) custom-call(s32[3]{0:T(128)S(1)} %pad_add_fusion.pos, f32[128,256]{1,0:T(8,128)S(1)} %add_add_fusion.mine, f32[128,256]{1,0:T(8,128)S(1)} %collective-permute-done.14.other, f32[256,256]{1,0:T(8,128)S(1)} %get-tuple-element.27.rows), custom_call_target="tpu_custom_call" | custom-call | flops 671088640 | bytes 1048576 | tf_op jit(solution)/shard_map/factor/pallas_call | solution.py:29
  108.8 1.8 %project.1 = bf16[1024,256]{1,0:T(8,128)(2,1)} custom-call(s32[3]{0:T(128)S(1)} %pad_add_fusion.pos, bf16[256,256]{1,0:T(8,128)(2,1)S(1)} %get-tuple-element.29.high, bf16[256,256]{1,0:T(8,128)(2,1)S(1)} %get-tuple-element.30.low, bf16[256,256]{1,0:T(8,128)(2,1)S(1)} %columns.1.refs_0_, bf16[256,256]{1,0:T(8,128)(2,1)S(1)} %collective-permute-done.18.refs_1_, ...), custom_call_target="tpu_custom_call" | custom-call | flops 268435456 | bytes 2097152 | tf_op jit(solution)/shard_map/project/pallas_call | solution.py:29
  (35 shorter events, 1.2 us)
Async XLA Ops:
  0.6 46.5 %copy-start.5 = (s32[96]{0:T(128)S(1)}, s32[96]{0:T(128)}, u32[]{:S(2)}) copy-start(s32[96]{0:T(128)} %cols.3) | copy-start | bytes 1156
  0.6 46.4 %copy-start.3 = (s32[96]{0:T(128)S(1)}, s32[96]{0:T(128)}, u32[]{:S(2)}) copy-start(s32[96]{0:T(128)} %rows.5) | copy-start | bytes 1156
  1.4 1.9 %copy-start = (bf16[96,128,128]{2,1,0:T(8,128)(2,1)S(1)}, bf16[96,128,128]{2,1,0:T(8,128)(2,1)}, u32[]{:S(2)}) copy-start(bf16[96,128,128]{2,1,0:T(8,128)(2,1)} %tiles.3) | copy-start | bytes 9437188
  3.3 0.7 copy-start.2
  3.9 0.7 copy-start.4
  4.6 1.0 copy-start.6
  5.6 41.4 %copy-start.1 = (bf16[96,128,128]{2,1,0:T(8,128)(2,1)S(1)}, bf16[96,128,128]{2,1,0:T(8,128)(2,1)}, u32[]{:S(2)}) copy-start(bf16[96,128,128]{2,1,0:T(8,128)(2,1)} %tiles.3) | copy-start | bytes 9437188
  8.6 2.0 %collective-permute-start = (bf16[1024,256]{1,0:T(8,128)(2,1)S(1)}, bf16[1024,256]{1,0:T(8,128)(2,1)S(1)}, u32[]{:S(2)}, u32[]{:S(2)}) collective-permute-start(bf16[1024,256]{1,0:T(8,128)(2,1)S(1)} %get-tuple-element.20), channel_id=1, source_target_pairs={{0,1},{1,0},{2,3},{3,2},{4,5},{5,4},{6,7},{7,6},{8,9},{9,8},{10,11... | collective-permute-start | bytes 1572872 | tf_op jit(solution)/shard_map/ppermute | solution.py:227
  11.2 8.7 %collective-permute-start.1 = (bf16[256,256]{1,0:T(8,128)(2,1)S(1)}, bf16[256,256]{1,0:T(8,128)(2,1)S(1)}, u32[]{:S(2)}, u32[]{:S(2)}) collective-permute-start(bf16[256,256]{1,0:T(8,128)(2,1)S(1)} %get-tuple-element.22), channel_id=1, source_target_pairs={{0,2},{1,3},{2,0},{3,1},{4,6},{5,7},{6,4},{7,5},{8,10},{9,11},{10,... | collective-permute-start | bytes 393224 | tf_op jit(solution)/shard_map/ppermute | solution.py:230
  14.1 12.9 %collective-permute-start.2 = (bf16[256,256]{1,0:T(8,128)(2,1)S(1)}, bf16[256,256]{1,0:T(8,128)(2,1)S(1)}, u32[]{:S(2)}, u32[]{:S(2)}) collective-permute-start(bf16[256,256]{1,0:T(8,128)(2,1)S(1)} %get-tuple-element.23), channel_id=1, source_target_pairs={{0,4},{1,5},{2,6},{3,7},{4,0},{5,1},{6,2},{7,3},{8,12},{9,13},{10,... | collective-permute-start | bytes 393224 | tf_op jit(solution)/shard_map/ppermute | solution.py:230
  17.0 10.1 %collective-permute-start.3 = (bf16[256,256]{1,0:T(8,128)(2,1)S(1)}, bf16[256,256]{1,0:T(8,128)(2,1)S(1)}, u32[]{:S(2)}, u32[]{:S(2)}) collective-permute-start(bf16[256,256]{1,0:T(8,128)(2,1)S(1)} %get-tuple-element.24), channel_id=1, source_target_pairs={{0,6},{1,7},{2,4},{3,5},{4,2},{5,3},{6,0},{7,1},{8,14},{9,15},{10,... | collective-permute-start | bytes 393224 | tf_op jit(solution)/shard_map/ppermute | solution.py:230
  27.1 8.0 %collective-permute-start.9 = (bf16[256,256]{1,0:T(8,128)(2,1)S(1)}, bf16[256,256]{1,0:T(8,128)(2,1)S(1)}, u32[]{:S(2)}, u32[]{:S(2)}) collective-permute-start(bf16[256,256]{1,0:T(8,128)(2,1)S(1)} %get-tuple-element.25.refs_0_), channel_id=1, source_target_pairs={{0,6},{1,7},{2,4},{3,5},{4,2},{5,3},{6,0},{7,1},{8,14},{9,15},{10,... | collective-permute-start | bytes 393224 | tf_op jit(solution)/shard_map/ppermute | solution.py:230
  29.7 11.3 %collective-permute-start.7 = (bf16[256,256]{1,0:T(8,128)(2,1)S(1)}, bf16[256,256]{1,0:T(8,128)(2,1)S(1)}, u32[]{:S(2)}, u32[]{:S(2)}) collective-permute-start(bf16[256,256]{1,0:T(8,128)(2,1)S(1)} %get-tuple-element.25.refs_0_), channel_id=1, source_target_pairs={{0,4},{1,5},{2,6},{3,7},{4,0},{5,1},{6,2},{7,3},{8,12},{9,13},{10,... | collective-permute-start | bytes 393224 | tf_op jit(solution)/shard_map/ppermute | solution.py:230
  31.1 9.9 %collective-permute-start.5 = (bf16[256,256]{1,0:T(8,128)(2,1)S(1)}, bf16[256,256]{1,0:T(8,128)(2,1)S(1)}, u32[]{:S(2)}, u32[]{:S(2)}) collective-permute-start(bf16[256,256]{1,0:T(8,128)(2,1)S(1)} %get-tuple-element.25.refs_0_), channel_id=1, source_target_pairs={{0,2},{1,3},{2,0},{3,1},{4,6},{5,7},{6,4},{7,5},{8,10},{9,11},{10,... | collective-permute-start | bytes 393224 | tf_op jit(solution)/shard_map/ppermute | solution.py:230
  31.6 10.0 %collective-permute-start.4 = (bf16[256,256]{1,0:T(8,128)(2,1)S(1)}, bf16[256,256]{1,0:T(8,128)(2,1)S(1)}, u32[]{:S(2)}, u32[]{:S(2)}) collective-permute-start(bf16[256,256]{1,0:T(8,128)(2,1)S(1)} %get-tuple-element.25.refs_0_), channel_id=1, source_target_pairs={{0,1},{1,0},{2,3},{3,2},{4,5},{5,4},{6,7},{7,6},{8,9},{9,8},{10,11... | collective-permute-start | bytes 393224 | tf_op jit(solution)/shard_map/ppermute | solution.py:227
  35.1 6.4 %collective-permute-start.10 = (bf16[256,256]{1,0:T(8,128)(2,1)S(1)}, bf16[256,256]{1,0:T(8,128)(2,1)S(1)}, u32[]{:S(2)}, u32[]{:S(2)}) collective-permute-start(bf16[256,256]{1,0:T(8,128)(2,1)S(1)} %collective-permute-done.9.refs_6_), channel_id=1, source_target_pairs={{0,1},{1,0},{2,3},{3,2},{4,5},{5,4},{6,7},{7,6},{8,9},{9,8},{10,11... | collective-permute-start | bytes 393224 | tf_op jit(solution)/shard_map/ppermute | solution.py:227
  41.0 1.3 %collective-permute-start.8 = (bf16[256,256]{1,0:T(8,128)(2,1)S(1)}, bf16[256,256]{1,0:T(8,128)(2,1)S(1)}, u32[]{:S(2)}, u32[]{:S(2)}) collective-permute-start(bf16[256,256]{1,0:T(8,128)(2,1)S(1)} %collective-permute-done.7.refs_4_), channel_id=1, source_target_pairs={{0,1},{1,0},{2,3},{3,2},{4,5},{5,4},{6,7},{7,6},{8,9},{9,8},{10,11... | collective-permute-start | bytes 393224 | tf_op jit(solution)/shard_map/ppermute | solution.py:227
  41.0 1.5 %collective-permute-start.6 = (bf16[256,256]{1,0:T(8,128)(2,1)S(1)}, bf16[256,256]{1,0:T(8,128)(2,1)S(1)}, u32[]{:S(2)}, u32[]{:S(2)}) collective-permute-start(bf16[256,256]{1,0:T(8,128)(2,1)S(1)} %collective-permute-done.5.refs_2_), channel_id=1, source_target_pairs={{0,1},{1,0},{2,3},{3,2},{4,5},{5,4},{6,7},{7,6},{8,9},{9,8},{10,11... | collective-permute-start | bytes 393224 | tf_op jit(solution)/shard_map/ppermute | solution.py:227
  43.5 14.0 %collective-permute-start.13 = (f32[128,256]{1,0:T(8,128)S(1)}, f32[128,256]{1,0:T(8,128)S(1)}, u32[]{:S(2)}, u32[]{:S(2)}) collective-permute-start(f32[128,256]{1,0:T(8,128)S(1)} %get-tuple-element.26), channel_id=1, source_target_pairs={{0,24},{8,16},{16,8},{24,0},{1,25},{9,17},{17,9},{25,1},{2,26},{10... | collective-permute-start | bytes 393224 | tf_op jit(solution)/shard_map/ppermute | solution.py:233
  45.9 13.2 %collective-permute-start.12 = (f32[128,256]{1,0:T(8,128)S(1)}, f32[128,256]{1,0:T(8,128)S(1)}, u32[]{:S(2)}, u32[]{:S(2)}) collective-permute-start(f32[128,256]{1,0:T(8,128)S(1)} %get-tuple-element.26), channel_id=1, source_target_pairs={{0,16},{8,24},{16,0},{24,8},{1,17},{9,25},{17,1},{25,9},{2,18},{10... | collective-permute-start | bytes 393224 | tf_op jit(solution)/shard_map/ppermute | solution.py:233
  46.7 12.5 %collective-permute-start.11 = (f32[128,256]{1,0:T(8,128)S(1)}, f32[128,256]{1,0:T(8,128)S(1)}, u32[]{:S(2)}, u32[]{:S(2)}) collective-permute-start(f32[128,256]{1,0:T(8,128)S(1)} %get-tuple-element.26), channel_id=1, source_target_pairs={{0,8},{8,0},{16,24},{24,16},{1,9},{9,1},{17,25},{25,17},{2,10},{10... | collective-permute-start | bytes 393224 | tf_op jit(solution)/shard_map/ppermute | solution.py:233
  55.0 6.5 %collective-permute-start.15 = (bf16[256,256]{1,0:T(8,128)(2,1)S(1)}, bf16[256,256]{1,0:T(8,128)(2,1)S(1)}, u32[]{:S(2)}, u32[]{:S(2)}) collective-permute-start(bf16[256,256]{1,0:T(8,128)(2,1)S(1)} %get-tuple-element.33), channel_id=1, source_target_pairs={{0,8},{8,0},{16,24},{24,16},{1,9},{9,1},{17,25},{25,17},{2,10},{10... | collective-permute-start | bytes 393224 | tf_op jit(solution)/shard_map/ppermute | solution.py:233
  57.6 7.3 %collective-permute-start.16 = (bf16[256,256]{1,0:T(8,128)(2,1)S(1)}, bf16[256,256]{1,0:T(8,128)(2,1)S(1)}, u32[]{:S(2)}, u32[]{:S(2)}) collective-permute-start(bf16[256,256]{1,0:T(8,128)(2,1)S(1)} %get-tuple-element.34), channel_id=1, source_target_pairs={{0,16},{8,24},{16,0},{24,8},{1,17},{9,25},{17,1},{25,9},{2,18},{10... | collective-permute-start | bytes 393224 | tf_op jit(solution)/shard_map/ppermute | solution.py:233
  57.6 7.3 %collective-permute-start.17 = (bf16[256,256]{1,0:T(8,128)(2,1)S(1)}, bf16[256,256]{1,0:T(8,128)(2,1)S(1)}, u32[]{:S(2)}, u32[]{:S(2)}) collective-permute-start(bf16[256,256]{1,0:T(8,128)(2,1)S(1)} %get-tuple-element.35), channel_id=1, source_target_pairs={{0,24},{8,16},{16,8},{24,0},{1,25},{9,17},{17,9},{25,1},{2,26},{10... | collective-permute-start | bytes 393224 | tf_op jit(solution)/shard_map/ppermute | solution.py:233
  59.1 9.3 %collective-permute-start.14 = (f32[128,256]{1,0:T(8,128)S(1)}, f32[128,256]{1,0:T(8,128)S(1)}, u32[]{:S(2)}, u32[]{:S(2)}) collective-permute-start(f32[128,256]{1,0:T(8,128)S(1)} %add_add_fusion.mine), channel_id=1, source_target_pairs={{0,1},{1,0},{2,3},{3,2},{4,5},{5,4},{6,7},{7,6},{8,9},{9,8},{10,11... | collective-permute-start | bytes 393224 | tf_op jit(solution)/shard_map/ppermute | solution.py:227
  64.9 43.9 %collective-permute-start.20 = (bf16[256,256]{1,0:T(8,128)(2,1)S(1)}, bf16[256,256]{1,0:T(8,128)(2,1)S(1)}, u32[]{:S(2)}, u32[]{:S(2)}) collective-permute-start(bf16[256,256]{1,0:T(8,128)(2,1)S(1)} %columns.1.refs_0_), channel_id=1, source_target_pairs={{0,24},{8,16},{16,8},{24,0},{1,25},{9,17},{17,9},{25,1},{2,26},{10... | collective-permute-start | bytes 393224 | tf_op jit(solution)/shard_map/ppermute | solution.py:233
  66.3 42.6 %collective-permute-start.19 = (bf16[256,256]{1,0:T(8,128)(2,1)S(1)}, bf16[256,256]{1,0:T(8,128)(2,1)S(1)}, u32[]{:S(2)}, u32[]{:S(2)}) collective-permute-start(bf16[256,256]{1,0:T(8,128)(2,1)S(1)} %columns.1.refs_0_), channel_id=1, source_target_pairs={{0,16},{8,24},{16,0},{24,8},{1,17},{9,25},{17,1},{25,9},{2,18},{10... | collective-permute-start | bytes 393224 | tf_op jit(solution)/shard_map/ppermute | solution.py:233
  67.0 41.8 %collective-permute-start.18 = (bf16[256,256]{1,0:T(8,128)(2,1)S(1)}, bf16[256,256]{1,0:T(8,128)(2,1)S(1)}, u32[]{:S(2)}, u32[]{:S(2)}) collective-permute-start(bf16[256,256]{1,0:T(8,128)(2,1)S(1)} %columns.1.refs_0_), channel_id=1, source_target_pairs={{0,8},{8,0},{16,24},{24,16},{1,9},{9,1},{17,25},{25,17},{2,10},{10... | collective-permute-start | bytes 393224 | tf_op jit(solution)/shard_map/ppermute | solution.py:233

commit v2 on v1

v2 whole, which is shorter than its diff:
```python
import functools

import jax
import jax.numpy as jnp
from jax import lax
from jax.experimental import pallas as pl
from jax.experimental.pallas import tpu as pltpu
from jax.sharding import PartitionSpec as P

RB_DEV = 16
CORES = 2
LOADS = 4
TOKEN = (8, 128)
CODE = 256
LANES = 128
SKETCH_LIMIT = 50
TURN_LIMIT = 44
MIB = 1024 * 1024
BF = jnp.bfloat16
F32 = jnp.float32

NN = (((1,), (0,)), ((), ()))
NT = (((1,), (1,)), ((), ()))
TN = (((0,), (0,)), ((), ()))

SPACES = {"v": pltpu.VMEM, "s": pltpu.SMEM, "h": pltpu.HBM, "a": pl.ANY}


def call(name, body, ins, outs, scratch=(), limit=24, flops=0, nbytes=0):
    return pl.pallas_call(
        body,
        out_shape=outs,
        in_specs=[pl.BlockSpec(memory_space=SPACES[space]) for space, _ in ins],
        out_specs=[pl.BlockSpec(memory_space=pltpu.VMEM) for _ in outs],
        scratch_shapes=list(scratch),
        compiler_params=pltpu.CompilerParams(vmem_limit_bytes=limit * MIB),
        cost_estimate=pl.CostEstimate(flops=flops, bytes_accessed=nbytes, transcendentals=0),
        name=name,
    )(*[array for _, array in ins])


def dot(a, b, dims=NN):
    return lax.dot_general(a, b, dims, preferred_element_type=F32)


def dot_short(a, b, dims=NN):
    return dot(a.astype(BF), b.astype(BF), dims)


def split(x):
    high = x.astype(BF)
    return high, (x - high.astype(F32)).astype(BF)


def dot_long(a, b, dims=NN):
    a_high, a_low = split(a)
    b_high, b_low = split(b)
    return dot(a_high, b_high, dims) + (dot(a_high, b_low, dims) + dot(a_low, b_high, dims))


def place():
    col = lax.axis_index("col")
    return col // CORES, col % CORES


def far_first(count):
    return [count - 1] + list(range(1, count - 1))


def rows_at(index, count):
    return pl.ds(pl.multiple_of(index * count, count), count)


def put_live(codes, codes_smem, tiles_hbm, tiles, sems, clear, put):
    load = tiles.shape[0] // LOADS
    first = pltpu.make_async_copy(codes, codes_smem, sems.at[LOADS])
    first.start()
    copies = []
    for k in range(LOADS):
        piece = pl.ds(k * load, load)
        copies.append(pltpu.make_async_copy(tiles_hbm.at[piece], tiles.at[piece], sems.at[k]))
    for copy in copies:
        copy.start()
    clear()
    first.wait()

    def step(slot, carry):
        code = codes_smem[slot]
        put(slot, code // CODE, code % CODE)
        return carry

    live = codes_smem[tiles.shape[0]]
    for k, copy in enumerate(copies):
        copy.wait()
        lax.fori_loop(k * load, jnp.clip(live, k * load, (k + 1) * load), step, 0)


def sketch_kernel(share, codes, tiles_hbm, omega_hbm, sent, kept, codes_smem, tiles, omega, dense, sems):
    size_b = tiles.shape[1]
    last = pltpu.make_async_copy(omega_hbm, omega, sems.at[LOADS + 1])
    last.start()

    def clear():
        dense[...] = jnp.zeros_like(dense)

    def put(slot, row, col):
        dense[col, rows_at(row, size_b), :] = tiles[slot]

    put_live(codes, codes_smem, tiles_hbm, tiles, sems, clear, put)
    last.wait()
    _, core = place()
    for out, owner in ((sent, 1 - core), (kept, core)):
        for step in range(out.shape[0] // share):
            here = rows_at(step * CORES + owner, share)
            left = jnp.concatenate([dense[c, here, :] for c in range(dense.shape[0])], axis=1)
            out[step * share : (step + 1) * share, :] = dot(left, omega[...]).astype(out.dtype)


def turn_kernel(codes, tiles_hbm, _, turned, token, codes_smem, tiles, sems):
    size_b = tiles.shape[1]
    token[...] = jnp.zeros_like(token)

    def clear():
        turned[...] = jnp.zeros_like(turned)

    def put(slot, row, col):
        turned[row, rows_at(col, size_b), :] = tiles[slot].T

    put_live(codes, codes_smem, tiles_hbm, tiles, sems, clear, put)


def pair_kernel(share, kept, came, own, token, *sends):
    z, _ = place()
    token[...] = jnp.zeros_like(token)
    for step in range(len(sends) + 1):
        here = rows_at(z ^ step, share)
        total = kept[here, :] + came[here, :].astype(F32)
        if step == 0:
            own[...] = total
        else:
            sends[step - 1][...] = total.astype(BF)


def columns_kernel(count, own, *refs):
    total = own[...]
    for ref in refs[:count]:
        total = total + ref[...].astype(F32)
    refs[count][...] = total.astype(BF)


def tree_kernel(own, *refs):
    refs[-1][...] = tree_sum([own[...]] + [ref[...] for ref in reversed(refs[:-1])])


def tree_sum(terms):
    while len(terms) > 1:
        terms = [terms[i] + terms[i + 1] for i in range(0, len(terms), 2)]
    return terms[0]


def rows_kernel(count, own, *refs):
    total = own[...]
    for ref in refs[:count]:
        total = total + ref[...].astype(F32)
    refs[-2][...] = total
    refs[-1][...] = total.astype(BF)


def pack_kernel(order, own, *refs):
    out = refs[-1]
    z, _ = place()
    share = own.shape[0]
    out[rows_at(z, share), :] = own[...]
    for step, ref in zip(order, refs):
        out[rows_at(z ^ step, share), :] = ref[...]


def full_kernel(share, mine, other, full):
    _, core = place()
    for z in range(mine.shape[0] // share):
        here = slice(z * share, (z + 1) * share)
        full[rows_at(z * CORES + core, share), :] = mine[here, :]
        full[rows_at(z * CORES + (1 - core), share), :] = other[here, :]


def back_kernel(turned, full, own, gram, *sends):
    me = lax.axis_index("row")
    _, core = place()
    share = own.shape[0]
    half = gram.shape[1]
    quarter = half // CORES
    for side in range(CORES):

        @pl.when(core == side)
        def _():
            diagonal = full[:, side * half : (side + 1) * half]
            gram[:half, :] = dot(diagonal, diagonal, TN)
            lower = full[:, half + side * quarter : half + (side + 1) * quarter]
            gram[half:, :] = dot(lower, full[:, :half], TN)

    for step in list(range(1, len(sends) + 1)) + [0]:
        here = rows_at(me ^ step, share)
        left = jnp.concatenate([turned[r, here, :] for r in range(turned.shape[0])], axis=1)
        product = dot(left, full[...])
        if step == 0:
            own[...] = product
        else:
            sends[step - 1][...] = product.astype(BF)


def factor_kernel(scale, *refs):
    mine, other, rows, high, low, basis, work, inverse = refs
    _, core = place()
    size = work.shape[0]
    half, quarter = size // CORES, size // (2 * CORES)
    for source, owner in ((mine, core), (other, 1 - core)):
        for side in range(CORES):

            @pl.when(owner == side)
            def _():
                work[side * half : (side + 1) * half, side * half : (side + 1) * half] = source[:half, :]
                here = slice(half + side * quarter, half + (side + 1) * quarter)
                work[here, :half] = source[half:, :]
    work[:half, half:] = work[half:, :half].T
    gram = work[...]
    row_id = lax.broadcasted_iota(jnp.int32, (size, size), 0)
    col_id = lax.broadcasted_iota(jnp.int32, (size, size), 1)
    eye = (row_id == col_id).astype(F32)
    diagonal = gram * eye
    scale_col = lax.rsqrt(jnp.sum(diagonal, axis=1, keepdims=True))
    scale_row = lax.rsqrt(jnp.sum(diagonal, axis=0, keepdims=True))
    excess = gram * scale_col * scale_row - eye
    below = (row_id > col_id).astype(F32)
    phi_mask = below + 0.5 * eye
    keep_mask = below + 2.0 * eye
    near = -(excess * phi_mask)
    for step in range(3):
        mul = dot_long if step == 2 else dot_short
        turn = excess + mul(near, excess)
        rest = near * keep_mask + turn + mul(near + turn, near, NT)
        phi = rest * phi_mask
        near = near - phi - mul(phi, near)
    inverse[...] = (near + eye) * scale_row
    converged = jnp.max(jnp.abs(phi)) < 1e-2

    @pl.when(jnp.logical_not(converged))
    def _():
        work[...] = gram * scale_col * scale_row
        inverse[...] = eye

        def eliminate(k, carry):
            row = work[pl.ds(k, 1), :]
            pivot = jnp.sum(jnp.where(col_id[:1] == k, row, 0.0), axis=1, keepdims=True)
            column = jnp.sum(jnp.where(col_id == k, work[...], 0.0), axis=1, keepdims=True)
            factor = jnp.where(row_id[:, :1] > k, column / pivot, 0.0)
            source = inverse[pl.ds(k, 1), :]
            inverse[...] = inverse[...] - factor * source
            inverse[pl.ds(k, 1), :] = source * lax.rsqrt(pivot)
            work[...] = work[...] - factor * row
            return carry

        lax.fori_loop(0, size, eliminate, 0)
        inverse[...] = inverse[...] * scale_row

    high_part, low_part = split(inverse[...] * scale)
    high[...] = high_part
    low[...] = low_part
    row_high, row_low = split(rows[...])
    basis[...] = (
        dot(row_high, high_part, NT) + (dot(row_high, low_part, NT) + dot(row_low, high_part, NT))
    ).astype(BF)


def project_kernel(scale, count, high, low, *refs):
    out = refs[-1]
    me = lax.axis_index("row")
    share = refs[0].shape[0]
    for index, step in enumerate([0] + list(reversed(range(1, count)))):
        chunk = refs[index][...]
        product = dot(chunk, high[...], NT) + dot(chunk, low[...], NT)
        out[rows_at(me ^ step, share), :] = (product * scale).astype(BF)


def shards(tiles, tile_rows, tile_cols, counts, omega):
    slots, size_b, _ = tiles.shape
    rank = omega.shape[1]
    cols_here = omega.shape[0]
    col_blocks = cols_here // size_b
    row_groups = lax.axis_size("row")
    col_groups = lax.axis_size("col")
    zs = col_groups // CORES
    rows_here = RB_DEV * size_b
    share = rows_here // col_groups
    back_share = cols_here // row_groups
    total_rows = rows_here * row_groups

    def swap_core(x):
        return lax.ppermute(x, "col", [(i, i ^ 1) for i in range(col_groups)])

    def swap_z(x, step):
        return lax.ppermute(x, "col", [(i, i ^ (CORES * step)) for i in range(col_groups)])

    def swap_row(x, step):
        return lax.ppermute(x, "row", [(i, i ^ step) for i in range(row_groups)])

    def array(shape, kind):
        return jax.ShapeDtypeStruct(shape, kind)

    def vs(*xs):
        return [("v", x) for x in xs]

    part_shape = (share, rank)
    places = tile_rows * CODE + tile_cols
    padded = (slots // LANES + 1) * LANES
    codes = jnp.where(jnp.arange(padded) < slots, jnp.pad(places, (0, padded - slots)), counts[0])
    inputs = [("a", codes), ("h", tiles)]
    slot_scratch = [pltpu.SMEM((padded,), jnp.int32), pltpu.VMEM(tiles.shape, BF)]
    sent, kept = call(
        "sketch",
        functools.partial(sketch_kernel, share),
        inputs + [("h", omega)],
        [array((zs * share, rank), BF), array((zs * share, rank), F32)],
        slot_scratch
        + [
            pltpu.VMEM(omega.shape, BF),
            pltpu.VMEM((col_blocks, rows_here, size_b), BF),
            pltpu.SemaphoreType.DMA((LOADS + 2,)),
        ],
        limit=SKETCH_LIMIT,
        flops=2 * rows_here * cols_here * rank,
        nbytes=6 * MIB,
    )
    own, token, *sends = call(
        "pair",
        functools.partial(pair_kernel, share),
        vs(kept, swap_core(sent)),
        [array(part_shape, F32), array(TOKEN, F32)] + [array(part_shape, BF)] * (zs - 1),
        nbytes=MIB,
    )
    gets = [swap_z(x, k + 1) for k, x in enumerate(sends)]
    turned, token = call(
        "turn",
        turn_kernel,
        inputs + [("a", token)],
        [array((RB_DEV, cols_here, size_b), BF), array(TOKEN, F32)],
        slot_scratch + [pltpu.SemaphoreType.DMA((LOADS + 1,))],
        limit=TURN_LIMIT,
        nbytes=8 * MIB,
    )
    own_rows, rows_bf = call(
        "rows",
        functools.partial(rows_kernel, len(gets)),
        vs(own, *gets) + [("a", token)],
        [array(part_shape, F32), array(part_shape, BF)],
        nbytes=MIB,
    )
    chunks = {k: swap_z(rows_bf, k) for k in range(1, zs)}
    order = list(reversed(far_first(zs)))
    (mine,) = call(
        "pack",
        functools.partial(pack_kernel, order),
        vs(rows_bf, *[chunks[k] for k in order]),
        [array((zs * share, rank), BF)],
        nbytes=MIB,
    )
    (full,) = call(
        "full",
        functools.partial(full_kernel, share),
        vs(mine, swap_core(mine)),
        [array((rows_here, rank), BF)],
        nbytes=MIB,
    )
    half = rank // CORES
    gram_shape = (half + half // CORES, half)
    own, gram, *sends = call(
        "back",
        back_kernel,
        vs(turned, full),
        [array((back_share, rank), F32), array(gram_shape, F32)] + [array((back_share, rank), BF)] * (row_groups - 1),
        flops=2 * rows_here * cols_here * rank,
        nbytes=6 * MIB,
    )
    gets = [swap_row(x, k + 1) for k, x in enumerate(sends)]
    (back_sum,) = call(
        "columns",
        functools.partial(columns_kernel, len(gets)),
        vs(own, *gets),
        [array((back_share, rank), BF)],
        nbytes=1,
    )
    backs = [back_sum] + [swap_row(back_sum, k) for k in reversed(range(1, row_groups))]
    terms = [gram] + [swap_row(gram, k) for k in reversed(range(1, row_groups))]
    (gram_sum,) = call("tree", tree_kernel, vs(*terms), [array(gram_shape, F32)], nbytes=1)
    high, low, basis = call(
        "factor",
        functools.partial(factor_kernel, float(total_rows) ** 0.5),
        vs(gram_sum, swap_core(gram_sum), own_rows),
        [array((rank, rank), BF), array((rank, rank), BF), array((share, rank), BF)],
        [pltpu.VMEM((rank, rank), F32), pltpu.VMEM((rank, rank), F32)],
        flops=1,
        nbytes=1,
    )
    (projected,) = call(
        "project",
        functools.partial(project_kernel, float(RB_DEV * row_groups) ** -0.5, row_groups),
        vs(high, low, *backs),
        [array((cols_here, rank), BF)],
        flops=4 * cols_here * rank * rank,
        nbytes=2 * MIB,
    )
    return basis, projected


def solution(mesh):
    return jax.shard_map(
        shards,
        mesh=mesh,
        in_specs=(
            P(("row", "col"), None, None),
            P(("row", "col")),
            P(("row", "col")),
            P(("row", "col")),
            P("col", None),
        ),
        out_specs=(P(("row", "col"), None), P("col", None)),
        check_vma=False,
    )
```

time: 111 us -> 101 us (0.910)
  waiting for transfers between devices: 27.9 us -> 20.6 us
  local copies, waits for them, and re-layouts: 4.26 us -> 1.05 us
  Pallas kernels: 54.8 us -> 52.2 us
  starting transfers between devices: 22.2 us -> 24 us
    ppermute x6, waiting for transfers between devices: 19.5 us -> 14.2 us  [swap_z(): lax.ppermute(x, 'col', [(i, i ^ CORES * step) for i in range(col_groups)])]
    ppermute x9, waiting for transfers between devices: 5.61 us -> 1.61 us  [swap_row(): return lax.ppermute(x, 'row', [(i, i ^ step) for i in range(row_groups)])]
    unnamed x14 -> x4, local copies, waits for them, and re-layouts: 4.26 us -> 1.05 us
    pallas_call x9 -> x11, Pallas kernels: 54.8 us -> 52.2 us  [call(): pl.pallas_call(body, out_shape=outs, in_specs=[pl.BlockSpec(memory_space=...]
    ppermute x6 -> x3, waiting for transfers between devices: 2.78 us -> 4.72 us  [swap_core(): return lax.ppermute(x, 'col', [(i, i ^ 1) for i in range(col_groups)])]
    ppermute x9, starting transfers between devices: 11.2 us -> 13 us  [swap_row(): return lax.ppermute(x, 'row', [(i, i ^ step) for i in range(row_groups)])]
  transfers between devices with their start and end apart: 21 -> 18, of which waited for: 9 -> 9; matrix products, arithmetic and copies ran while one was open for 0% -> 0% of each run, Pallas kernels for 44% -> 45%
where the time goes in v2:
time: 101 us; the launch traced here: 100 us
  Pallas kernels  52.2 us (52%)
  starting transfers between devices  24 us (24%)
  waiting for transfers between devices  20.6 us (20%)
  between operations  1.53 us (2%)
  local copies, waits for them, and re-layouts  1.05 us (1%)
    pallas_call x11, Pallas kernels, call(): pl.pallas_call(body, out_shape=outs, in_specs=[pl.BlockSpec(memory_space=...  52.2 us
    ppermute x6, waiting for transfers between devices, swap_z(): lax.ppermute(x, 'col', [(i, i ^ CORES * step) for i in range(col_groups)])  14.2 us
    ppermute x9, starting transfers between devices, swap_row(): return lax.ppermute(x, 'row', [(i, i ^ step) for i in range(row_groups)])  13 us
    ppermute x6, starting transfers between devices, swap_z(): lax.ppermute(x, 'col', [(i, i ^ CORES * step) for i in range(col_groups)])  9.94 us
    ppermute x3, waiting for transfers between devices, swap_core(): return lax.ppermute(x, 'col', [(i, i ^ 1) for i in range(col_groups)])  4.72 us
  transfers between devices with their start and end apart: 18, of which 9 were waited for; matrix products, arithmetic and copies ran while one was open for 0% of the time, Pallas kernels for 45%

profile of v2, /device:TPU:0, one launch (start us, length us, event | category | flops | bytes accessed | tf_op | source)
XLA Modules:
  0.0 100.1 jit_solution(4935936755615509328)
XLA Ops:
  1.4 0.8 multiply_add_fusion
  2.3 1.0 %copy-done.1 = bf16[1024,256]{1,0:T(8,128)(2,1)S(1)} copy-done((bf16[1024,256]{1,0:T(8,128)(2,1)S(1)}, bf16[1024,256]{1,0:T(8,128)(2,1)}, u32[]{:S(2)}) %copy-start.1) | copy-done | bytes 524312
  3.3 3.4 %sketch.1 = (bf16[1024,256]{1,0:T(8,128)(2,1)S(1)}, f32[1024,256]{1,0:T(8,128)S(1)}) custom-call(s32[128]{0:T(128)S(1)} %compare_select_fusion.codes, bf16[96,128,128]{2,1,0:T(8,128)(2,1)} %tiles_hbm.3, bf16[1024,256]{1,0:T(8,128)(2,1)S(1)} %copy-done.1), custom_call_target="tpu_custom_call" | custom-call | flops 1073741824 | bytes 6291456 | tf_op jit(solution)/shard_map/sketch/pallas_call | solution.py:30
  6.7 0.9 collective-permute-start
  7.7 1.5 %collective-permute-done.came = bf16[1024,256]{1,0:T(8,128)(2,1)S(1)} collective-permute-done((bf16[1024,256]{1,0:T(8,128)(2,1)S(1)}, bf16[1024,256]{1,0:T(8,128)(2,1)S(1)}, u32[]{:S(2)}, u32[]{:S(2)}) %collective-permute-start) | collective-permute-done | bytes 524320 | tf_op jit(solution)/shard_map/ppermute | solution.py:298
  9.2 0.1 pair.1
  9.3 2.7 %collective-permute-start.1 = (bf16[256,256]{1,0:T(8,128)(2,1)S(1)}, bf16[256,256]{1,0:T(8,128)(2,1)S(1)}, u32[]{:S(2)}, u32[]{:S(2)}) collective-permute-start(bf16[256,256]{1,0:T(8,128)(2,1)S(1)} %get-tuple-element.26), channel_id=1, source_target_pairs={{0,2},{1,3},{2,0},{3,1},{4,6},{5,7},{6,4},{7,5},{8,10},{9,11},{10,... | collective-permute-start | bytes 393224 | tf_op jit(solution)/shard_map/ppermute | solution.py:301
  12.0 2.8 %collective-permute-start.2 = (bf16[256,256]{1,0:T(8,128)(2,1)S(1)}, bf16[256,256]{1,0:T(8,128)(2,1)S(1)}, u32[]{:S(2)}, u32[]{:S(2)}) collective-permute-start(bf16[256,256]{1,0:T(8,128)(2,1)S(1)} %get-tuple-element.27), channel_id=1, source_target_pairs={{0,4},{1,5},{2,6},{3,7},{4,0},{5,1},{6,2},{7,3},{8,12},{9,13},{10,... | collective-permute-start | bytes 393224 | tf_op jit(solution)/shard_map/ppermute | solution.py:301
  14.8 5.5 %turn.1 = (bf16[16,1024,128]{2,1,0:T(8,128)(2,1)S(1)}, f32[8,128]{1,0:T(8,128)S(1)}) custom-call(s32[128]{0:T(128)S(1)} %compare_select_fusion.codes, bf16[96,128,128]{2,1,0:T(8,128)(2,1)S(1)} %copy-done, f32[8,128]{1,0:T(8,128)S(1)} %get-tuple-element.23._), custom_call_target="tpu_custom_call" | custom-call | bytes 8388608 | tf_op jit(solution)/shard_map/turn/pallas_call | solution.py:30
  20.3 4.6 %collective-permute-done.2.refs_1_ = bf16[256,256]{1,0:T(8,128)(2,1)S(1)} collective-permute-done((bf16[256,256]{1,0:T(8,128)(2,1)S(1)}, bf16[256,256]{1,0:T(8,128)(2,1)S(1)}, u32[]{:S(2)}, u32[]{:S(2)}) %collective-permute-start.2) | collective-permute-done | bytes 131104 | tf_op jit(solution)/shard_map/ppermute | solution.py:301
  25.0 2.8 %collective-permute-start.6 = (bf16[256,256]{1,0:T(8,128)(2,1)S(1)}, bf16[256,256]{1,0:T(8,128)(2,1)S(1)}, u32[]{:S(2)}, u32[]{:S(2)}) collective-permute-start(bf16[256,256]{1,0:T(8,128)(2,1)S(1)} %get-tuple-element.30.own), channel_id=1, source_target_pairs={{0,6},{1,7},{2,4},{3,5},{4,2},{5,3},{6,0},{7,1},{8,14},{9,15},{10,... | collective-permute-start | bytes 393224 | tf_op jit(solution)/shard_map/ppermute | solution.py:301
  27.8 1.4 %collective-permute-start.5 = (bf16[256,256]{1,0:T(8,128)(2,1)S(1)}, bf16[256,256]{1,0:T(8,128)(2,1)S(1)}, u32[]{:S(2)}, u32[]{:S(2)}) collective-permute-start(bf16[256,256]{1,0:T(8,128)(2,1)S(1)} %get-tuple-element.30.own), channel_id=1, source_target_pairs={{0,2},{1,3},{2,0},{3,1},{4,6},{5,7},{6,4},{7,5},{8,10},{9,11},{10,... | collective-permute-start | bytes 393224 | tf_op jit(solution)/shard_map/ppermute | solution.py:301
  29.2 0.2 collective-permute-start.4
  29.4 3.7 %collective-permute-done.6.refs_2_ = bf16[256,256]{1,0:T(8,128)(2,1)S(1)} collective-permute-done((bf16[256,256]{1,0:T(8,128)(2,1)S(1)}, bf16[256,256]{1,0:T(8,128)(2,1)S(1)}, u32[]{:S(2)}, u32[]{:S(2)}) %collective-permute-start.6) | collective-permute-done | bytes 131104 | tf_op jit(solution)/shard_map/ppermute | solution.py:301
  33.1 0.9 collective-permute-done.5.refs_1_
  34.1 5.0 %collective-permute-done.4.refs_0_ = bf16[256,256]{1,0:T(8,128)(2,1)S(1)} collective-permute-done((bf16[256,256]{1,0:T(8,128)(2,1)S(1)}, bf16[256,256]{1,0:T(8,128)(2,1)S(1)}, u32[]{:S(2)}, u32[]{:S(2)}) %collective-permute-start.4) | collective-permute-done | bytes 131104 | tf_op jit(solution)/shard_map/ppermute | solution.py:301
  39.2 1.9 %collective-permute-done.7.other = bf16[1024,256]{1,0:T(8,128)(2,1)S(1)} collective-permute-done((bf16[1024,256]{1,0:T(8,128)(2,1)S(1)}, bf16[1024,256]{1,0:T(8,128)(2,1)S(1)}, u32[]{:S(2)}, u32[]{:S(2)}) %collective-permute-start.7) | collective-permute-done | bytes 524320 | tf_op jit(solution)/shard_map/ppermute | solution.py:298
  41.2 1.7 %back.1 = (f32[256,256]{1,0:T(8,128)S(1)}, f32[192,128]{1,0:T(8,128)S(1)}, bf16[256,256]{1,0:T(8,128)(2,1)S(1)}, bf16[256,256]{1,0:T(8,128)(2,1)S(1)}, bf16[256,256]{1,0:T(8,128)(2,1)S(1)}) custom-call(bf16[16,1024,128]{2,1,0:T(8,128)(2,1)S(1)} %get-tuple-element.24.turned, bf16[2048,256]{1,0:T(8,128)(2,1)S(1)} %full.1), custom_call_target="tpu_custom_call" | custom-call | flops 1073741824 | bytes 6291456 | tf_op jit(solution)/shard_map/back/pallas_call | solution.py:30
  42.9 1.6 %collective-permute-start.12 = (bf16[256,256]{1,0:T(8,128)(2,1)S(1)}, bf16[256,256]{1,0:T(8,128)(2,1)S(1)}, u32[]{:S(2)}, u32[]{:S(2)}) collective-permute-start(bf16[256,256]{1,0:T(8,128)(2,1)S(1)} %get-tuple-element.37), channel_id=1, source_target_pairs={{0,8},{8,0},{16,24},{24,16},{1,9},{9,1},{17,25},{25,17},{2,10},{10... | collective-permute-start | bytes 393224 | tf_op jit(solution)/shard_map/ppermute | solution.py:304
  44.5 1.5 %collective-permute-start.13 = (bf16[256,256]{1,0:T(8,128)(2,1)S(1)}, bf16[256,256]{1,0:T(8,128)(2,1)S(1)}, u32[]{:S(2)}, u32[]{:S(2)}) collective-permute-start(bf16[256,256]{1,0:T(8,128)(2,1)S(1)} %get-tuple-element.38), channel_id=1, source_target_pairs={{0,16},{8,24},{16,0},{24,8},{1,17},{9,25},{17,1},{25,9},{2,18},{10... | collective-permute-start | bytes 393224 | tf_op jit(solution)/shard_map/ppermute | solution.py:304
  45.9 0.5 collective-permute-start.14
  46.5 1.5 %collective-permute-start.10 = (f32[192,128]{1,0:T(8,128)S(1)}, f32[192,128]{1,0:T(8,128)S(1)}, u32[]{:S(2)}, u32[]{:S(2)}) collective-permute-start(f32[192,128]{1,0:T(8,128)S(1)} %get-tuple-element.31.own), channel_id=1, source_target_pairs={{0,8},{8,0},{16,24},{24,16},{1,9},{9,1},{17,25},{25,17},{2,10},{10... | collective-permute-start | bytes 294920 | tf_op jit(solution)/shard_map/ppermute | solution.py:304
  47.9 1.5 %collective-permute-start.9 = (f32[192,128]{1,0:T(8,128)S(1)}, f32[192,128]{1,0:T(8,128)S(1)}, u32[]{:S(2)}, u32[]{:S(2)}) collective-permute-start(f32[192,128]{1,0:T(8,128)S(1)} %get-tuple-element.31.own), channel_id=1, source_target_pairs={{0,16},{8,24},{16,0},{24,8},{1,17},{9,25},{17,1},{25,9},{2,18},{10... | collective-permute-start | bytes 294920 | tf_op jit(solution)/shard_map/ppermute | solution.py:304
  49.4 2.3 %collective-permute-start.8 = (f32[192,128]{1,0:T(8,128)S(1)}, f32[192,128]{1,0:T(8,128)S(1)}, u32[]{:S(2)}, u32[]{:S(2)}) collective-permute-start(f32[192,128]{1,0:T(8,128)S(1)} %get-tuple-element.31.own), channel_id=1, source_target_pairs={{0,24},{8,16},{16,8},{24,0},{1,25},{9,17},{17,9},{25,1},{2,26},{10... | collective-permute-start | bytes 294920 | tf_op jit(solution)/shard_map/ppermute | solution.py:304
  51.7 1.2 %collective-permute-done.13.refs_1_ = bf16[256,256]{1,0:T(8,128)(2,1)S(1)} collective-permute-done((bf16[256,256]{1,0:T(8,128)(2,1)S(1)}, bf16[256,256]{1,0:T(8,128)(2,1)S(1)}, u32[]{:S(2)}, u32[]{:S(2)}) %collective-permute-start.13) | collective-permute-done | bytes 131104 | tf_op jit(solution)/shard_map/ppermute | solution.py:304
  52.9 0.3 collective-permute-done.14.refs_2_
  53.3 1.3 %collective-permute-start.17 = (bf16[256,256]{1,0:T(8,128)(2,1)S(1)}, bf16[256,256]{1,0:T(8,128)(2,1)S(1)}, u32[]{:S(2)}, u32[]{:S(2)}) collective-permute-start(bf16[256,256]{1,0:T(8,128)(2,1)S(1)} %columns.1.refs_0_), channel_id=1, source_target_pairs={{0,8},{8,0},{16,24},{24,16},{1,9},{9,1},{17,25},{25,17},{2,10},{10... | collective-permute-start | bytes 393224 | tf_op jit(solution)/shard_map/ppermute | solution.py:304
  54.7 1.5 %collective-permute-start.16 = (bf16[256,256]{1,0:T(8,128)(2,1)S(1)}, bf16[256,256]{1,0:T(8,128)(2,1)S(1)}, u32[]{:S(2)}, u32[]{:S(2)}) collective-permute-start(bf16[256,256]{1,0:T(8,128)(2,1)S(1)} %columns.1.refs_0_), channel_id=1, source_target_pairs={{0,16},{8,24},{16,0},{24,8},{1,17},{9,25},{17,1},{25,9},{2,18},{10... | collective-permute-start | bytes 393224 | tf_op jit(solution)/shard_map/ppermute | solution.py:304
  56.1 1.4 %collective-permute-start.15 = (bf16[256,256]{1,0:T(8,128)(2,1)S(1)}, bf16[256,256]{1,0:T(8,128)(2,1)S(1)}, u32[]{:S(2)}, u32[]{:S(2)}) collective-permute-start(bf16[256,256]{1,0:T(8,128)(2,1)S(1)} %columns.1.refs_0_), channel_id=1, source_target_pairs={{0,24},{8,16},{16,8},{24,0},{1,25},{9,17},{17,9},{25,1},{2,26},{10... | collective-permute-start | bytes 393224 | tf_op jit(solution)/shard_map/ppermute | solution.py:304
  57.6 1.3 %collective-permute-done.11.refs_1_ = f32[192,128]{1,0:T(8,128)S(1)} collective-permute-done((f32[192,128]{1,0:T(8,128)S(1)}, f32[192,128]{1,0:T(8,128)S(1)}, u32[]{:S(2)}, u32[]{:S(2)}) %collective-permute-start.11) | collective-permute-done | bytes 98336 | tf_op jit(solution)/shard_map/ppermute | solution.py:298
  58.9 39.9 %factor.1 = (bf16[256,256]{1,0:T(8,128)(2,1)S(1)}, bf16[256,256]{1,0:T(8,128)(2,1)S(1)}, bf16[256,256]{1,0:T(8,128)(2,1)}) custom-call(f32[192,128]{1,0:T(8,128)S(1)} %tree.1.refs_0_, f32[192,128]{1,0:T(8,128)S(1)} %collective-permute-done.11.refs_1_, f32[256,256]{1,0:T(8,128)S(1)} %get-tuple-element.32.refs_2_), custom_call_target="tpu_custom_call" | custom-call | flops 1 | bytes 1 | tf_op jit(solution)/shard_map/factor/pallas_call | solution.py:30
  98.8 1.3 %project.1 = bf16[1024,256]{1,0:T(8,128)(2,1)} custom-call(bf16[256,256]{1,0:T(8,128)(2,1)S(1)} %get-tuple-element.34.high, bf16[256,256]{1,0:T(8,128)(2,1)S(1)} %get-tuple-element.35.low, bf16[256,256]{1,0:T(8,128)(2,1)S(1)} %columns.1.refs_0_, bf16[256,256]{1,0:T(8,128)(2,1)S(1)} %collective-permute-done.15.refs_1_, ...), custom_call_target="tpu_custom_call" | custom-call | flops 268435456 | bytes 2097152 | tf_op jit(solution)/shard_map/project/pallas_call | solution.py:30
  (21 shorter events, 0.5 us)
Async XLA Ops:
  0.6 14.2 %copy-start = (bf16[96,128,128]{2,1,0:T(8,128)(2,1)S(1)}, bf16[96,128,128]{2,1,0:T(8,128)(2,1)}, u32[]{:S(2)}) copy-start(bf16[96,128,128]{2,1,0:T(8,128)(2,1)} %tiles_hbm.3) | copy-start | bytes 9437188
  2.3 1.0 %copy-start.1 = (bf16[1024,256]{1,0:T(8,128)(2,1)S(1)}, bf16[1024,256]{1,0:T(8,128)(2,1)}, u32[]{:S(2)}) copy-start(bf16[1024,256]{1,0:T(8,128)(2,1)} %omega_hbm.1) | copy-start | bytes 1572868
  6.7 2.5 %collective-permute-start = (bf16[1024,256]{1,0:T(8,128)(2,1)S(1)}, bf16[1024,256]{1,0:T(8,128)(2,1)S(1)}, u32[]{:S(2)}, u32[]{:S(2)}) collective-permute-start(bf16[1024,256]{1,0:T(8,128)(2,1)S(1)} %get-tuple-element.22), channel_id=1, source_target_pairs={{0,1},{1,0},{2,3},{3,2},{4,5},{5,4},{6,7},{7,6},{8,9},{9,8},{10,11... | collective-permute-start | bytes 1572872 | tf_op jit(solution)/shard_map/ppermute | solution.py:298
  9.3 11.0 %collective-permute-start.1 = (bf16[256,256]{1,0:T(8,128)(2,1)S(1)}, bf16[256,256]{1,0:T(8,128)(2,1)S(1)}, u32[]{:S(2)}, u32[]{:S(2)}) collective-permute-start(bf16[256,256]{1,0:T(8,128)(2,1)S(1)} %get-tuple-element.26), channel_id=1, source_target_pairs={{0,2},{1,3},{2,0},{3,1},{4,6},{5,7},{6,4},{7,5},{8,10},{9,11},{10,... | collective-permute-start | bytes 393224 | tf_op jit(solution)/shard_map/ppermute | solution.py:301
  12.0 12.9 %collective-permute-start.2 = (bf16[256,256]{1,0:T(8,128)(2,1)S(1)}, bf16[256,256]{1,0:T(8,128)(2,1)S(1)}, u32[]{:S(2)}, u32[]{:S(2)}) collective-permute-start(bf16[256,256]{1,0:T(8,128)(2,1)S(1)} %get-tuple-element.27), channel_id=1, source_target_pairs={{0,4},{1,5},{2,6},{3,7},{4,0},{5,1},{6,2},{7,3},{8,12},{9,13},{10,... | collective-permute-start | bytes 393224 | tf_op jit(solution)/shard_map/ppermute | solution.py:301
  14.8 10.1 %collective-permute-start.3 = (bf16[256,256]{1,0:T(8,128)(2,1)S(1)}, bf16[256,256]{1,0:T(8,128)(2,1)S(1)}, u32[]{:S(2)}, u32[]{:S(2)}) collective-permute-start(bf16[256,256]{1,0:T(8,128)(2,1)S(1)} %get-tuple-element.28), channel_id=1, source_target_pairs={{0,6},{1,7},{2,4},{3,5},{4,2},{5,3},{6,0},{7,1},{8,14},{9,15},{10,... | collective-permute-start | bytes 393224 | tf_op jit(solution)/shard_map/ppermute | solution.py:301
  25.0 8.2 %collective-permute-start.6 = (bf16[256,256]{1,0:T(8,128)(2,1)S(1)}, bf16[256,256]{1,0:T(8,128)(2,1)S(1)}, u32[]{:S(2)}, u32[]{:S(2)}) collective-permute-start(bf16[256,256]{1,0:T(8,128)(2,1)S(1)} %get-tuple-element.30.own), channel_id=1, source_target_pairs={{0,6},{1,7},{2,4},{3,5},{4,2},{5,3},{6,0},{7,1},{8,14},{9,15},{10,... | collective-permute-start | bytes 393224 | tf_op jit(solution)/shard_map/ppermute | solution.py:301
  27.8 6.3 %collective-permute-start.5 = (bf16[256,256]{1,0:T(8,128)(2,1)S(1)}, bf16[256,256]{1,0:T(8,128)(2,1)S(1)}, u32[]{:S(2)}, u32[]{:S(2)}) collective-permute-start(bf16[256,256]{1,0:T(8,128)(2,1)S(1)} %get-tuple-element.30.own), channel_id=1, source_target_pairs={{0,2},{1,3},{2,0},{3,1},{4,6},{5,7},{6,4},{7,5},{8,10},{9,11},{10,... | collective-permute-start | bytes 393224 | tf_op jit(solution)/shard_map/ppermute | solution.py:301
  29.2 9.9 %collective-permute-start.4 = (bf16[256,256]{1,0:T(8,128)(2,1)S(1)}, bf16[256,256]{1,0:T(8,128)(2,1)S(1)}, u32[]{:S(2)}, u32[]{:S(2)}) collective-permute-start(bf16[256,256]{1,0:T(8,128)(2,1)S(1)} %get-tuple-element.30.own), channel_id=1, source_target_pairs={{0,4},{1,5},{2,6},{3,7},{4,0},{5,1},{6,2},{7,3},{8,12},{9,13},{10,... | collective-permute-start | bytes 393224 | tf_op jit(solution)/shard_map/ppermute | solution.py:301
  39.1 2.0 %collective-permute-start.7 = (bf16[1024,256]{1,0:T(8,128)(2,1)S(1)}, bf16[1024,256]{1,0:T(8,128)(2,1)S(1)}, u32[]{:S(2)}, u32[]{:S(2)}) collective-permute-start(bf16[1024,256]{1,0:T(8,128)(2,1)S(1)} %pack.1.mine), channel_id=1, source_target_pairs={{0,1},{1,0},{2,3},{3,2},{4,5},{5,4},{6,7},{7,6},{8,9},{9,8},{10,11... | collective-permute-start | bytes 1572872 | tf_op jit(solution)/shard_map/ppermute | solution.py:298
  42.9 6.5 %collective-permute-start.12 = (bf16[256,256]{1,0:T(8,128)(2,1)S(1)}, bf16[256,256]{1,0:T(8,128)(2,1)S(1)}, u32[]{:S(2)}, u32[]{:S(2)}) collective-permute-start(bf16[256,256]{1,0:T(8,128)(2,1)S(1)} %get-tuple-element.37), channel_id=1, source_target_pairs={{0,8},{8,0},{16,24},{24,16},{1,9},{9,1},{17,25},{25,17},{2,10},{10... | collective-permute-start | bytes 393224 | tf_op jit(solution)/shard_map/ppermute | solution.py:304
  44.5 8.5 %collective-permute-start.13 = (bf16[256,256]{1,0:T(8,128)(2,1)S(1)}, bf16[256,256]{1,0:T(8,128)(2,1)S(1)}, u32[]{:S(2)}, u32[]{:S(2)}) collective-permute-start(bf16[256,256]{1,0:T(8,128)(2,1)S(1)} %get-tuple-element.38), channel_id=1, source_target_pairs={{0,16},{8,24},{16,0},{24,8},{1,17},{9,25},{17,1},{25,9},{2,18},{10... | collective-permute-start | bytes 393224 | tf_op jit(solution)/shard_map/ppermute | solution.py:304
  45.9 7.3 %collective-permute-start.14 = (bf16[256,256]{1,0:T(8,128)(2,1)S(1)}, bf16[256,256]{1,0:T(8,128)(2,1)S(1)}, u32[]{:S(2)}, u32[]{:S(2)}) collective-permute-start(bf16[256,256]{1,0:T(8,128)(2,1)S(1)} %get-tuple-element.39), channel_id=1, source_target_pairs={{0,24},{8,16},{16,8},{24,0},{1,25},{9,17},{17,9},{25,1},{2,26},{10... | collective-permute-start | bytes 393224 | tf_op jit(solution)/shard_map/ppermute | solution.py:304
  46.5 9.7 %collective-permute-start.10 = (f32[192,128]{1,0:T(8,128)S(1)}, f32[192,128]{1,0:T(8,128)S(1)}, u32[]{:S(2)}, u32[]{:S(2)}) collective-permute-start(f32[192,128]{1,0:T(8,128)S(1)} %get-tuple-element.31.own), channel_id=1, source_target_pairs={{0,8},{8,0},{16,24},{24,16},{1,9},{9,1},{17,25},{25,17},{2,10},{10... | collective-permute-start | bytes 294920 | tf_op jit(solution)/shard_map/ppermute | solution.py:304
  47.9 9.6 %collective-permute-start.9 = (f32[192,128]{1,0:T(8,128)S(1)}, f32[192,128]{1,0:T(8,128)S(1)}, u32[]{:S(2)}, u32[]{:S(2)}) collective-permute-start(f32[192,128]{1,0:T(8,128)S(1)} %get-tuple-element.31.own), channel_id=1, source_target_pairs={{0,16},{8,24},{16,0},{24,8},{1,17},{9,25},{17,1},{25,9},{2,18},{10... | collective-permute-start | bytes 294920 | tf_op jit(solution)/shard_map/ppermute | solution.py:304
  49.4 8.1 %collective-permute-start.8 = (f32[192,128]{1,0:T(8,128)S(1)}, f32[192,128]{1,0:T(8,128)S(1)}, u32[]{:S(2)}, u32[]{:S(2)}) collective-permute-start(f32[192,128]{1,0:T(8,128)S(1)} %get-tuple-element.31.own), channel_id=1, source_target_pairs={{0,24},{8,16},{16,8},{24,0},{1,25},{9,17},{17,9},{25,1},{2,26},{10... | collective-permute-start | bytes 294920 | tf_op jit(solution)/shard_map/ppermute | solution.py:304
  53.3 45.5 %collective-permute-start.17 = (bf16[256,256]{1,0:T(8,128)(2,1)S(1)}, bf16[256,256]{1,0:T(8,128)(2,1)S(1)}, u32[]{:S(2)}, u32[]{:S(2)}) collective-permute-start(bf16[256,256]{1,0:T(8,128)(2,1)S(1)} %columns.1.refs_0_), channel_id=1, source_target_pairs={{0,8},{8,0},{16,24},{24,16},{1,9},{9,1},{17,25},{25,17},{2,10},{10... | collective-permute-start | bytes 393224 | tf_op jit(solution)/shard_map/ppermute | solution.py:304
  54.7 44.1 %collective-permute-start.16 = (bf16[256,256]{1,0:T(8,128)(2,1)S(1)}, bf16[256,256]{1,0:T(8,128)(2,1)S(1)}, u32[]{:S(2)}, u32[]{:S(2)}) collective-permute-start(bf16[256,256]{1,0:T(8,128)(2,1)S(1)} %columns.1.refs_0_), channel_id=1, source_target_pairs={{0,16},{8,24},{16,0},{24,8},{1,17},{9,25},{17,1},{25,9},{2,18},{10... | collective-permute-start | bytes 393224 | tf_op jit(solution)/shard_map/ppermute | solution.py:304
  56.1 42.7 %collective-permute-start.15 = (bf16[256,256]{1,0:T(8,128)(2,1)S(1)}, bf16[256,256]{1,0:T(8,128)(2,1)S(1)}, u32[]{:S(2)}, u32[]{:S(2)}) collective-permute-start(bf16[256,256]{1,0:T(8,128)(2,1)S(1)} %columns.1.refs_0_), channel_id=1, source_target_pairs={{0,24},{8,16},{16,8},{24,0},{1,25},{9,17},{17,9},{25,1},{2,26},{10... | collective-permute-start | bytes 393224 | tf_op jit(solution)/shard_map/ppermute | solution.py:304
  57.5 1.4 %collective-permute-start.11 = (f32[192,128]{1,0:T(8,128)S(1)}, f32[192,128]{1,0:T(8,128)S(1)}, u32[]{:S(2)}, u32[]{:S(2)}) collective-permute-start(f32[192,128]{1,0:T(8,128)S(1)} %tree.1.refs_0_), channel_id=1, source_target_pairs={{0,1},{1,0},{2,3},{3,2},{4,5},{5,4},{6,7},{7,6},{8,9},{9,8},{10,11... | collective-permute-start | bytes 294920 | tf_op jit(solution)/shard_map/ppermute | solution.py:298

commit v3 on v2

--- a/solution.py
+++ b/solution.py
@@ -9,12 +9,10 @@
 
 RB_DEV = 16
 CORES = 2
+SIDES = 2
+FACTOR_FLOPS = 40
 LOADS = 4
 TOKEN = (8, 128)
-CODE = 256
-LANES = 128
-SKETCH_LIMIT = 50
-TURN_LIMIT = 44
 MIB = 1024 * 1024
 BF = jnp.bfloat16
 F32 = jnp.float32
@@ -36,7 +34,7 @@
         compiler_params=pltpu.CompilerParams(vmem_limit_bytes=limit * MIB),
         cost_estimate=pl.CostEstimate(flops=flops, bytes_accessed=nbytes, transcendentals=0),
         name=name,
-    )(*[array for _, array in ins])
+    )(*[pltpu.with_memory_space_constraint(array, pltpu.HBM) if space == "h" else array for space, array in ins])
 
 
 def dot(a, b, dims=NN):
@@ -71,33 +69,42 @@
     return pl.ds(pl.multiple_of(index * count, count), count)
 
 
-def put_live(codes, codes_smem, tiles_hbm, tiles, sems, clear, put):
+def put_live(live, places_hbm, places, tiles_hbm, tiles, sems, clear, put):
     load = tiles.shape[0] // LOADS
-    first = pltpu.make_async_copy(codes, codes_smem, sems.at[LOADS])
-    first.start()
+    rows, cols = places
+    firsts = [
+        pltpu.make_async_copy(source, target, sems.at[LOADS + k])
+        for k, (source, target) in enumerate(zip(places_hbm, places))
+    ]
     copies = []
     for k in range(LOADS):
         piece = pl.ds(k * load, load)
         copies.append(pltpu.make_async_copy(tiles_hbm.at[piece], tiles.at[piece], sems.at[k]))
-    for copy in copies:
+    for copy in firsts + copies:
         copy.start()
     clear()
-    first.wait()
+    for copy in firsts:
+        copy.wait()
 
     def step(slot, carry):
-        code = codes_smem[slot]
-        put(slot, code // CODE, code % CODE)
+        put(slot, rows[slot], cols[slot])
         return carry
 
-    live = codes_smem[tiles.shape[0]]
     for k, copy in enumerate(copies):
         copy.wait()
         lax.fori_loop(k * load, jnp.clip(live, k * load, (k + 1) * load), step, 0)
 
 
-def sketch_kernel(share, codes, tiles_hbm, omega_hbm, sent, kept, codes_smem, tiles, omega, dense, sems):
+def multiply(share, owner, dense, omega, out):
+    for step in range(out.shape[0] // share):
+        here = rows_at(step * CORES + owner, share)
+        left = jnp.concatenate([dense[c, here, :] for c in range(dense.shape[0])], axis=1)
+        out[step * share : (step + 1) * share, :] = dot(left, omega[...]).astype(out.dtype)
+
+
+def sketch_kernel(share, counts, rows_hbm, cols_hbm, tiles_hbm, omega_hbm, sent, dense, omega, rows, cols, tiles, sems):
     size_b = tiles.shape[1]
-    last = pltpu.make_async_copy(omega_hbm, omega, sems.at[LOADS + 1])
+    last = pltpu.make_async_copy(omega_hbm, omega, sems.at[LOADS + 2])
     last.start()
 
     def clear():
@@ -106,17 +113,18 @@
     def put(slot, row, col):
         dense[col, rows_at(row, size_b), :] = tiles[slot]
 
-    put_live(codes, codes_smem, tiles_hbm, tiles, sems, clear, put)
+    put_live(counts[0], (rows_hbm, cols_hbm), (rows, cols), tiles_hbm, tiles, sems, clear, put)
     last.wait()
     _, core = place()
-    for out, owner in ((sent, 1 - core), (kept, core)):
-        for step in range(out.shape[0] // share):
-            here = rows_at(step * CORES + owner, share)
-            left = jnp.concatenate([dense[c, here, :] for c in range(dense.shape[0])], axis=1)
-            out[step * share : (step + 1) * share, :] = dot(left, omega[...]).astype(out.dtype)
-
-
-def turn_kernel(codes, tiles_hbm, _, turned, token, codes_smem, tiles, sems):
+    multiply(share, 1 - core, dense, omega, sent)
+
+
+def kept_kernel(share, dense, omega, kept):
+    _, core = place()
+    multiply(share, core, dense, omega, kept)
+
+
+def turn_kernel(counts, rows_hbm, cols_hbm, tiles_hbm, _, turned, token, rows, cols, tiles, sems):
     size_b = tiles.shape[1]
     token[...] = jnp.zeros_like(token)
 
@@ -126,7 +134,7 @@
     def put(slot, row, col):
         turned[row, rows_at(col, size_b), :] = tiles[slot].T
 
-    put_live(codes, codes_smem, tiles_hbm, tiles, sems, clear, put)
+    put_live(counts[0], (rows_hbm, cols_hbm), (rows, cols), tiles_hbm, tiles, sems, clear, put)
 
 
 def pair_kernel(share, kept, came, own, token, *sends):
@@ -148,8 +156,8 @@
     refs[count][...] = total.astype(BF)
 
 
-def tree_kernel(own, *refs):
-    refs[-1][...] = tree_sum([own[...]] + [ref[...] for ref in reversed(refs[:-1])])
+def tree_kernel(count, own, *refs):
+    refs[-1][...] = tree_sum([own[...]] + [ref[...] for ref in refs[: count - 1]])
 
 
 def tree_sum(terms):
@@ -183,21 +191,27 @@
         full[rows_at(z * CORES + (1 - core), share), :] = other[here, :]
 
 
-def back_kernel(turned, full, own, gram, *sends):
+def gram_kernel(mine, gram):
+    z, _ = place()
+    half = gram.shape[1]
+    quarter = half // SIDES
+    for side in range(SIDES):
+
+        @pl.when(z % SIDES == side)
+        def _():
+            diagonal = mine[:, side * half : (side + 1) * half]
+            gram[:half, :] = dot(diagonal, diagonal, TN)
+            lower = mine[:, half + side * quarter : half + (side + 1) * quarter]
+            gram[half:, :] = dot(lower, mine[:, :half], TN)
+
+
+def two_kernel(first, second, out):
+    out[...] = first[...] + second[...]
+
+
+def back_kernel(turned, full, _, own, *sends):
     me = lax.axis_index("row")
-    _, core = place()
     share = own.shape[0]
-    half = gram.shape[1]
-    quarter = half // CORES
-    for side in range(CORES):
-
-        @pl.when(core == side)
-        def _():
-            diagonal = full[:, side * half : (side + 1) * half]
-            gram[:half, :] = dot(diagonal, diagonal, TN)
-            lower = full[:, half + side * quarter : half + (side + 1) * quarter]
-            gram[half:, :] = dot(lower, full[:, :half], TN)
-
     for step in list(range(1, len(sends) + 1)) + [0]:
         here = rows_at(me ^ step, share)
         left = jnp.concatenate([turned[r, here, :] for r in range(turned.shape[0])], axis=1)
@@ -210,17 +224,13 @@
 
 def factor_kernel(scale, *refs):
     mine, other, rows, high, low, basis, work, inverse = refs
-    _, core = place()
     size = work.shape[0]
-    half, quarter = size // CORES, size // (2 * CORES)
-    for source, owner in ((mine, core), (other, 1 - core)):
-        for side in range(CORES):
-
-            @pl.when(owner == side)
-            def _():
-                work[side * half : (side + 1) * half, side * half : (side + 1) * half] = source[:half, :]
-                here = slice(half + side * quarter, half + (side + 1) * quarter)
-                work[here, :half] = source[half:, :]
+    half, quarter = size // SIDES, size // (2 * SIDES)
+    z, _ = place()
+    for side in range(SIDES):
+        blocks = jnp.where(z % SIDES == side, mine[...], other[...])
+        work[side * half : (side + 1) * half, side * half : (side + 1) * half] = blocks[:half, :]
+        work[half + side * quarter : half + (side + 1) * quarter, :half] = blocks[half:, :]
     work[:half, half:] = work[half:, :half].T
     gram = work[...]
     row_id = lax.broadcasted_iota(jnp.int32, (size, size), 0)
@@ -275,8 +285,8 @@
     out = refs[-1]
     me = lax.axis_index("row")
     share = refs[0].shape[0]
-    for index, step in enumerate([0] + list(reversed(range(1, count)))):
-        chunk = refs[index][...]
+    for step in range(count):
+        chunk = refs[step][...]
         product = dot(chunk, high[...], NT) + dot(chunk, low[...], NT)
         out[rows_at(me ^ step, share), :] = (product * scale).astype(BF)
 
@@ -310,41 +320,48 @@
         return [("v", x) for x in xs]
 
     part_shape = (share, rank)
-    places = tile_rows * CODE + tile_cols
-    padded = (slots // LANES + 1) * LANES
-    codes = jnp.where(jnp.arange(padded) < slots, jnp.pad(places, (0, padded - slots)), counts[0])
-    inputs = [("a", codes), ("h", tiles)]
-    slot_scratch = [pltpu.SMEM((padded,), jnp.int32), pltpu.VMEM(tiles.shape, BF)]
-    sent, kept = call(
+    inputs = [("s", counts), ("h", tile_rows), ("h", tile_cols), ("h", tiles)]
+    slot_scratch = [
+        pltpu.SMEM((slots,), jnp.int32),
+        pltpu.SMEM((slots,), jnp.int32),
+        pltpu.VMEM(tiles.shape, BF),
+    ]
+    sent, dense, omega_here = call(
         "sketch",
         functools.partial(sketch_kernel, share),
         inputs + [("h", omega)],
-        [array((zs * share, rank), BF), array((zs * share, rank), F32)],
-        slot_scratch
-        + [
-            pltpu.VMEM(omega.shape, BF),
-            pltpu.VMEM((col_blocks, rows_here, size_b), BF),
-            pltpu.SemaphoreType.DMA((LOADS + 2,)),
+        [
+            array((zs * share, rank), BF),
+            array((col_blocks, rows_here, size_b), BF),
+            array(omega.shape, BF),
         ],
-        limit=SKETCH_LIMIT,
-        flops=2 * rows_here * cols_here * rank,
+        slot_scratch + [pltpu.SemaphoreType.DMA((LOADS + 3,))],
+        flops=rows_here * cols_here * rank,
         nbytes=6 * MIB,
+    )
+    came = swap_core(sent)
+    (kept,) = call(
+        "kept",
+        functools.partial(kept_kernel, share),
+        vs(dense, omega_here),
+        [array((zs * share, rank), F32)],
+        flops=rows_here * cols_here * rank,
+        nbytes=1,
     )
     own, token, *sends = call(
         "pair",
         functools.partial(pair_kernel, share),
-        vs(kept, swap_core(sent)),
+        vs(kept, came),
         [array(part_shape, F32), array(TOKEN, F32)] + [array(part_shape, BF)] * (zs - 1),
         nbytes=MIB,
     )
-    gets = [swap_z(x, k + 1) for k, x in enumerate(sends)]
+    gets = [swap_z(sends[k - 1], k) for k in far_first(zs)]
     turned, token = call(
         "turn",
         turn_kernel,
         inputs + [("a", token)],
         [array((RB_DEV, cols_here, size_b), BF), array(TOKEN, F32)],
-        slot_scratch + [pltpu.SemaphoreType.DMA((LOADS + 1,))],
-        limit=TURN_LIMIT,
+        slot_scratch + [pltpu.SemaphoreType.DMA((LOADS + 2,))],
         nbytes=8 * MIB,
     )
     own_rows, rows_bf = call(
@@ -355,7 +372,7 @@
         nbytes=MIB,
     )
     chunks = {k: swap_z(rows_bf, k) for k in range(1, zs)}
-    order = list(reversed(far_first(zs)))
+    order = far_first(zs)
     (mine,) = call(
         "pack",
         functools.partial(pack_kernel, order),
@@ -370,13 +387,15 @@
         [array((rows_here, rank), BF)],
         nbytes=MIB,
     )
-    half = rank // CORES
-    gram_shape = (half + half // CORES, half)
-    own, gram, *sends = call(
+    half = rank // SIDES
+    gram_rows = half + half // SIDES
+    gram_out = [array((gram_rows, half), F32)]
+    (gram,) = call("gram", gram_kernel, vs(mine), gram_out, nbytes=1)
+    own, *sends = call(
         "back",
         back_kernel,
-        vs(turned, full),
-        [array((back_share, rank), F32), array(gram_shape, F32)] + [array((back_share, rank), BF)] * (row_groups - 1),
+        vs(turned, full) + [("a", gram)],
+        [array((back_share, rank), F32)] + [array((back_share, rank), BF)] * (row_groups - 1),
         flops=2 * rows_here * cols_here * rank,
         nbytes=6 * MIB,
     )
@@ -388,16 +407,17 @@
         [array((back_share, rank), BF)],
         nbytes=1,
     )
-    backs = [back_sum] + [swap_row(back_sum, k) for k in reversed(range(1, row_groups))]
-    terms = [gram] + [swap_row(gram, k) for k in reversed(range(1, row_groups))]
-    (gram_sum,) = call("tree", tree_kernel, vs(*terms), [array(gram_shape, F32)], nbytes=1)
+    backs = [back_sum] + [swap_row(back_sum, k) for k in range(1, row_groups)]
+    terms = [gram] + [swap_row(gram, k) for k in range(1, row_groups)]
+    (gram,) = call("tree", functools.partial(tree_kernel, len(terms)), vs(*terms) + [("a", own)], gram_out, nbytes=1)
+    (gram,) = call("two", two_kernel, vs(gram, swap_core(gram)), gram_out, nbytes=1)
     high, low, basis = call(
         "factor",
         functools.partial(factor_kernel, float(total_rows) ** 0.5),
-        vs(gram_sum, swap_core(gram_sum), own_rows),
+        vs(gram, swap_z(gram, 1), own_rows),
         [array((rank, rank), BF), array((rank, rank), BF), array((share, rank), BF)],
         [pltpu.VMEM((rank, rank), F32), pltpu.VMEM((rank, rank), F32)],
-        flops=1,
+        flops=int(FACTOR_FLOPS * rank**3),
         nbytes=1,
     )
     (projected,) = call(

time: 101 us -> 95.1 us (0.942)
  starting transfers between devices: 24 us -> 21.9 us
  local copies, waits for them, and re-layouts: 1.05 us -> 0 us
    ppermute x3, waiting for transfers between devices: 4.72 us -> 2.12 us  [swap_core(): return lax.ppermute(x, 'col', [(i, i ^ 1) for i in range(col_groups)])]
    ppermute x9, waiting for transfers between devices: 1.61 us -> 4.14 us  [swap_row(): return lax.ppermute(x, 'row', [(i, i ^ step) for i in range(row_groups)])]
    ppermute x9, starting transfers between devices: 13 us -> 10.7 us  [swap_row(): return lax.ppermute(x, 'row', [(i, i ^ step) for i in range(row_groups)])]
    unnamed x4 -> x0, local copies, waits for them, and re-layouts: 1.05 us -> none
    pallas_call x11 -> x14, Pallas kernels: 52.2 us -> 51.5 us  [call(): pl.pallas_call(body, out_shape=outs, in_specs=[pl.BlockSpec(memory_space=...]
    ppermute x6 -> x7, starting transfers between devices: 9.94 us -> 10.4 us  [swap_z(): lax.ppermute(x, 'col', [(i, i ^ CORES * step) for i in range(col_groups)])]
    ppermute x6 -> x7, waiting for transfers between devices: 14.2 us -> 13.9 us  [swap_z(): lax.ppermute(x, 'col', [(i, i ^ CORES * step) for i in range(col_groups)])]
  transfers between devices with their start and end apart: 18 -> 19, of which waited for: 9 -> 10; matrix products, arithmetic and copies ran while one was open for 0% -> 0% of each run, Pallas kernels for 45% -> 50%
where the time goes in v3:
time: 95.1 us; the launch traced here: 95 us
  Pallas kernels  51.5 us (54%)
  starting transfers between devices  21.9 us (23%)
  waiting for transfers between devices  20.2 us (21%)
  between operations  1.39 us (1%)
    pallas_call x14, Pallas kernels, call(): pl.pallas_call(body, out_shape=outs, in_specs=[pl.BlockSpec(memory_space=...  51.5 us
    ppermute x7, waiting for transfers between devices, swap_z(): lax.ppermute(x, 'col', [(i, i ^ CORES * step) for i in range(col_groups)])  13.9 us
    ppermute x9, starting transfers between devices, swap_row(): return lax.ppermute(x, 'row', [(i, i ^ step) for i in range(row_groups)])  10.7 us
    ppermute x7, starting transfers between devices, swap_z(): lax.ppermute(x, 'col', [(i, i ^ CORES * step) for i in range(col_groups)])  10.4 us
    ppermute x9, waiting for transfers between devices, swap_row(): return lax.ppermute(x, 'row', [(i, i ^ step) for i in range(row_groups)])  4.14 us
    ppermute x3, waiting for transfers between devices, swap_core(): return lax.ppermute(x, 'col', [(i, i ^ 1) for i in range(col_groups)])  2.12 us
  transfers between devices with their start and end apart: 19, of which 10 were waited for; matrix products, arithmetic and copies ran while one was open for 0% of the time, Pallas kernels for 50%

profile of v3, /device:TPU:0, one launch (start us, length us, event | category | flops | bytes accessed | tf_op | source)
XLA Modules:
  0.0 95.0 jit_solution(2652796325298816548)
XLA Ops:
  1.3 2.8 %sketch.1 = (bf16[1024,256]{1,0:T(8,128)(2,1)S(1)}, bf16[8,2048,128]{2,1,0:T(8,128)(2,1)S(1)}, bf16[1024,256]{1,0:T(8,128)(2,1)S(1)}) custom-call(s32[1]{0:T(128)S(6)} %copy.7.counts, s32[96]{0:T(128)} %rows_hbm.3, s32[96]{0:T(128)} %cols_hbm.3, bf16[96,128,128]{2,1,0:T(8,128)(2,1)} %tiles_hbm.3, bf16[1024,256]{1,0:T(8,128)(2,1)} %omega_hbm.1), custom_call_target="tpu_custom_call" | custom-call | flops 536870912 | bytes 6291456 | tf_op jit(solution)/shard_map/sketch/pallas_call | solution.py:28
  4.1 0.7 collective-permute-start
  4.8 0.7 kept.1
  5.5 0.8 collective-permute-done.came
  6.4 4.9 %collective-permute-start.1 = (bf16[256,256]{1,0:T(8,128)(2,1)S(1)}, bf16[256,256]{1,0:T(8,128)(2,1)S(1)}, u32[]{:S(2)}, u32[]{:S(2)}) collective-permute-start(bf16[256,256]{1,0:T(8,128)(2,1)S(1)} %get-tuple-element.25), channel_id=1, source_target_pairs={{0,6},{1,7},{2,4},{3,5},{4,2},{5,3},{6,0},{7,1},{8,14},{9,15},{10,... | collective-permute-start | bytes 393224 | tf_op jit(solution)/shard_map/ppermute | solution.py:311
  11.2 0.6 collective-permute-start.3
  11.9 4.9 %turn.1 = (bf16[16,1024,128]{2,1,0:T(8,128)(2,1)S(1)}, f32[8,128]{1,0:T(8,128)S(1)}) custom-call(s32[1]{0:T(128)S(6)} %copy.7.counts, s32[96]{0:T(128)} %rows_hbm.3, s32[96]{0:T(128)} %cols_hbm.3, bf16[96,128,128]{2,1,0:T(8,128)(2,1)} %tiles_hbm.3, f32[8,128]{1,0:T(8,128)S(1)} %get-tuple-element.28._), custom_call_target="tpu_custom_call" | custom-call | bytes 8388608 | tf_op jit(solution)/shard_map/turn/pallas_call | solution.py:28
  16.8 2.1 %collective-permute-done.2.refs_1_ = bf16[256,256]{1,0:T(8,128)(2,1)S(1)} collective-permute-done((bf16[256,256]{1,0:T(8,128)(2,1)S(1)}, bf16[256,256]{1,0:T(8,128)(2,1)S(1)}, u32[]{:S(2)}, u32[]{:S(2)}) %collective-permute-start.2) | collective-permute-done | bytes 131104 | tf_op jit(solution)/shard_map/ppermute | solution.py:311
  18.9 3.7 %collective-permute-done.3.refs_2_ = bf16[256,256]{1,0:T(8,128)(2,1)S(1)} collective-permute-done((bf16[256,256]{1,0:T(8,128)(2,1)S(1)}, bf16[256,256]{1,0:T(8,128)(2,1)S(1)}, u32[]{:S(2)}, u32[]{:S(2)}) %collective-permute-start.3) | collective-permute-done | bytes 131104 | tf_op jit(solution)/shard_map/ppermute | solution.py:311
  22.7 2.5 %collective-permute-start.4 = (bf16[256,256]{1,0:T(8,128)(2,1)S(1)}, bf16[256,256]{1,0:T(8,128)(2,1)S(1)}, u32[]{:S(2)}, u32[]{:S(2)}) collective-permute-start(bf16[256,256]{1,0:T(8,128)(2,1)S(1)} %get-tuple-element.30.own), channel_id=1, source_target_pairs={{0,6},{1,7},{2,4},{3,5},{4,2},{5,3},{6,0},{7,1},{8,14},{9,15},{10,... | collective-permute-start | bytes 393224 | tf_op jit(solution)/shard_map/ppermute | solution.py:311
  25.2 1.9 %collective-permute-start.6 = (bf16[256,256]{1,0:T(8,128)(2,1)S(1)}, bf16[256,256]{1,0:T(8,128)(2,1)S(1)}, u32[]{:S(2)}, u32[]{:S(2)}) collective-permute-start(bf16[256,256]{1,0:T(8,128)(2,1)S(1)} %get-tuple-element.30.own), channel_id=1, source_target_pairs={{0,4},{1,5},{2,6},{3,7},{4,0},{5,1},{6,2},{7,3},{8,12},{9,13},{10,... | collective-permute-start | bytes 393224 | tf_op jit(solution)/shard_map/ppermute | solution.py:311
  27.2 3.8 %collective-permute-done.4.refs_0_ = bf16[256,256]{1,0:T(8,128)(2,1)S(1)} collective-permute-done((bf16[256,256]{1,0:T(8,128)(2,1)S(1)}, bf16[256,256]{1,0:T(8,128)(2,1)S(1)}, u32[]{:S(2)}, u32[]{:S(2)}) %collective-permute-start.4) | collective-permute-done | bytes 131104 | tf_op jit(solution)/shard_map/ppermute | solution.py:311
  31.0 2.2 %collective-permute-done.5.refs_1_ = bf16[256,256]{1,0:T(8,128)(2,1)S(1)} collective-permute-done((bf16[256,256]{1,0:T(8,128)(2,1)S(1)}, bf16[256,256]{1,0:T(8,128)(2,1)S(1)}, u32[]{:S(2)}, u32[]{:S(2)}) %collective-permute-start.5) | collective-permute-done | bytes 131104 | tf_op jit(solution)/shard_map/ppermute | solution.py:311
  33.2 2.1 %collective-permute-done.6.refs_2_ = bf16[256,256]{1,0:T(8,128)(2,1)S(1)} collective-permute-done((bf16[256,256]{1,0:T(8,128)(2,1)S(1)}, bf16[256,256]{1,0:T(8,128)(2,1)S(1)}, u32[]{:S(2)}, u32[]{:S(2)}) %collective-permute-start.6) | collective-permute-done | bytes 131104 | tf_op jit(solution)/shard_map/ppermute | solution.py:311
  35.4 0.3 gram.1._.own
  35.7 1.6 %collective-permute-start.7 = (f32[192,128]{1,0:T(8,128)S(1)}, f32[192,128]{1,0:T(8,128)S(1)}, u32[]{:S(2)}, u32[]{:S(2)}) collective-permute-start(f32[192,128]{1,0:T(8,128)S(1)} %gram.1._.own), channel_id=1, source_target_pairs={{0,8},{8,0},{16,24},{24,16},{1,9},{9,1},{17,25},{25,17},{2,10},{10... | collective-permute-start | bytes 294920 | tf_op jit(solution)/shard_map/ppermute | solution.py:314
  37.3 1.6 %collective-permute-start.8 = (f32[192,128]{1,0:T(8,128)S(1)}, f32[192,128]{1,0:T(8,128)S(1)}, u32[]{:S(2)}, u32[]{:S(2)}) collective-permute-start(f32[192,128]{1,0:T(8,128)S(1)} %gram.1._.own), channel_id=1, source_target_pairs={{0,16},{8,24},{16,0},{24,8},{1,17},{9,25},{17,1},{25,9},{2,18},{10... | collective-permute-start | bytes 294920 | tf_op jit(solution)/shard_map/ppermute | solution.py:314
  38.9 0.4 collective-permute-start.9
  39.4 1.2 %back.1 = (f32[256,256]{1,0:T(8,128)S(1)}, bf16[256,256]{1,0:T(8,128)(2,1)S(1)}, bf16[256,256]{1,0:T(8,128)(2,1)S(1)}, bf16[256,256]{1,0:T(8,128)(2,1)S(1)}) custom-call(bf16[16,1024,128]{2,1,0:T(8,128)(2,1)S(1)} %get-tuple-element.31.turned, bf16[2048,256]{1,0:T(8,128)(2,1)S(1)} %full.1, f32[192,128]{1,0:T(8,128)S(1)} %gram.1._.own), custom_call_target="tpu_custom_call" | custom-call | flops 1073741824 | bytes 6291456 | tf_op jit(solution)/shard_map/back/pallas_call | solution.py:28
  40.6 1.6 %collective-permute-start.13 = (bf16[256,256]{1,0:T(8,128)(2,1)S(1)}, bf16[256,256]{1,0:T(8,128)(2,1)S(1)}, u32[]{:S(2)}, u32[]{:S(2)}) collective-permute-start(bf16[256,256]{1,0:T(8,128)(2,1)S(1)} %get-tuple-element.37), channel_id=1, source_target_pairs={{0,8},{8,0},{16,24},{24,16},{1,9},{9,1},{17,25},{25,17},{2,10},{10... | collective-permute-start | bytes 393224 | tf_op jit(solution)/shard_map/ppermute | solution.py:314
  42.2 1.6 %collective-permute-start.14 = (bf16[256,256]{1,0:T(8,128)(2,1)S(1)}, bf16[256,256]{1,0:T(8,128)(2,1)S(1)}, u32[]{:S(2)}, u32[]{:S(2)}) collective-permute-start(bf16[256,256]{1,0:T(8,128)(2,1)S(1)} %get-tuple-element.38), channel_id=1, source_target_pairs={{0,16},{8,24},{16,0},{24,8},{1,17},{9,25},{17,1},{25,9},{2,18},{10... | collective-permute-start | bytes 393224 | tf_op jit(solution)/shard_map/ppermute | solution.py:314
  43.8 0.4 collective-permute-start.15
  44.2 0.8 collective-permute-done.9.refs_2_
  45.1 1.3 %collective-permute-done.11.second = f32[192,128]{1,0:T(8,128)S(1)} collective-permute-done((f32[192,128]{1,0:T(8,128)S(1)}, f32[192,128]{1,0:T(8,128)S(1)}, u32[]{:S(2)}, u32[]{:S(2)}) %collective-permute-start.11) | collective-permute-done | bytes 98336 | tf_op jit(solution)/shard_map/ppermute | solution.py:308
  46.4 0.5 collective-permute-start.12
  46.9 0.2 collective-permute-done.13.refs_0_
  47.1 3.1 %collective-permute-done.14.refs_1_ = bf16[256,256]{1,0:T(8,128)(2,1)S(1)} collective-permute-done((bf16[256,256]{1,0:T(8,128)(2,1)S(1)}, bf16[256,256]{1,0:T(8,128)(2,1)S(1)}, u32[]{:S(2)}, u32[]{:S(2)}) %collective-permute-start.14) | collective-permute-done | bytes 131104 | tf_op jit(solution)/shard_map/ppermute | solution.py:314
  50.3 1.1 %collective-permute-start.16 = (bf16[256,256]{1,0:T(8,128)(2,1)S(1)}, bf16[256,256]{1,0:T(8,128)(2,1)S(1)}, u32[]{:S(2)}, u32[]{:S(2)}) collective-permute-start(bf16[256,256]{1,0:T(8,128)(2,1)S(1)} %columns.1.refs_0_), channel_id=1, source_target_pairs={{0,8},{8,0},{16,24},{24,16},{1,9},{9,1},{17,25},{25,17},{2,10},{10... | collective-permute-start | bytes 393224 | tf_op jit(solution)/shard_map/ppermute | solution.py:314
  51.4 0.8 collective-permute-start.17
  52.1 1.7 %collective-permute-start.18 = (bf16[256,256]{1,0:T(8,128)(2,1)S(1)}, bf16[256,256]{1,0:T(8,128)(2,1)S(1)}, u32[]{:S(2)}, u32[]{:S(2)}) collective-permute-start(bf16[256,256]{1,0:T(8,128)(2,1)S(1)} %columns.1.refs_0_), channel_id=1, source_target_pairs={{0,24},{8,16},{16,8},{24,0},{1,25},{9,17},{17,9},{25,1},{2,26},{10... | collective-permute-start | bytes 393224 | tf_op jit(solution)/shard_map/ppermute | solution.py:314
  53.8 39.9 %factor.1 = (bf16[256,256]{1,0:T(8,128)(2,1)S(1)}, bf16[256,256]{1,0:T(8,128)(2,1)S(1)}, bf16[256,256]{1,0:T(8,128)(2,1)}) custom-call(f32[192,128]{1,0:T(8,128)S(1)} %two.1.refs_0_, f32[192,128]{1,0:T(8,128)S(1)} %collective-permute-done.12.refs_1_, f32[256,256]{1,0:T(8,128)S(1)} %get-tuple-element.33.refs_2_), custom_call_target="tpu_custom_call" | custom-call | flops 671088640 | bytes 1 | tf_op jit(solution)/shard_map/factor/pallas_call | solution.py:28
  93.7 1.3 %project.1 = bf16[1024,256]{1,0:T(8,128)(2,1)} custom-call(bf16[256,256]{1,0:T(8,128)(2,1)S(1)} %get-tuple-element.35.high, bf16[256,256]{1,0:T(8,128)(2,1)S(1)} %get-tuple-element.36.low, bf16[256,256]{1,0:T(8,128)(2,1)S(1)} %columns.1.refs_0_, bf16[256,256]{1,0:T(8,128)(2,1)S(1)} %collective-permute-done.16.refs_1_, ...), custom_call_target="tpu_custom_call" | custom-call | flops 268435456 | bytes 2097152 | tf_op jit(solution)/shard_map/project/pallas_call | solution.py:28
  (20 shorter events, 0.6 us)
Async XLA Ops:
  4.1 2.2 %collective-permute-start = (bf16[1024,256]{1,0:T(8,128)(2,1)S(1)}, bf16[1024,256]{1,0:T(8,128)(2,1)S(1)}, u32[]{:S(2)}, u32[]{:S(2)}) collective-permute-start(bf16[1024,256]{1,0:T(8,128)(2,1)S(1)} %get-tuple-element.23), channel_id=1, source_target_pairs={{0,1},{1,0},{2,3},{3,2},{4,5},{5,4},{6,7},{7,6},{8,9},{9,8},{10,11... | collective-permute-start | bytes 1572872 | tf_op jit(solution)/shard_map/ppermute | solution.py:308
  6.4 10.4 %collective-permute-start.1 = (bf16[256,256]{1,0:T(8,128)(2,1)S(1)}, bf16[256,256]{1,0:T(8,128)(2,1)S(1)}, u32[]{:S(2)}, u32[]{:S(2)}) collective-permute-start(bf16[256,256]{1,0:T(8,128)(2,1)S(1)} %get-tuple-element.25), channel_id=1, source_target_pairs={{0,6},{1,7},{2,4},{3,5},{4,2},{5,3},{6,0},{7,1},{8,14},{9,15},{10,... | collective-permute-start | bytes 393224 | tf_op jit(solution)/shard_map/ppermute | solution.py:311
  11.2 7.7 %collective-permute-start.2 = (bf16[256,256]{1,0:T(8,128)(2,1)S(1)}, bf16[256,256]{1,0:T(8,128)(2,1)S(1)}, u32[]{:S(2)}, u32[]{:S(2)}) collective-permute-start(bf16[256,256]{1,0:T(8,128)(2,1)S(1)} %get-tuple-element.26), channel_id=1, source_target_pairs={{0,2},{1,3},{2,0},{3,1},{4,6},{5,7},{6,4},{7,5},{8,10},{9,11},{10,... | collective-permute-start | bytes 393224 | tf_op jit(solution)/shard_map/ppermute | solution.py:311
  11.2 11.4 %collective-permute-start.3 = (bf16[256,256]{1,0:T(8,128)(2,1)S(1)}, bf16[256,256]{1,0:T(8,128)(2,1)S(1)}, u32[]{:S(2)}, u32[]{:S(2)}) collective-permute-start(bf16[256,256]{1,0:T(8,128)(2,1)S(1)} %get-tuple-element.27), channel_id=1, source_target_pairs={{0,4},{1,5},{2,6},{3,7},{4,0},{5,1},{6,2},{7,3},{8,12},{9,13},{10,... | collective-permute-start | bytes 393224 | tf_op jit(solution)/shard_map/ppermute | solution.py:311
  22.7 8.3 %collective-permute-start.4 = (bf16[256,256]{1,0:T(8,128)(2,1)S(1)}, bf16[256,256]{1,0:T(8,128)(2,1)S(1)}, u32[]{:S(2)}, u32[]{:S(2)}) collective-permute-start(bf16[256,256]{1,0:T(8,128)(2,1)S(1)} %get-tuple-element.30.own), channel_id=1, source_target_pairs={{0,6},{1,7},{2,4},{3,5},{4,2},{5,3},{6,0},{7,1},{8,14},{9,15},{10,... | collective-permute-start | bytes 393224 | tf_op jit(solution)/shard_map/ppermute | solution.py:311
  25.2 8.0 %collective-permute-start.5 = (bf16[256,256]{1,0:T(8,128)(2,1)S(1)}, bf16[256,256]{1,0:T(8,128)(2,1)S(1)}, u32[]{:S(2)}, u32[]{:S(2)}) collective-permute-start(bf16[256,256]{1,0:T(8,128)(2,1)S(1)} %get-tuple-element.30.own), channel_id=1, source_target_pairs={{0,2},{1,3},{2,0},{3,1},{4,6},{5,7},{6,4},{7,5},{8,10},{9,11},{10,... | collective-permute-start | bytes 393224 | tf_op jit(solution)/shard_map/ppermute | solution.py:311
  25.2 10.0 %collective-permute-start.6 = (bf16[256,256]{1,0:T(8,128)(2,1)S(1)}, bf16[256,256]{1,0:T(8,128)(2,1)S(1)}, u32[]{:S(2)}, u32[]{:S(2)}) collective-permute-start(bf16[256,256]{1,0:T(8,128)(2,1)S(1)} %get-tuple-element.30.own), channel_id=1, source_target_pairs={{0,4},{1,5},{2,6},{3,7},{4,0},{5,1},{6,2},{7,3},{8,12},{9,13},{10,... | collective-permute-start | bytes 393224 | tf_op jit(solution)/shard_map/ppermute | solution.py:311
  35.3 4.0 %collective-permute-start.10 = (bf16[1024,256]{1,0:T(8,128)(2,1)S(1)}, bf16[1024,256]{1,0:T(8,128)(2,1)S(1)}, u32[]{:S(2)}, u32[]{:S(2)}) collective-permute-start(bf16[1024,256]{1,0:T(8,128)(2,1)S(1)} %pack.1.mine), channel_id=1, source_target_pairs={{0,1},{1,0},{2,3},{3,2},{4,5},{5,4},{6,7},{7,6},{8,9},{9,8},{10,11... | collective-permute-start | bytes 1572872 | tf_op jit(solution)/shard_map/ppermute | solution.py:308
  35.7 8.1 %collective-permute-start.7 = (f32[192,128]{1,0:T(8,128)S(1)}, f32[192,128]{1,0:T(8,128)S(1)}, u32[]{:S(2)}, u32[]{:S(2)}) collective-permute-start(f32[192,128]{1,0:T(8,128)S(1)} %gram.1._.own), channel_id=1, source_target_pairs={{0,8},{8,0},{16,24},{24,16},{1,9},{9,1},{17,25},{25,17},{2,10},{10... | collective-permute-start | bytes 294920 | tf_op jit(solution)/shard_map/ppermute | solution.py:314
  37.3 6.9 %collective-permute-start.8 = (f32[192,128]{1,0:T(8,128)S(1)}, f32[192,128]{1,0:T(8,128)S(1)}, u32[]{:S(2)}, u32[]{:S(2)}) collective-permute-start(f32[192,128]{1,0:T(8,128)S(1)} %gram.1._.own), channel_id=1, source_target_pairs={{0,16},{8,24},{16,0},{24,8},{1,17},{9,25},{17,1},{25,9},{2,18},{10... | collective-permute-start | bytes 294920 | tf_op jit(solution)/shard_map/ppermute | solution.py:314
  38.9 6.1 %collective-permute-start.9 = (f32[192,128]{1,0:T(8,128)S(1)}, f32[192,128]{1,0:T(8,128)S(1)}, u32[]{:S(2)}, u32[]{:S(2)}) collective-permute-start(f32[192,128]{1,0:T(8,128)S(1)} %gram.1._.own), channel_id=1, source_target_pairs={{0,24},{8,16},{16,8},{24,0},{1,25},{9,17},{17,9},{25,1},{2,26},{10... | collective-permute-start | bytes 294920 | tf_op jit(solution)/shard_map/ppermute | solution.py:314
  40.6 6.5 %collective-permute-start.13 = (bf16[256,256]{1,0:T(8,128)(2,1)S(1)}, bf16[256,256]{1,0:T(8,128)(2,1)S(1)}, u32[]{:S(2)}, u32[]{:S(2)}) collective-permute-start(bf16[256,256]{1,0:T(8,128)(2,1)S(1)} %get-tuple-element.37), channel_id=1, source_target_pairs={{0,8},{8,0},{16,24},{24,16},{1,9},{9,1},{17,25},{25,17},{2,10},{10... | collective-permute-start | bytes 393224 | tf_op jit(solution)/shard_map/ppermute | solution.py:314
  42.2 8.0 %collective-permute-start.14 = (bf16[256,256]{1,0:T(8,128)(2,1)S(1)}, bf16[256,256]{1,0:T(8,128)(2,1)S(1)}, u32[]{:S(2)}, u32[]{:S(2)}) collective-permute-start(bf16[256,256]{1,0:T(8,128)(2,1)S(1)} %get-tuple-element.38), channel_id=1, source_target_pairs={{0,16},{8,24},{16,0},{24,8},{1,17},{9,25},{17,1},{25,9},{2,18},{10... | collective-permute-start | bytes 393224 | tf_op jit(solution)/shard_map/ppermute | solution.py:314
  43.8 6.4 %collective-permute-start.15 = (bf16[256,256]{1,0:T(8,128)(2,1)S(1)}, bf16[256,256]{1,0:T(8,128)(2,1)S(1)}, u32[]{:S(2)}, u32[]{:S(2)}) collective-permute-start(bf16[256,256]{1,0:T(8,128)(2,1)S(1)} %get-tuple-element.39), channel_id=1, source_target_pairs={{0,24},{8,16},{16,8},{24,0},{1,25},{9,17},{17,9},{25,1},{2,26},{10... | collective-permute-start | bytes 393224 | tf_op jit(solution)/shard_map/ppermute | solution.py:314
  45.1 1.4 %collective-permute-start.11 = (f32[192,128]{1,0:T(8,128)S(1)}, f32[192,128]{1,0:T(8,128)S(1)}, u32[]{:S(2)}, u32[]{:S(2)}) collective-permute-start(f32[192,128]{1,0:T(8,128)S(1)} %tree.1.first), channel_id=1, source_target_pairs={{0,1},{1,0},{2,3},{3,2},{4,5},{5,4},{6,7},{7,6},{8,9},{9,8},{10,11... | collective-permute-start | bytes 294920 | tf_op jit(solution)/shard_map/ppermute | solution.py:308
  46.4 7.4 %collective-permute-start.12 = (f32[192,128]{1,0:T(8,128)S(1)}, f32[192,128]{1,0:T(8,128)S(1)}, u32[]{:S(2)}, u32[]{:S(2)}) collective-permute-start(f32[192,128]{1,0:T(8,128)S(1)} %two.1.refs_0_), channel_id=1, source_target_pairs={{0,2},{1,3},{2,0},{3,1},{4,6},{5,7},{6,4},{7,5},{8,10},{9,11},{10,... | collective-permute-start | bytes 294920 | tf_op jit(solution)/shard_map/ppermute | solution.py:311
  50.3 43.4 %collective-permute-start.16 = (bf16[256,256]{1,0:T(8,128)(2,1)S(1)}, bf16[256,256]{1,0:T(8,128)(2,1)S(1)}, u32[]{:S(2)}, u32[]{:S(2)}) collective-permute-start(bf16[256,256]{1,0:T(8,128)(2,1)S(1)} %columns.1.refs_0_), channel_id=1, source_target_pairs={{0,8},{8,0},{16,24},{24,16},{1,9},{9,1},{17,25},{25,17},{2,10},{10... | collective-permute-start | bytes 393224 | tf_op jit(solution)/shard_map/ppermute | solution.py:314
  51.4 42.4 %collective-permute-start.17 = (bf16[256,256]{1,0:T(8,128)(2,1)S(1)}, bf16[256,256]{1,0:T(8,128)(2,1)S(1)}, u32[]{:S(2)}, u32[]{:S(2)}) collective-permute-start(bf16[256,256]{1,0:T(8,128)(2,1)S(1)} %columns.1.refs_0_), channel_id=1, source_target_pairs={{0,16},{8,24},{16,0},{24,8},{1,17},{9,25},{17,1},{25,9},{2,18},{10... | collective-permute-start | bytes 393224 | tf_op jit(solution)/shard_map/ppermute | solution.py:314
  52.1 41.6 %collective-permute-start.18 = (bf16[256,256]{1,0:T(8,128)(2,1)S(1)}, bf16[256,256]{1,0:T(8,128)(2,1)S(1)}, u32[]{:S(2)}, u32[]{:S(2)}) collective-permute-start(bf16[256,256]{1,0:T(8,128)(2,1)S(1)} %columns.1.refs_0_), channel_id=1, source_target_pairs={{0,24},{8,16},{16,8},{24,0},{1,25},{9,17},{17,9},{25,1},{2,26},{10... | collective-permute-start | bytes 393224 | tf_op jit(solution)/shard_map/ppermute | solution.py:314

commit v4 on v3

--- a/solution.py
+++ b/solution.py
@@ -10,8 +10,8 @@
 RB_DEV = 16
 CORES = 2
 SIDES = 2
-FACTOR_FLOPS = 40
-LOADS = 4
+FACTOR_FLOPS = 45
+LOADS = 8
 TOKEN = (8, 128)
 MIB = 1024 * 1024
 BF = jnp.bfloat16
@@ -76,12 +76,19 @@
         pltpu.make_async_copy(source, target, sems.at[LOADS + k])
         for k, (source, target) in enumerate(zip(places_hbm, places))
     ]
-    copies = []
+    for copy in firsts:
+        copy.start()
+
+    def bring(k):
+        piece = pl.ds(k * load, load)
+        return pltpu.make_async_copy(tiles_hbm.at[piece], tiles.at[piece], sems.at[k])
+
     for k in range(LOADS):
-        piece = pl.ds(k * load, load)
-        copies.append(pltpu.make_async_copy(tiles_hbm.at[piece], tiles.at[piece], sems.at[k]))
-    for copy in firsts + copies:
-        copy.start()
+
+        @pl.when(live > k * load)
+        def _():
+            bring(k).start()
+
     clear()
     for copy in firsts:
         copy.wait()
@@ -90,9 +97,12 @@
         put(slot, rows[slot], cols[slot])
         return carry
 
-    for k, copy in enumerate(copies):
-        copy.wait()
-        lax.fori_loop(k * load, jnp.clip(live, k * load, (k + 1) * load), step, 0)
+    for k in range(LOADS):
+
+        @pl.when(live > k * load)
+        def _():
+            bring(k).wait()
+            lax.fori_loop(k * load, jnp.minimum(live, (k + 1) * load), step, 0)
 
 
 def multiply(share, owner, dense, omega, out):
@@ -194,15 +204,34 @@
 def gram_kernel(mine, gram):
     z, _ = place()
     half = gram.shape[1]
-    quarter = half // SIDES
+    quarter, eighth = half // 2, half // 4
     for side in range(SIDES):
 
         @pl.when(z % SIDES == side)
         def _():
-            diagonal = mine[:, side * half : (side + 1) * half]
-            gram[:half, :] = dot(diagonal, diagonal, TN)
+            columns = mine[:, side * half : (side + 1) * half]
+            block = dot(columns, columns, TN)
             lower = mine[:, half + side * quarter : half + (side + 1) * quarter]
-            gram[half:, :] = dot(lower, mine[:, :half], TN)
+            gram[:quarter, :quarter] = block[:quarter, :quarter]
+            gram[:quarter, quarter:] = block[quarter:, quarter:]
+            gram[quarter : quarter + eighth, :quarter] = block[quarter : quarter + eighth, :quarter]
+            gram[quarter : quarter + eighth, quarter:] = block[quarter + eighth :, :quarter]
+            gram[quarter + eighth :, :] = dot(lower, mine[:, :half], TN)
+
+
+def unpack(blocks, side, work):
+    half = blocks.shape[1]
+    quarter, eighth = half // 2, half // 4
+    first = side * half
+    middle, last = first + quarter, first + half
+    work[first:middle, first:middle] = blocks[:quarter, :quarter]
+    work[middle:last, middle:last] = blocks[:quarter, quarter:]
+    below = jnp.concatenate(
+        [blocks[quarter : quarter + eighth, :quarter], blocks[quarter : quarter + eighth, quarter:]], axis=0
+    )
+    work[middle:last, first:middle] = below
+    work[first:middle, middle:last] = below.T
+    work[half + side * quarter : half + (side + 1) * quarter, :half] = blocks[quarter + eighth :, :]
 
 
 def two_kernel(first, second, out):
@@ -225,12 +254,10 @@
 def factor_kernel(scale, *refs):
     mine, other, rows, high, low, basis, work, inverse = refs
     size = work.shape[0]
-    half, quarter = size // SIDES, size // (2 * SIDES)
+    half = size // SIDES
     z, _ = place()
     for side in range(SIDES):
-        blocks = jnp.where(z % SIDES == side, mine[...], other[...])
-        work[side * half : (side + 1) * half, side * half : (side + 1) * half] = blocks[:half, :]
-        work[half + side * quarter : half + (side + 1) * quarter, :half] = blocks[half:, :]
+        unpack(jnp.where(z % SIDES == side, mine[...], other[...]), side, work)
     work[:half, half:] = work[half:, :half].T
     gram = work[...]
     row_id = lax.broadcasted_iota(jnp.int32, (size, size), 0)
@@ -251,7 +278,7 @@
         phi = rest * phi_mask
         near = near - phi - mul(phi, near)
     inverse[...] = (near + eye) * scale_row
-    converged = jnp.max(jnp.abs(phi)) < 1e-2
+    converged = jnp.sum(phi * phi) < 4e-4
 
     @pl.when(jnp.logical_not(converged))
     def _():
@@ -388,7 +415,7 @@
         nbytes=MIB,
     )
     half = rank // SIDES
-    gram_rows = half + half // SIDES
+    gram_rows = half // 2 + half // 4 + half // 2
     gram_out = [array((gram_rows, half), F32)]
     (gram,) = call("gram", gram_kernel, vs(mine), gram_out, nbytes=1)
     own, *sends = call(

time: 95.1 us -> 95 us (level)
  Pallas kernels: 51.5 us -> 54.7 us
  waiting for transfers between devices: 20.2 us -> 17.5 us
    pallas_call x14, Pallas kernels: 51.5 us -> 54.7 us  [call(): pl.pallas_call(body, out_shape=outs, in_specs=[pl.BlockSpec(memory_space=...]
    ppermute x7, waiting for transfers between devices: 13.9 us -> 11.3 us  [swap_z(): lax.ppermute(x, 'col', [(i, i ^ CORES * step) for i in range(col_groups)])]
  transfers between devices with their start and end apart: 19 -> 19, of which waited for: 10 -> 9; matrix products, arithmetic and copies ran while one was open for 0% -> 0% of each run, Pallas kernels for 50% -> 53%
where the time goes in v4:
time: 95 us; the launch traced here: 94.9 us
  Pallas kernels  54.7 us (58%)
  starting transfers between devices  21.3 us (22%)
  waiting for transfers between devices  17.5 us (18%)
  between operations  1.39 us (1%)
    pallas_call x14, Pallas kernels, call(): pl.pallas_call(body, out_shape=outs, in_specs=[pl.BlockSpec(memory_space=...  54.7 us
    ppermute x7, waiting for transfers between devices, swap_z(): lax.ppermute(x, 'col', [(i, i ^ CORES * step) for i in range(col_groups)])  11.3 us
    ppermute x9, starting transfers between devices, swap_row(): return lax.ppermute(x, 'row', [(i, i ^ step) for i in range(row_groups)])  10.7 us
    ppermute x7, starting transfers between devices, swap_z(): lax.ppermute(x, 'col', [(i, i ^ CORES * step) for i in range(col_groups)])  10.4 us
    ppermute x9, waiting for transfers between devices, swap_row(): return lax.ppermute(x, 'row', [(i, i ^ step) for i in range(row_groups)])  3.76 us
    ppermute x3, waiting for transfers between devices, swap_core(): return lax.ppermute(x, 'col', [(i, i ^ 1) for i in range(col_groups)])  2.46 us
  transfers between devices with their start and end apart: 19, of which 9 were waited for; matrix products, arithmetic and copies ran while one was open for 0% of the time, Pallas kernels for 53%

profile of v4, /device:TPU:0, one launch (start us, length us, event | category | flops | bytes accessed | tf_op | source)
XLA Modules:
  0.0 94.9 jit_solution(4523833364537031095)
XLA Ops:
  1.3 2.9 %sketch.1 = (bf16[1024,256]{1,0:T(8,128)(2,1)S(1)}, bf16[8,2048,128]{2,1,0:T(8,128)(2,1)S(1)}, bf16[1024,256]{1,0:T(8,128)(2,1)S(1)}) custom-call(s32[1]{0:T(128)S(6)} %copy.7.counts, s32[96]{0:T(128)} %rows_hbm.3, s32[96]{0:T(128)} %cols_hbm.3, bf16[96,128,128]{2,1,0:T(8,128)(2,1)} %tiles_hbm.3, bf16[1024,256]{1,0:T(8,128)(2,1)} %omega_hbm.1), custom_call_target="tpu_custom_call" | custom-call | flops 536870912 | bytes 6291456 | tf_op jit(solution)/shard_map/sketch/pallas_call | solution.py:28
  4.2 0.7 kept.1
  4.9 1.2 %collective-permute-done.came = bf16[1024,256]{1,0:T(8,128)(2,1)S(1)} collective-permute-done((bf16[1024,256]{1,0:T(8,128)(2,1)S(1)}, bf16[1024,256]{1,0:T(8,128)(2,1)S(1)}, u32[]{:S(2)}, u32[]{:S(2)}) %collective-permute-start) | collective-permute-done | bytes 524320 | tf_op jit(solution)/shard_map/ppermute | solution.py:335
  6.1 0.1 pair.1
  6.2 4.8 %collective-permute-start.1 = (bf16[256,256]{1,0:T(8,128)(2,1)S(1)}, bf16[256,256]{1,0:T(8,128)(2,1)S(1)}, u32[]{:S(2)}, u32[]{:S(2)}) collective-permute-start(bf16[256,256]{1,0:T(8,128)(2,1)S(1)} %get-tuple-element.25), channel_id=1, source_target_pairs={{0,6},{1,7},{2,4},{3,5},{4,2},{5,3},{6,0},{7,1},{8,14},{9,15},{10,... | collective-permute-start | bytes 393224 | tf_op jit(solution)/shard_map/ppermute | solution.py:338
  11.0 0.6 collective-permute-start.3
  11.6 7.8 %turn.1 = (bf16[16,1024,128]{2,1,0:T(8,128)(2,1)S(1)}, f32[8,128]{1,0:T(8,128)S(1)}) custom-call(s32[1]{0:T(128)S(6)} %copy.7.counts, s32[96]{0:T(128)} %rows_hbm.3, s32[96]{0:T(128)} %cols_hbm.3, bf16[96,128,128]{2,1,0:T(8,128)(2,1)} %tiles_hbm.3, f32[8,128]{1,0:T(8,128)S(1)} %get-tuple-element.28._), custom_call_target="tpu_custom_call" | custom-call | bytes 8388608 | tf_op jit(solution)/shard_map/turn/pallas_call | solution.py:28
  19.5 3.2 %collective-permute-done.3.refs_2_ = bf16[256,256]{1,0:T(8,128)(2,1)S(1)} collective-permute-done((bf16[256,256]{1,0:T(8,128)(2,1)S(1)}, bf16[256,256]{1,0:T(8,128)(2,1)S(1)}, u32[]{:S(2)}, u32[]{:S(2)}) %collective-permute-start.3) | collective-permute-done | bytes 131104 | tf_op jit(solution)/shard_map/ppermute | solution.py:338
  22.7 0.1 rows.1
  22.8 2.5 %collective-permute-start.4 = (bf16[256,256]{1,0:T(8,128)(2,1)S(1)}, bf16[256,256]{1,0:T(8,128)(2,1)S(1)}, u32[]{:S(2)}, u32[]{:S(2)}) collective-permute-start(bf16[256,256]{1,0:T(8,128)(2,1)S(1)} %get-tuple-element.30.own), channel_id=1, source_target_pairs={{0,6},{1,7},{2,4},{3,5},{4,2},{5,3},{6,0},{7,1},{8,14},{9,15},{10,... | collective-permute-start | bytes 393224 | tf_op jit(solution)/shard_map/ppermute | solution.py:338
  25.3 1.9 %collective-permute-start.6 = (bf16[256,256]{1,0:T(8,128)(2,1)S(1)}, bf16[256,256]{1,0:T(8,128)(2,1)S(1)}, u32[]{:S(2)}, u32[]{:S(2)}) collective-permute-start(bf16[256,256]{1,0:T(8,128)(2,1)S(1)} %get-tuple-element.30.own), channel_id=1, source_target_pairs={{0,4},{1,5},{2,6},{3,7},{4,0},{5,1},{6,2},{7,3},{8,12},{9,13},{10,... | collective-permute-start | bytes 393224 | tf_op jit(solution)/shard_map/ppermute | solution.py:338
  27.2 3.8 %collective-permute-done.4.refs_0_ = bf16[256,256]{1,0:T(8,128)(2,1)S(1)} collective-permute-done((bf16[256,256]{1,0:T(8,128)(2,1)S(1)}, bf16[256,256]{1,0:T(8,128)(2,1)S(1)}, u32[]{:S(2)}, u32[]{:S(2)}) %collective-permute-start.4) | collective-permute-done | bytes 131104 | tf_op jit(solution)/shard_map/ppermute | solution.py:338
  31.1 4.1 %collective-permute-done.5.refs_1_ = bf16[256,256]{1,0:T(8,128)(2,1)S(1)} collective-permute-done((bf16[256,256]{1,0:T(8,128)(2,1)S(1)}, bf16[256,256]{1,0:T(8,128)(2,1)S(1)}, u32[]{:S(2)}, u32[]{:S(2)}) %collective-permute-start.5) | collective-permute-done | bytes 131104 | tf_op jit(solution)/shard_map/ppermute | solution.py:338
  35.1 0.2 collective-permute-done.6.refs_2_
  35.4 0.4 gram.1._.own
  35.8 1.4 %collective-permute-start.7 = (f32[160,128]{1,0:T(8,128)S(1)}, f32[160,128]{1,0:T(8,128)S(1)}, u32[]{:S(2)}, u32[]{:S(2)}) collective-permute-start(f32[160,128]{1,0:T(8,128)S(1)} %gram.1._.own), channel_id=1, source_target_pairs={{0,8},{8,0},{16,24},{24,16},{1,9},{9,1},{17,25},{25,17},{2,10},{10... | collective-permute-start | bytes 245768 | tf_op jit(solution)/shard_map/ppermute | solution.py:341
  37.2 1.4 %collective-permute-start.8 = (f32[160,128]{1,0:T(8,128)S(1)}, f32[160,128]{1,0:T(8,128)S(1)}, u32[]{:S(2)}, u32[]{:S(2)}) collective-permute-start(f32[160,128]{1,0:T(8,128)S(1)} %gram.1._.own), channel_id=1, source_target_pairs={{0,16},{8,24},{16,0},{24,8},{1,17},{9,25},{17,1},{25,9},{2,18},{10... | collective-permute-start | bytes 245768 | tf_op jit(solution)/shard_map/ppermute | solution.py:341
  38.6 0.7 collective-permute-start.9
  39.3 0.1 full.1
  39.4 1.2 %back.1 = (f32[256,256]{1,0:T(8,128)S(1)}, bf16[256,256]{1,0:T(8,128)(2,1)S(1)}, bf16[256,256]{1,0:T(8,128)(2,1)S(1)}, bf16[256,256]{1,0:T(8,128)(2,1)S(1)}) custom-call(bf16[16,1024,128]{2,1,0:T(8,128)(2,1)S(1)} %get-tuple-element.31.turned, bf16[2048,256]{1,0:T(8,128)(2,1)S(1)} %full.1, f32[160,128]{1,0:T(8,128)S(1)} %gram.1._.own), custom_call_target="tpu_custom_call" | custom-call | flops 1073741824 | bytes 6291456 | tf_op jit(solution)/shard_map/back/pallas_call | solution.py:28
  40.7 1.5 %collective-permute-start.13 = (bf16[256,256]{1,0:T(8,128)(2,1)S(1)}, bf16[256,256]{1,0:T(8,128)(2,1)S(1)}, u32[]{:S(2)}, u32[]{:S(2)}) collective-permute-start(bf16[256,256]{1,0:T(8,128)(2,1)S(1)} %get-tuple-element.37), channel_id=1, source_target_pairs={{0,8},{8,0},{16,24},{24,16},{1,9},{9,1},{17,25},{25,17},{2,10},{10... | collective-permute-start | bytes 393224 | tf_op jit(solution)/shard_map/ppermute | solution.py:341
  42.1 1.4 %collective-permute-start.14 = (bf16[256,256]{1,0:T(8,128)(2,1)S(1)}, bf16[256,256]{1,0:T(8,128)(2,1)S(1)}, u32[]{:S(2)}, u32[]{:S(2)}) collective-permute-start(bf16[256,256]{1,0:T(8,128)(2,1)S(1)} %get-tuple-element.38), channel_id=1, source_target_pairs={{0,16},{8,24},{16,0},{24,8},{1,17},{9,25},{17,1},{25,9},{2,18},{10... | collective-permute-start | bytes 393224 | tf_op jit(solution)/shard_map/ppermute | solution.py:341
  43.5 0.7 collective-permute-start.15
  44.4 1.3 %collective-permute-done.11.second = f32[160,128]{1,0:T(8,128)S(1)} collective-permute-done((f32[160,128]{1,0:T(8,128)S(1)}, f32[160,128]{1,0:T(8,128)S(1)}, u32[]{:S(2)}, u32[]{:S(2)}) %collective-permute-start.11) | collective-permute-done | bytes 81952 | tf_op jit(solution)/shard_map/ppermute | solution.py:335
  45.7 0.5 collective-permute-start.12
  46.2 0.4 collective-permute-done.13.refs_0_
  46.6 3.3 %collective-permute-done.14.refs_1_ = bf16[256,256]{1,0:T(8,128)(2,1)S(1)} collective-permute-done((bf16[256,256]{1,0:T(8,128)(2,1)S(1)}, bf16[256,256]{1,0:T(8,128)(2,1)S(1)}, u32[]{:S(2)}, u32[]{:S(2)}) %collective-permute-start.14) | collective-permute-done | bytes 131104 | tf_op jit(solution)/shard_map/ppermute | solution.py:341
  50.0 1.0 %collective-permute-start.16 = (bf16[256,256]{1,0:T(8,128)(2,1)S(1)}, bf16[256,256]{1,0:T(8,128)(2,1)S(1)}, u32[]{:S(2)}, u32[]{:S(2)}) collective-permute-start(bf16[256,256]{1,0:T(8,128)(2,1)S(1)} %columns.1.refs_0_), channel_id=1, source_target_pairs={{0,8},{8,0},{16,24},{24,16},{1,9},{9,1},{17,25},{25,17},{2,10},{10... | collective-permute-start | bytes 393224 | tf_op jit(solution)/shard_map/ppermute | solution.py:341
  50.9 0.9 collective-permute-start.17
  51.8 1.7 %collective-permute-start.18 = (bf16[256,256]{1,0:T(8,128)(2,1)S(1)}, bf16[256,256]{1,0:T(8,128)(2,1)S(1)}, u32[]{:S(2)}, u32[]{:S(2)}) collective-permute-start(bf16[256,256]{1,0:T(8,128)(2,1)S(1)} %columns.1.refs_0_), channel_id=1, source_target_pairs={{0,24},{8,16},{16,8},{24,0},{1,25},{9,17},{17,9},{25,1},{2,26},{10... | collective-permute-start | bytes 393224 | tf_op jit(solution)/shard_map/ppermute | solution.py:341
  53.5 40.1 %factor.1 = (bf16[256,256]{1,0:T(8,128)(2,1)S(1)}, bf16[256,256]{1,0:T(8,128)(2,1)S(1)}, bf16[256,256]{1,0:T(8,128)(2,1)}) custom-call(f32[160,128]{1,0:T(8,128)S(1)} %two.1.refs_0_, f32[160,128]{1,0:T(8,128)S(1)} %collective-permute-done.12.refs_1_, f32[256,256]{1,0:T(8,128)S(1)} %get-tuple-element.33.refs_2_), custom_call_target="tpu_custom_call" | custom-call | flops 754974720 | bytes 1 | tf_op jit(solution)/shard_map/factor/pallas_call | solution.py:28
  93.6 1.3 %project.1 = bf16[1024,256]{1,0:T(8,128)(2,1)} custom-call(bf16[256,256]{1,0:T(8,128)(2,1)S(1)} %get-tuple-element.35.high, bf16[256,256]{1,0:T(8,128)(2,1)S(1)} %get-tuple-element.36.low, bf16[256,256]{1,0:T(8,128)(2,1)S(1)} %columns.1.refs_0_, bf16[256,256]{1,0:T(8,128)(2,1)S(1)} %collective-permute-done.16.refs_1_, ...), custom_call_target="tpu_custom_call" | custom-call | flops 268435456 | bytes 2097152 | tf_op jit(solution)/shard_map/project/pallas_call | solution.py:28
  (20 shorter events, 0.5 us)
Async XLA Ops:
  4.1 2.0 %collective-permute-start = (bf16[1024,256]{1,0:T(8,128)(2,1)S(1)}, bf16[1024,256]{1,0:T(8,128)(2,1)S(1)}, u32[]{:S(2)}, u32[]{:S(2)}) collective-permute-start(bf16[1024,256]{1,0:T(8,128)(2,1)S(1)} %get-tuple-element.23), channel_id=1, source_target_pairs={{0,1},{1,0},{2,3},{3,2},{4,5},{5,4},{6,7},{7,6},{8,9},{9,8},{10,11... | collective-permute-start | bytes 1572872 | tf_op jit(solution)/shard_map/ppermute | solution.py:335
  6.2 13.2 %collective-permute-start.1 = (bf16[256,256]{1,0:T(8,128)(2,1)S(1)}, bf16[256,256]{1,0:T(8,128)(2,1)S(1)}, u32[]{:S(2)}, u32[]{:S(2)}) collective-permute-start(bf16[256,256]{1,0:T(8,128)(2,1)S(1)} %get-tuple-element.25), channel_id=1, source_target_pairs={{0,6},{1,7},{2,4},{3,5},{4,2},{5,3},{6,0},{7,1},{8,14},{9,15},{10,... | collective-permute-start | bytes 393224 | tf_op jit(solution)/shard_map/ppermute | solution.py:338
  11.0 8.5 %collective-permute-start.2 = (bf16[256,256]{1,0:T(8,128)(2,1)S(1)}, bf16[256,256]{1,0:T(8,128)(2,1)S(1)}, u32[]{:S(2)}, u32[]{:S(2)}) collective-permute-start(bf16[256,256]{1,0:T(8,128)(2,1)S(1)} %get-tuple-element.26), channel_id=1, source_target_pairs={{0,2},{1,3},{2,0},{3,1},{4,6},{5,7},{6,4},{7,5},{8,10},{9,11},{10,... | collective-permute-start | bytes 393224 | tf_op jit(solution)/shard_map/ppermute | solution.py:338
  11.0 11.7 %collective-permute-start.3 = (bf16[256,256]{1,0:T(8,128)(2,1)S(1)}, bf16[256,256]{1,0:T(8,128)(2,1)S(1)}, u32[]{:S(2)}, u32[]{:S(2)}) collective-permute-start(bf16[256,256]{1,0:T(8,128)(2,1)S(1)} %get-tuple-element.27), channel_id=1, source_target_pairs={{0,4},{1,5},{2,6},{3,7},{4,0},{5,1},{6,2},{7,3},{8,12},{9,13},{10,... | collective-permute-start | bytes 393224 | tf_op jit(solution)/shard_map/ppermute | solution.py:338
  22.8 8.3 %collective-permute-start.4 = (bf16[256,256]{1,0:T(8,128)(2,1)S(1)}, bf16[256,256]{1,0:T(8,128)(2,1)S(1)}, u32[]{:S(2)}, u32[]{:S(2)}) collective-permute-start(bf16[256,256]{1,0:T(8,128)(2,1)S(1)} %get-tuple-element.30.own), channel_id=1, source_target_pairs={{0,6},{1,7},{2,4},{3,5},{4,2},{5,3},{6,0},{7,1},{8,14},{9,15},{10,... | collective-permute-start | bytes 393224 | tf_op jit(solution)/shard_map/ppermute | solution.py:338
  25.3 9.8 %collective-permute-start.5 = (bf16[256,256]{1,0:T(8,128)(2,1)S(1)}, bf16[256,256]{1,0:T(8,128)(2,1)S(1)}, u32[]{:S(2)}, u32[]{:S(2)}) collective-permute-start(bf16[256,256]{1,0:T(8,128)(2,1)S(1)} %get-tuple-element.30.own), channel_id=1, source_target_pairs={{0,2},{1,3},{2,0},{3,1},{4,6},{5,7},{6,4},{7,5},{8,10},{9,11},{10,... | collective-permute-start | bytes 393224 | tf_op jit(solution)/shard_map/ppermute | solution.py:338
  25.3 10.0 %collective-permute-start.6 = (bf16[256,256]{1,0:T(8,128)(2,1)S(1)}, bf16[256,256]{1,0:T(8,128)(2,1)S(1)}, u32[]{:S(2)}, u32[]{:S(2)}) collective-permute-start(bf16[256,256]{1,0:T(8,128)(2,1)S(1)} %get-tuple-element.30.own), channel_id=1, source_target_pairs={{0,4},{1,5},{2,6},{3,7},{4,0},{5,1},{6,2},{7,3},{8,12},{9,13},{10,... | collective-permute-start | bytes 393224 | tf_op jit(solution)/shard_map/ppermute | solution.py:338
  35.4 4.0 %collective-permute-start.10 = (bf16[1024,256]{1,0:T(8,128)(2,1)S(1)}, bf16[1024,256]{1,0:T(8,128)(2,1)S(1)}, u32[]{:S(2)}, u32[]{:S(2)}) collective-permute-start(bf16[1024,256]{1,0:T(8,128)(2,1)S(1)} %pack.1.mine), channel_id=1, source_target_pairs={{0,1},{1,0},{2,3},{3,2},{4,5},{5,4},{6,7},{7,6},{8,9},{9,8},{10,11... | collective-permute-start | bytes 1572872 | tf_op jit(solution)/shard_map/ppermute | solution.py:335
  35.8 7.7 %collective-permute-start.7 = (f32[160,128]{1,0:T(8,128)S(1)}, f32[160,128]{1,0:T(8,128)S(1)}, u32[]{:S(2)}, u32[]{:S(2)}) collective-permute-start(f32[160,128]{1,0:T(8,128)S(1)} %gram.1._.own), channel_id=1, source_target_pairs={{0,8},{8,0},{16,24},{24,16},{1,9},{9,1},{17,25},{25,17},{2,10},{10... | collective-permute-start | bytes 245768 | tf_op jit(solution)/shard_map/ppermute | solution.py:341
  37.2 7.0 %collective-permute-start.8 = (f32[160,128]{1,0:T(8,128)S(1)}, f32[160,128]{1,0:T(8,128)S(1)}, u32[]{:S(2)}, u32[]{:S(2)}) collective-permute-start(f32[160,128]{1,0:T(8,128)S(1)} %gram.1._.own), channel_id=1, source_target_pairs={{0,16},{8,24},{16,0},{24,8},{1,17},{9,25},{17,1},{25,9},{2,18},{10... | collective-permute-start | bytes 245768 | tf_op jit(solution)/shard_map/ppermute | solution.py:341
  38.6 5.7 %collective-permute-start.9 = (f32[160,128]{1,0:T(8,128)S(1)}, f32[160,128]{1,0:T(8,128)S(1)}, u32[]{:S(2)}, u32[]{:S(2)}) collective-permute-start(f32[160,128]{1,0:T(8,128)S(1)} %gram.1._.own), channel_id=1, source_target_pairs={{0,24},{8,16},{16,8},{24,0},{1,25},{9,17},{17,9},{25,1},{2,26},{10... | collective-permute-start | bytes 245768 | tf_op jit(solution)/shard_map/ppermute | solution.py:341
  40.7 5.9 %collective-permute-start.13 = (bf16[256,256]{1,0:T(8,128)(2,1)S(1)}, bf16[256,256]{1,0:T(8,128)(2,1)S(1)}, u32[]{:S(2)}, u32[]{:S(2)}) collective-permute-start(bf16[256,256]{1,0:T(8,128)(2,1)S(1)} %get-tuple-element.37), channel_id=1, source_target_pairs={{0,8},{8,0},{16,24},{24,16},{1,9},{9,1},{17,25},{25,17},{2,10},{10... | collective-permute-start | bytes 393224 | tf_op jit(solution)/shard_map/ppermute | solution.py:341
  42.1 7.8 %collective-permute-start.14 = (bf16[256,256]{1,0:T(8,128)(2,1)S(1)}, bf16[256,256]{1,0:T(8,128)(2,1)S(1)}, u32[]{:S(2)}, u32[]{:S(2)}) collective-permute-start(bf16[256,256]{1,0:T(8,128)(2,1)S(1)} %get-tuple-element.38), channel_id=1, source_target_pairs={{0,16},{8,24},{16,0},{24,8},{1,17},{9,25},{17,1},{25,9},{2,18},{10... | collective-permute-start | bytes 393224 | tf_op jit(solution)/shard_map/ppermute | solution.py:341
  43.5 6.4 %collective-permute-start.15 = (bf16[256,256]{1,0:T(8,128)(2,1)S(1)}, bf16[256,256]{1,0:T(8,128)(2,1)S(1)}, u32[]{:S(2)}, u32[]{:S(2)}) collective-permute-start(bf16[256,256]{1,0:T(8,128)(2,1)S(1)} %get-tuple-element.39), channel_id=1, source_target_pairs={{0,24},{8,16},{16,8},{24,0},{1,25},{9,17},{17,9},{25,1},{2,26},{10... | collective-permute-start | bytes 393224 | tf_op jit(solution)/shard_map/ppermute | solution.py:341
  44.3 1.3 %collective-permute-start.11 = (f32[160,128]{1,0:T(8,128)S(1)}, f32[160,128]{1,0:T(8,128)S(1)}, u32[]{:S(2)}, u32[]{:S(2)}) collective-permute-start(f32[160,128]{1,0:T(8,128)S(1)} %tree.1.first), channel_id=1, source_target_pairs={{0,1},{1,0},{2,3},{3,2},{4,5},{5,4},{6,7},{7,6},{8,9},{9,8},{10,11... | collective-permute-start | bytes 245768 | tf_op jit(solution)/shard_map/ppermute | solution.py:335
  45.7 7.8 %collective-permute-start.12 = (f32[160,128]{1,0:T(8,128)S(1)}, f32[160,128]{1,0:T(8,128)S(1)}, u32[]{:S(2)}, u32[]{:S(2)}) collective-permute-start(f32[160,128]{1,0:T(8,128)S(1)} %two.1.refs_0_), channel_id=1, source_target_pairs={{0,2},{1,3},{2,0},{3,1},{4,6},{5,7},{6,4},{7,5},{8,10},{9,11},{10,... | collective-permute-start | bytes 245768 | tf_op jit(solution)/shard_map/ppermute | solution.py:338
  50.0 43.6 %collective-permute-start.16 = (bf16[256,256]{1,0:T(8,128)(2,1)S(1)}, bf16[256,256]{1,0:T(8,128)(2,1)S(1)}, u32[]{:S(2)}, u32[]{:S(2)}) collective-permute-start(bf16[256,256]{1,0:T(8,128)(2,1)S(1)} %columns.1.refs_0_), channel_id=1, source_target_pairs={{0,8},{8,0},{16,24},{24,16},{1,9},{9,1},{17,25},{25,17},{2,10},{10... | collective-permute-start | bytes 393224 | tf_op jit(solution)/shard_map/ppermute | solution.py:341
  50.9 42.7 %collective-permute-start.17 = (bf16[256,256]{1,0:T(8,128)(2,1)S(1)}, bf16[256,256]{1,0:T(8,128)(2,1)S(1)}, u32[]{:S(2)}, u32[]{:S(2)}) collective-permute-start(bf16[256,256]{1,0:T(8,128)(2,1)S(1)} %columns.1.refs_0_), channel_id=1, source_target_pairs={{0,16},{8,24},{16,0},{24,8},{1,17},{9,25},{17,1},{25,9},{2,18},{10... | collective-permute-start | bytes 393224 | tf_op jit(solution)/shard_map/ppermute | solution.py:341
  51.8 41.8 %collective-permute-start.18 = (bf16[256,256]{1,0:T(8,128)(2,1)S(1)}, bf16[256,256]{1,0:T(8,128)(2,1)S(1)}, u32[]{:S(2)}, u32[]{:S(2)}) collective-permute-start(bf16[256,256]{1,0:T(8,128)(2,1)S(1)} %columns.1.refs_0_), channel_id=1, source_target_pairs={{0,24},{8,16},{16,8},{24,0},{1,25},{9,17},{17,9},{25,1},{2,26},{10... | collective-permute-start | bytes 393224 | tf_op jit(solution)/shard_map/ppermute | solution.py:341

commit v5 on v4

--- a/solution.py
+++ b/solution.py
@@ -115,9 +115,9 @@
 def sketch_kernel(share, counts, rows_hbm, cols_hbm, tiles_hbm, omega_hbm, sent, dense, omega, rows, cols, tiles, sems):
     size_b = tiles.shape[1]
     last = pltpu.make_async_copy(omega_hbm, omega, sems.at[LOADS + 2])
-    last.start()
 
     def clear():
+        last.start()
         dense[...] = jnp.zeros_like(dense)
 
     def put(slot, row, col):
@@ -309,13 +309,22 @@
 
 
 def project_kernel(scale, count, high, low, *refs):
-    out = refs[-1]
+    out, work, sems = refs[-3:]
     me = lax.axis_index("row")
     share = refs[0].shape[0]
+    copies = []
     for step in range(count):
         chunk = refs[step][...]
         product = dot(chunk, high[...], NT) + dot(chunk, low[...], NT)
-        out[rows_at(me ^ step, share), :] = (product * scale).astype(BF)
+        work[step * share : (step + 1) * share, :] = (product * scale).astype(BF)
+        copies.append(
+            pltpu.make_async_copy(
+                work.at[pl.ds(step * share, share)], out.at[rows_at(me ^ step, share)], sems.at[step]
+            )
+        )
+        copies[-1].start()
+    for copy in copies:
+        copy.wait()
 
 
 def shards(tiles, tile_rows, tile_cols, counts, omega):
@@ -447,14 +456,17 @@
         flops=int(FACTOR_FLOPS * rank**3),
         nbytes=1,
     )
-    (projected,) = call(
-        "project",
+    ins = [high, low, *backs]
+    projected = pl.pallas_call(
         functools.partial(project_kernel, float(RB_DEV * row_groups) ** -0.5, row_groups),
-        vs(high, low, *backs),
-        [array((cols_here, rank), BF)],
-        flops=4 * cols_here * rank * rank,
-        nbytes=2 * MIB,
-    )
+        out_shape=pltpu.HBM((cols_here, rank), BF),
+        in_specs=[pl.BlockSpec(memory_space=pltpu.VMEM)] * len(ins),
+        out_specs=pl.BlockSpec(memory_space=pltpu.HBM),
+        scratch_shapes=[pltpu.VMEM((cols_here, rank), BF), pltpu.SemaphoreType.DMA((row_groups,))],
+        compiler_params=pltpu.CompilerParams(vmem_limit_bytes=24 * MIB),
+        cost_estimate=pl.CostEstimate(flops=4 * cols_here * rank * rank, bytes_accessed=2 * MIB, transcendentals=0),
+        name="project",
+    )(*ins)
     return basis, projected
 
 

time: 95 us -> 94.8 us (level)
  Pallas kernels: 54.7 us -> 53.2 us
    pallas_call x14 -> x13, Pallas kernels: 54.7 us -> 51.9 us  [call(): pl.pallas_call(body, out_shape=outs, in_specs=[pl.BlockSpec(memory_space=...]
    ppermute x7, waiting for transfers between devices: 11.3 us -> 12.8 us  [swap_z(): lax.ppermute(x, 'col', [(i, i ^ CORES * step) for i in range(col_groups)])]
    pallas_call x0 -> x1, Pallas kernels: none -> 1.21 us  [shards(): pl.pallas_call(functools.partial(project_kernel, float(RB_DEV * row_group...]
  transfers between devices with their start and end apart: 19 -> 19, of which waited for: 9 -> 10; matrix products, arithmetic and copies ran while one was open for 0% -> 0% of each run, Pallas kernels for 53% -> 52%
where the time goes in v5:
time: 94.8 us; the launch traced here: 94.5 us
  Pallas kernels  53.2 us (56%)
  starting transfers between devices  21.8 us (23%)
  waiting for transfers between devices  18.2 us (19%)
  between operations  1.38 us (1%)
    pallas_call x13, Pallas kernels, call(): pl.pallas_call(body, out_shape=outs, in_specs=[pl.BlockSpec(memory_space=...  51.9 us
    ppermute x7, waiting for transfers between devices, swap_z(): lax.ppermute(x, 'col', [(i, i ^ CORES * step) for i in range(col_groups)])  12.8 us
    ppermute x9, starting transfers between devices, swap_row(): return lax.ppermute(x, 'row', [(i, i ^ step) for i in range(row_groups)])  10.7 us
    ppermute x7, starting transfers between devices, swap_z(): lax.ppermute(x, 'col', [(i, i ^ CORES * step) for i in range(col_groups)])  10.3 us
    ppermute x9, waiting for transfers between devices, swap_row(): return lax.ppermute(x, 'row', [(i, i ^ step) for i in range(row_groups)])  3.38 us
    ppermute x3, waiting for transfers between devices, swap_core(): return lax.ppermute(x, 'col', [(i, i ^ 1) for i in range(col_groups)])  2.1 us
  transfers between devices with their start and end apart: 19, of which 10 were waited for; matrix products, arithmetic and copies ran while one was open for 0% of the time, Pallas kernels for 52%

profile of v5, /device:TPU:0, one launch (start us, length us, event | category | flops | bytes accessed | tf_op | source)
XLA Modules:
  0.0 94.5 jit_solution(17413352840972526552)
XLA Ops:
  1.3 2.7 %sketch.1 = (bf16[1024,256]{1,0:T(8,128)(2,1)S(1)}, bf16[8,2048,128]{2,1,0:T(8,128)(2,1)S(1)}, bf16[1024,256]{1,0:T(8,128)(2,1)S(1)}) custom-call(s32[1]{0:T(128)S(6)} %copy.7.counts, s32[96]{0:T(128)} %rows_hbm.3, s32[96]{0:T(128)} %cols_hbm.3, bf16[96,128,128]{2,1,0:T(8,128)(2,1)} %tiles_hbm.3, bf16[1024,256]{1,0:T(8,128)(2,1)} %omega_hbm.1), custom_call_target="tpu_custom_call" | custom-call | flops 536870912 | bytes 6291456 | tf_op jit(solution)/shard_map/sketch/pallas_call | solution.py:28
  4.0 0.6 collective-permute-start
  4.6 0.7 kept.1
  5.3 0.8 collective-permute-done.came
  6.2 4.4 %collective-permute-start.1 = (bf16[256,256]{1,0:T(8,128)(2,1)S(1)}, bf16[256,256]{1,0:T(8,128)(2,1)S(1)}, u32[]{:S(2)}, u32[]{:S(2)}) collective-permute-start(bf16[256,256]{1,0:T(8,128)(2,1)S(1)} %get-tuple-element.25), channel_id=1, source_target_pairs={{0,6},{1,7},{2,4},{3,5},{4,2},{5,3},{6,0},{7,1},{8,14},{9,15},{10,... | collective-permute-start | bytes 393224 | tf_op jit(solution)/shard_map/ppermute | solution.py:347
  10.7 0.6 collective-permute-start.3
  11.3 6.5 %turn.1 = (bf16[16,1024,128]{2,1,0:T(8,128)(2,1)S(1)}, f32[8,128]{1,0:T(8,128)S(1)}) custom-call(s32[1]{0:T(128)S(6)} %copy.7.counts, s32[96]{0:T(128)} %rows_hbm.3, s32[96]{0:T(128)} %cols_hbm.3, bf16[96,128,128]{2,1,0:T(8,128)(2,1)} %tiles_hbm.3, f32[8,128]{1,0:T(8,128)S(1)} %get-tuple-element.28._), custom_call_target="tpu_custom_call" | custom-call | bytes 8388608 | tf_op jit(solution)/shard_map/turn/pallas_call | solution.py:28
  17.9 0.2 collective-permute-done.2.refs_1_
  18.1 4.3 %collective-permute-done.3.refs_2_ = bf16[256,256]{1,0:T(8,128)(2,1)S(1)} collective-permute-done((bf16[256,256]{1,0:T(8,128)(2,1)S(1)}, bf16[256,256]{1,0:T(8,128)(2,1)S(1)}, u32[]{:S(2)}, u32[]{:S(2)}) %collective-permute-start.3) | collective-permute-done | bytes 131104 | tf_op jit(solution)/shard_map/ppermute | solution.py:347
  22.4 2.7 %collective-permute-start.4 = (bf16[256,256]{1,0:T(8,128)(2,1)S(1)}, bf16[256,256]{1,0:T(8,128)(2,1)S(1)}, u32[]{:S(2)}, u32[]{:S(2)}) collective-permute-start(bf16[256,256]{1,0:T(8,128)(2,1)S(1)} %get-tuple-element.30.own), channel_id=1, source_target_pairs={{0,6},{1,7},{2,4},{3,5},{4,2},{5,3},{6,0},{7,1},{8,14},{9,15},{10,... | collective-permute-start | bytes 393224 | tf_op jit(solution)/shard_map/ppermute | solution.py:347
  25.1 1.7 %collective-permute-start.6 = (bf16[256,256]{1,0:T(8,128)(2,1)S(1)}, bf16[256,256]{1,0:T(8,128)(2,1)S(1)}, u32[]{:S(2)}, u32[]{:S(2)}) collective-permute-start(bf16[256,256]{1,0:T(8,128)(2,1)S(1)} %get-tuple-element.30.own), channel_id=1, source_target_pairs={{0,4},{1,5},{2,6},{3,7},{4,0},{5,1},{6,2},{7,3},{8,12},{9,13},{10,... | collective-permute-start | bytes 393224 | tf_op jit(solution)/shard_map/ppermute | solution.py:347
  26.9 3.8 %collective-permute-done.4.refs_0_ = bf16[256,256]{1,0:T(8,128)(2,1)S(1)} collective-permute-done((bf16[256,256]{1,0:T(8,128)(2,1)S(1)}, bf16[256,256]{1,0:T(8,128)(2,1)S(1)}, u32[]{:S(2)}, u32[]{:S(2)}) %collective-permute-start.4) | collective-permute-done | bytes 131104 | tf_op jit(solution)/shard_map/ppermute | solution.py:347
  30.7 3.9 %collective-permute-done.5.refs_1_ = bf16[256,256]{1,0:T(8,128)(2,1)S(1)} collective-permute-done((bf16[256,256]{1,0:T(8,128)(2,1)S(1)}, bf16[256,256]{1,0:T(8,128)(2,1)S(1)}, u32[]{:S(2)}, u32[]{:S(2)}) %collective-permute-start.5) | collective-permute-done | bytes 131104 | tf_op jit(solution)/shard_map/ppermute | solution.py:347
  34.7 0.5 collective-permute-done.6.refs_2_
  35.3 0.4 gram.1._.own
  35.7 1.2 %collective-permute-start.7 = (f32[160,128]{1,0:T(8,128)S(1)}, f32[160,128]{1,0:T(8,128)S(1)}, u32[]{:S(2)}, u32[]{:S(2)}) collective-permute-start(f32[160,128]{1,0:T(8,128)S(1)} %gram.1._.own), channel_id=1, source_target_pairs={{0,8},{8,0},{16,24},{24,16},{1,9},{9,1},{17,25},{25,17},{2,10},{10... | collective-permute-start | bytes 245768 | tf_op jit(solution)/shard_map/ppermute | solution.py:350
  36.9 1.7 %collective-permute-start.8 = (f32[160,128]{1,0:T(8,128)S(1)}, f32[160,128]{1,0:T(8,128)S(1)}, u32[]{:S(2)}, u32[]{:S(2)}) collective-permute-start(f32[160,128]{1,0:T(8,128)S(1)} %gram.1._.own), channel_id=1, source_target_pairs={{0,16},{8,24},{16,0},{24,8},{1,17},{9,25},{17,1},{25,9},{2,18},{10... | collective-permute-start | bytes 245768 | tf_op jit(solution)/shard_map/ppermute | solution.py:350
  38.6 0.6 collective-permute-start.9
  39.3 1.2 %back.1 = (f32[256,256]{1,0:T(8,128)S(1)}, bf16[256,256]{1,0:T(8,128)(2,1)S(1)}, bf16[256,256]{1,0:T(8,128)(2,1)S(1)}, bf16[256,256]{1,0:T(8,128)(2,1)S(1)}) custom-call(bf16[16,1024,128]{2,1,0:T(8,128)(2,1)S(1)} %get-tuple-element.31.turned, bf16[2048,256]{1,0:T(8,128)(2,1)S(1)} %full.1, f32[160,128]{1,0:T(8,128)S(1)} %gram.1._.own), custom_call_target="tpu_custom_call" | custom-call | flops 1073741824 | bytes 6291456 | tf_op jit(solution)/shard_map/back/pallas_call | solution.py:28
  40.5 1.2 %collective-permute-start.13 = (bf16[256,256]{1,0:T(8,128)(2,1)S(1)}, bf16[256,256]{1,0:T(8,128)(2,1)S(1)}, u32[]{:S(2)}, u32[]{:S(2)}) collective-permute-start(bf16[256,256]{1,0:T(8,128)(2,1)S(1)} %get-tuple-element.37), channel_id=1, source_target_pairs={{0,8},{8,0},{16,24},{24,16},{1,9},{9,1},{17,25},{25,17},{2,10},{10... | collective-permute-start | bytes 393224 | tf_op jit(solution)/shard_map/ppermute | solution.py:350
  41.8 1.7 %collective-permute-start.14 = (bf16[256,256]{1,0:T(8,128)(2,1)S(1)}, bf16[256,256]{1,0:T(8,128)(2,1)S(1)}, u32[]{:S(2)}, u32[]{:S(2)}) collective-permute-start(bf16[256,256]{1,0:T(8,128)(2,1)S(1)} %get-tuple-element.38), channel_id=1, source_target_pairs={{0,16},{8,24},{16,0},{24,8},{1,17},{9,25},{17,1},{25,9},{2,18},{10... | collective-permute-start | bytes 393224 | tf_op jit(solution)/shard_map/ppermute | solution.py:350
  43.5 0.6 collective-permute-start.15
  44.1 0.2 collective-permute-done.9.refs_2_
  44.4 1.3 %collective-permute-done.11.second = f32[160,128]{1,0:T(8,128)S(1)} collective-permute-done((f32[160,128]{1,0:T(8,128)S(1)}, f32[160,128]{1,0:T(8,128)S(1)}, u32[]{:S(2)}, u32[]{:S(2)}) %collective-permute-start.11) | collective-permute-done | bytes 81952 | tf_op jit(solution)/shard_map/ppermute | solution.py:344
  45.7 0.8 collective-permute-start.12
  46.5 2.1 %collective-permute-done.14.refs_1_ = bf16[256,256]{1,0:T(8,128)(2,1)S(1)} collective-permute-done((bf16[256,256]{1,0:T(8,128)(2,1)S(1)}, bf16[256,256]{1,0:T(8,128)(2,1)S(1)}, u32[]{:S(2)}, u32[]{:S(2)}) %collective-permute-start.14) | collective-permute-done | bytes 131104 | tf_op jit(solution)/shard_map/ppermute | solution.py:350
  48.6 1.0 %collective-permute-done.15.refs_2_ = bf16[256,256]{1,0:T(8,128)(2,1)S(1)} collective-permute-done((bf16[256,256]{1,0:T(8,128)(2,1)S(1)}, bf16[256,256]{1,0:T(8,128)(2,1)S(1)}, u32[]{:S(2)}, u32[]{:S(2)}) %collective-permute-start.15) | collective-permute-done | bytes 131104 | tf_op jit(solution)/shard_map/ppermute | solution.py:350
  49.7 1.2 %collective-permute-start.16 = (bf16[256,256]{1,0:T(8,128)(2,1)S(1)}, bf16[256,256]{1,0:T(8,128)(2,1)S(1)}, u32[]{:S(2)}, u32[]{:S(2)}) collective-permute-start(bf16[256,256]{1,0:T(8,128)(2,1)S(1)} %columns.1.refs_0_), channel_id=1, source_target_pairs={{0,8},{8,0},{16,24},{24,16},{1,9},{9,1},{17,25},{25,17},{2,10},{10... | collective-permute-start | bytes 393224 | tf_op jit(solution)/shard_map/ppermute | solution.py:350
  50.9 0.8 collective-permute-start.17
  51.7 1.5 %collective-permute-start.18 = (bf16[256,256]{1,0:T(8,128)(2,1)S(1)}, bf16[256,256]{1,0:T(8,128)(2,1)S(1)}, u32[]{:S(2)}, u32[]{:S(2)}) collective-permute-start(bf16[256,256]{1,0:T(8,128)(2,1)S(1)} %columns.1.refs_0_), channel_id=1, source_target_pairs={{0,24},{8,16},{16,8},{24,0},{1,25},{9,17},{17,9},{25,1},{2,26},{10... | collective-permute-start | bytes 393224 | tf_op jit(solution)/shard_map/ppermute | solution.py:350
  53.3 40.1 %factor.1 = (bf16[256,256]{1,0:T(8,128)(2,1)S(1)}, bf16[256,256]{1,0:T(8,128)(2,1)S(1)}, bf16[256,256]{1,0:T(8,128)(2,1)}) custom-call(f32[160,128]{1,0:T(8,128)S(1)} %two.1.refs_0_, f32[160,128]{1,0:T(8,128)S(1)} %collective-permute-done.12.refs_1_, f32[256,256]{1,0:T(8,128)S(1)} %get-tuple-element.33.refs_2_), custom_call_target="tpu_custom_call" | custom-call | flops 754974720 | bytes 1 | tf_op jit(solution)/shard_map/factor/pallas_call | solution.py:28
  93.3 1.2 %project.1 = bf16[1024,256]{1,0:T(8,128)(2,1)} custom-call(bf16[256,256]{1,0:T(8,128)(2,1)S(1)} %get-tuple-element.35.high, bf16[256,256]{1,0:T(8,128)(2,1)S(1)} %get-tuple-element.36.low, bf16[256,256]{1,0:T(8,128)(2,1)S(1)} %columns.1.refs_0_, bf16[256,256]{1,0:T(8,128)(2,1)S(1)} %collective-permute-done.16.refs_1_, ...), custom_call_target="tpu_custom_call" | custom-call | flops 268435456 | bytes 2097152 | tf_op jit(solution)/shard_map/project/pallas_call | solution.py:460
  (20 shorter events, 0.6 us)
Async XLA Ops:
  4.0 2.2 %collective-permute-start = (bf16[1024,256]{1,0:T(8,128)(2,1)S(1)}, bf16[1024,256]{1,0:T(8,128)(2,1)S(1)}, u32[]{:S(2)}, u32[]{:S(2)}) collective-permute-start(bf16[1024,256]{1,0:T(8,128)(2,1)S(1)} %get-tuple-element.23), channel_id=1, source_target_pairs={{0,1},{1,0},{2,3},{3,2},{4,5},{5,4},{6,7},{7,6},{8,9},{9,8},{10,11... | collective-permute-start | bytes 1572872 | tf_op jit(solution)/shard_map/ppermute | solution.py:344
  6.2 11.6 %collective-permute-start.1 = (bf16[256,256]{1,0:T(8,128)(2,1)S(1)}, bf16[256,256]{1,0:T(8,128)(2,1)S(1)}, u32[]{:S(2)}, u32[]{:S(2)}) collective-permute-start(bf16[256,256]{1,0:T(8,128)(2,1)S(1)} %get-tuple-element.25), channel_id=1, source_target_pairs={{0,6},{1,7},{2,4},{3,5},{4,2},{5,3},{6,0},{7,1},{8,14},{9,15},{10,... | collective-permute-start | bytes 393224 | tf_op jit(solution)/shard_map/ppermute | solution.py:347
  10.7 7.4 %collective-permute-start.2 = (bf16[256,256]{1,0:T(8,128)(2,1)S(1)}, bf16[256,256]{1,0:T(8,128)(2,1)S(1)}, u32[]{:S(2)}, u32[]{:S(2)}) collective-permute-start(bf16[256,256]{1,0:T(8,128)(2,1)S(1)} %get-tuple-element.26), channel_id=1, source_target_pairs={{0,2},{1,3},{2,0},{3,1},{4,6},{5,7},{6,4},{7,5},{8,10},{9,11},{10,... | collective-permute-start | bytes 393224 | tf_op jit(solution)/shard_map/ppermute | solution.py:347
  10.7 11.7 %collective-permute-start.3 = (bf16[256,256]{1,0:T(8,128)(2,1)S(1)}, bf16[256,256]{1,0:T(8,128)(2,1)S(1)}, u32[]{:S(2)}, u32[]{:S(2)}) collective-permute-start(bf16[256,256]{1,0:T(8,128)(2,1)S(1)} %get-tuple-element.27), channel_id=1, source_target_pairs={{0,4},{1,5},{2,6},{3,7},{4,0},{5,1},{6,2},{7,3},{8,12},{9,13},{10,... | collective-permute-start | bytes 393224 | tf_op jit(solution)/shard_map/ppermute | solution.py:347
  22.4 8.3 %collective-permute-start.4 = (bf16[256,256]{1,0:T(8,128)(2,1)S(1)}, bf16[256,256]{1,0:T(8,128)(2,1)S(1)}, u32[]{:S(2)}, u32[]{:S(2)}) collective-permute-start(bf16[256,256]{1,0:T(8,128)(2,1)S(1)} %get-tuple-element.30.own), channel_id=1, source_target_pairs={{0,6},{1,7},{2,4},{3,5},{4,2},{5,3},{6,0},{7,1},{8,14},{9,15},{10,... | collective-permute-start | bytes 393224 | tf_op jit(solution)/shard_map/ppermute | solution.py:347
  25.1 9.5 %collective-permute-start.5 = (bf16[256,256]{1,0:T(8,128)(2,1)S(1)}, bf16[256,256]{1,0:T(8,128)(2,1)S(1)}, u32[]{:S(2)}, u32[]{:S(2)}) collective-permute-start(bf16[256,256]{1,0:T(8,128)(2,1)S(1)} %get-tuple-element.30.own), channel_id=1, source_target_pairs={{0,2},{1,3},{2,0},{3,1},{4,6},{5,7},{6,4},{7,5},{8,10},{9,11},{10,... | collective-permute-start | bytes 393224 | tf_op jit(solution)/shard_map/ppermute | solution.py:347
  25.1 10.0 %collective-permute-start.6 = (bf16[256,256]{1,0:T(8,128)(2,1)S(1)}, bf16[256,256]{1,0:T(8,128)(2,1)S(1)}, u32[]{:S(2)}, u32[]{:S(2)}) collective-permute-start(bf16[256,256]{1,0:T(8,128)(2,1)S(1)} %get-tuple-element.30.own), channel_id=1, source_target_pairs={{0,4},{1,5},{2,6},{3,7},{4,0},{5,1},{6,2},{7,3},{8,12},{9,13},{10,... | collective-permute-start | bytes 393224 | tf_op jit(solution)/shard_map/ppermute | solution.py:347
  35.2 4.0 %collective-permute-start.10 = (bf16[1024,256]{1,0:T(8,128)(2,1)S(1)}, bf16[1024,256]{1,0:T(8,128)(2,1)S(1)}, u32[]{:S(2)}, u32[]{:S(2)}) collective-permute-start(bf16[1024,256]{1,0:T(8,128)(2,1)S(1)} %pack.1.mine), channel_id=1, source_target_pairs={{0,1},{1,0},{2,3},{3,2},{4,5},{5,4},{6,7},{7,6},{8,9},{9,8},{10,11... | collective-permute-start | bytes 1572872 | tf_op jit(solution)/shard_map/ppermute | solution.py:344
  35.7 7.9 %collective-permute-start.7 = (f32[160,128]{1,0:T(8,128)S(1)}, f32[160,128]{1,0:T(8,128)S(1)}, u32[]{:S(2)}, u32[]{:S(2)}) collective-permute-start(f32[160,128]{1,0:T(8,128)S(1)} %gram.1._.own), channel_id=1, source_target_pairs={{0,8},{8,0},{16,24},{24,16},{1,9},{9,1},{17,25},{25,17},{2,10},{10... | collective-permute-start | bytes 245768 | tf_op jit(solution)/shard_map/ppermute | solution.py:350
  36.9 7.2 %collective-permute-start.8 = (f32[160,128]{1,0:T(8,128)S(1)}, f32[160,128]{1,0:T(8,128)S(1)}, u32[]{:S(2)}, u32[]{:S(2)}) collective-permute-start(f32[160,128]{1,0:T(8,128)S(1)} %gram.1._.own), channel_id=1, source_target_pairs={{0,16},{8,24},{16,0},{24,8},{1,17},{9,25},{17,1},{25,9},{2,18},{10... | collective-permute-start | bytes 245768 | tf_op jit(solution)/shard_map/ppermute | solution.py:350
  38.6 5.7 %collective-permute-start.9 = (f32[160,128]{1,0:T(8,128)S(1)}, f32[160,128]{1,0:T(8,128)S(1)}, u32[]{:S(2)}, u32[]{:S(2)}) collective-permute-start(f32[160,128]{1,0:T(8,128)S(1)} %gram.1._.own), channel_id=1, source_target_pairs={{0,24},{8,16},{16,8},{24,0},{1,25},{9,17},{17,9},{25,1},{2,26},{10... | collective-permute-start | bytes 245768 | tf_op jit(solution)/shard_map/ppermute | solution.py:350
  40.5 6.0 %collective-permute-start.13 = (bf16[256,256]{1,0:T(8,128)(2,1)S(1)}, bf16[256,256]{1,0:T(8,128)(2,1)S(1)}, u32[]{:S(2)}, u32[]{:S(2)}) collective-permute-start(bf16[256,256]{1,0:T(8,128)(2,1)S(1)} %get-tuple-element.37), channel_id=1, source_target_pairs={{0,8},{8,0},{16,24},{24,16},{1,9},{9,1},{17,25},{25,17},{2,10},{10... | collective-permute-start | bytes 393224 | tf_op jit(solution)/shard_map/ppermute | solution.py:350
  41.8 6.8 %collective-permute-start.14 = (bf16[256,256]{1,0:T(8,128)(2,1)S(1)}, bf16[256,256]{1,0:T(8,128)(2,1)S(1)}, u32[]{:S(2)}, u32[]{:S(2)}) collective-permute-start(bf16[256,256]{1,0:T(8,128)(2,1)S(1)} %get-tuple-element.38), channel_id=1, source_target_pairs={{0,16},{8,24},{16,0},{24,8},{1,17},{9,25},{17,1},{25,9},{2,18},{10... | collective-permute-start | bytes 393224 | tf_op jit(solution)/shard_map/ppermute | solution.py:350
  43.5 6.1 %collective-permute-start.15 = (bf16[256,256]{1,0:T(8,128)(2,1)S(1)}, bf16[256,256]{1,0:T(8,128)(2,1)S(1)}, u32[]{:S(2)}, u32[]{:S(2)}) collective-permute-start(bf16[256,256]{1,0:T(8,128)(2,1)S(1)} %get-tuple-element.39), channel_id=1, source_target_pairs={{0,24},{8,16},{16,8},{24,0},{1,25},{9,17},{17,9},{25,1},{2,26},{10... | collective-permute-start | bytes 393224 | tf_op jit(solution)/shard_map/ppermute | solution.py:350
  44.3 1.3 %collective-permute-start.11 = (f32[160,128]{1,0:T(8,128)S(1)}, f32[160,128]{1,0:T(8,128)S(1)}, u32[]{:S(2)}, u32[]{:S(2)}) collective-permute-start(f32[160,128]{1,0:T(8,128)S(1)} %tree.1.first), channel_id=1, source_target_pairs={{0,1},{1,0},{2,3},{3,2},{4,5},{5,4},{6,7},{7,6},{8,9},{9,8},{10,11... | collective-permute-start | bytes 245768 | tf_op jit(solution)/shard_map/ppermute | solution.py:344
  45.7 7.6 %collective-permute-start.12 = (f32[160,128]{1,0:T(8,128)S(1)}, f32[160,128]{1,0:T(8,128)S(1)}, u32[]{:S(2)}, u32[]{:S(2)}) collective-permute-start(f32[160,128]{1,0:T(8,128)S(1)} %two.1.refs_0_), channel_id=1, source_target_pairs={{0,2},{1,3},{2,0},{3,1},{4,6},{5,7},{6,4},{7,5},{8,10},{9,11},{10,... | collective-permute-start | bytes 245768 | tf_op jit(solution)/shard_map/ppermute | solution.py:347
  49.7 43.6 %collective-permute-start.16 = (bf16[256,256]{1,0:T(8,128)(2,1)S(1)}, bf16[256,256]{1,0:T(8,128)(2,1)S(1)}, u32[]{:S(2)}, u32[]{:S(2)}) collective-permute-start(bf16[256,256]{1,0:T(8,128)(2,1)S(1)} %columns.1.refs_0_), channel_id=1, source_target_pairs={{0,8},{8,0},{16,24},{24,16},{1,9},{9,1},{17,25},{25,17},{2,10},{10... | collective-permute-start | bytes 393224 | tf_op jit(solution)/shard_map/ppermute | solution.py:350
  50.9 42.4 %collective-permute-start.17 = (bf16[256,256]{1,0:T(8,128)(2,1)S(1)}, bf16[256,256]{1,0:T(8,128)(2,1)S(1)}, u32[]{:S(2)}, u32[]{:S(2)}) collective-permute-start(bf16[256,256]{1,0:T(8,128)(2,1)S(1)} %columns.1.refs_0_), channel_id=1, source_target_pairs={{0,16},{8,24},{16,0},{24,8},{1,17},{9,25},{17,1},{25,9},{2,18},{10... | collective-permute-start | bytes 393224 | tf_op jit(solution)/shard_map/ppermute | solution.py:350
  51.7 41.6 %collective-permute-start.18 = (bf16[256,256]{1,0:T(8,128)(2,1)S(1)}, bf16[256,256]{1,0:T(8,128)(2,1)S(1)}, u32[]{:S(2)}, u32[]{:S(2)}) collective-permute-start(bf16[256,256]{1,0:T(8,128)(2,1)S(1)} %columns.1.refs_0_), channel_id=1, source_target_pairs={{0,24},{8,16},{16,8},{24,0},{1,25},{9,17},{17,9},{25,1},{2,26},{10... | collective-permute-start | bytes 393224 | tf_op jit(solution)/shard_map/ppermute | solution.py:350
